TPU v7x, 128 devices: a whole 4x4x4 slice. The times are simulated.
128 devices in a mesh: seq: 16 (over z, y), head: 8 (over x, core).
Axes of the slice: x: 4, y: 4, z: 4, core: 2. Of those that a mesh axis runs over, the one named last changes fastest.
Arguments:
- tokens: bfloat16 [8192, 2048], P(('seq', 'head')), may hold values from -6 to 6
- mixer_gain: float32 [2048], replicated, may hold values from 0.5 to 1.5
- mixer_weight: bfloat16 [2048, 16, 768], P(None, 'head'), may hold values from -0.125 to 0.125
- rate_weight: bfloat16 [2048, 2, 16], P(None, None, 'head'), may hold values from -0.125 to 0.125
- conv_weight: bfloat16 [4, 16, 512], P(None, 'head'), may hold values from -3 to 3
- decay_log: float32 [16], P('head')
- decay_bias: float32 [16], P('head'), may hold values from -2 to 1
- head_gain: float32 [256], replicated, may hold values from 0.5 to 1.5
- output_weight: bfloat16 [16, 256, 2048], P('head'), may hold values from -0.1875 to 0.1875
- feed_gain: float32 [2048], replicated, may hold values from 0.5 to 1.5
- gate_up_weight: bfloat16 [2048, 2, 5504], P(None, None, 'head'), may hold values from -0.125 to 0.125
- down_weight: bfloat16 [5504, 2048], P('head'), may hold values from -0.15625 to 0.15625
- doc_starts: int32 [4], replicated, may hold values from 1 to 8191, as said below
- cotangent: bfloat16 [8192, 2048], P(('seq', 'head')), may hold values from -6 to 6
Outputs:
- layer_out: bfloat16 [8192, 2048], P(('seq', 'head'))
- grad_tokens: float32 [8192, 2048], P(('seq', 'head'))
- grad_mixer_gain: float32 [2048], replicated
- grad_mixer_weight: float32 [2048, 16, 768], P('seq', 'head')
- grad_rate_weight: float32 [2048, 2, 16], P('seq', None, 'head')
- grad_conv_weight: float32 [4, 16, 512], P(None, 'head')
- grad_decay_log: float32 [16], P('head')
- grad_decay_bias: float32 [16], P('head')
- grad_head_gain: float32 [256], replicated
- grad_output_weight: float32 [16, 256, 2048], P('head', None, 'seq')
- grad_feed_gain: float32 [2048], replicated
- grad_gate_up_weight: float32 [2048, 2, 5504], P('seq', None, 'head')
- grad_down_weight: float32 [5504, 2048], P('head', 'seq')
Inputs may be any that keep to these rules, and one draw needn't show every extreme that they name: `doc_starts`: 4 increasing positions at which a new document begins: the first two lie within the first 512 positions, the last two within the last 512 positions.
All inputs are finite; a program needn't handle non-finite values.
Results may differ from a plain program's by a relative error of at most 0.022.
The roundings to bfloat16 on the way count: a program that leaves them out, or rounds other values in their place, can miss the bound.
Values may be sent and summed in bfloat16 or wider, within the bound.
A program may use at most 192 MiB of HBM per device.

v0:
```python
import jax
import jax.numpy as jnp
from jax import lax
from jax.sharding import PartitionSpec as P

D = 2048
DK = 128
DV = 256
KCONV = 4
GROUP = 64
MIXW = 768


highest = lax.Precision.HIGHEST


def passed_along(shard, axis, by):
    length = lax.axis_size(axis)
    pairs = [(i, i + by) for i in range(length) if 0 <= i + by < length]
    return lax.ppermute(shard, axis, pairs)


def rms_scale(values, gain):
    return values * lax.rsqrt(jnp.mean(values * values, axis=-1, keepdims=True) + 1e-05) * gain


def doc_index(doc_starts, positions):
    inside = jnp.sum((doc_starts[None, :] <= positions[:, None]).astype(jnp.int32), axis=1)
    return jnp.where(positions < 0, -1, inside)


def mixer_inputs(padded, doc_pad, rate_proj, conv_weight, decay_log, decay_bias):
    length = rate_proj.shape[0]
    conv_sum = jnp.zeros((length,) + padded.shape[1:], jnp.float32)
    for tap_index in range(KCONV):
        window = padded[tap_index : tap_index + length]
        valid = (doc_pad[tap_index : tap_index + length] == doc_pad[KCONV - 1 :]).astype(
            jnp.float32
        )
        conv_sum = conv_sum + conv_weight[tap_index] * window * valid[:, None, None]
    active = jax.nn.silu(conv_sum)
    query_vecs = active[..., :DK]
    key_vecs = active[..., DK : 2 * DK]
    val_vecs = active[..., 2 * DK :]
    query_vecs = (
        query_vecs
        * lax.rsqrt(jnp.sum(query_vecs * query_vecs, axis=-1, keepdims=True) + 1e-06)
        * DK ** (-0.5)
    )
    key_vecs = key_vecs * lax.rsqrt(jnp.sum(key_vecs * key_vecs, axis=-1, keepdims=True) + 1e-06)
    strength = jax.nn.sigmoid(rate_proj[:, 1])
    log_decay = -jnp.exp(decay_log) * jax.nn.softplus(rate_proj[:, 0] + decay_bias)
    return (query_vecs, key_vecs, val_vecs, strength, log_decay)


def solve_lower(system, rhs_vals):
    return jax.scipy.linalg.solve_triangular(system, rhs_vals, lower=True, unit_diagonal=True)


def group_step(carried, query_vecs, key_vecs, val_vecs, strength, log_decay, doc_part, prev_doc):
    queries = jnp.swapaxes(query_vecs, 0, 1)
    keyset = jnp.swapaxes(key_vecs, 0, 1)
    valset = jnp.swapaxes(val_vecs, 0, 1)
    beta_head = strength.T
    cumulative = jnp.cumsum(log_decay.T, axis=1)
    length = doc_part.shape[0]
    row_pos = lax.broadcasted_iota(jnp.int32, (length, length), 0)
    col_pos = lax.broadcasted_iota(jnp.int32, (length, length), 1)
    same_doc = (doc_part[:, None] == doc_part[None, :]) & (col_pos <= row_pos)
    spread = jnp.where(same_doc[None], cumulative[:, :, None] - cumulative[:, None, :], 0.0)
    decay_mat = jnp.where(same_doc[None], jnp.exp(spread), 0.0)
    carry_in = jnp.where((doc_part == prev_doc)[None, :], jnp.exp(cumulative), 0.0)
    key_gram = jnp.einsum("hcd,hsd->hcs", keyset, keyset, precision=highest)
    lower_part = jnp.where(
        (col_pos < row_pos)[None], beta_head[:, :, None] * decay_mat * key_gram, 0.0
    )
    system = lower_part + jnp.eye(length, dtype=jnp.float32)
    rhs_vals = beta_head[:, :, None] * valset - (beta_head * carry_in)[:, :, None] * jnp.einsum(
        "hcd,hvd->hcv", keyset, carried, precision=highest
    )
    fresh = jax.vmap(solve_lower)(system, rhs_vals)
    scores = decay_mat * jnp.einsum("hcd,hsd->hcs", queries, keyset, precision=highest)
    outputs = carry_in[:, :, None] * jnp.einsum(
        "hcd,hvd->hcv", queries, carried, precision=highest
    ) + jnp.einsum("hcs,hsv->hcv", scores, fresh, precision=highest)
    weighted = decay_mat[:, -1, :, None] * keyset
    updated = carry_in[:, -1, None, None] * carried + jnp.einsum(
        "hsv,hsd->hvd", fresh, weighted, precision=highest
    )
    return (updated, jnp.swapaxes(outputs, 0, 1))


def run_groups(
    start_state, query_vecs, key_vecs, val_vecs, strength, log_decay, doc_part, prev_docs
):
    pieces = tuple(
        (
            member.reshape((-1, GROUP) + member.shape[1:])
            for member in (query_vecs, key_vecs, val_vecs, strength, log_decay, doc_part)
        )
    ) + (prev_docs,)

    def advance(carried, piece):
        return group_step(carried, *piece)

    final, outputs = lax.scan(advance, start_state, pieces)
    return (final, outputs.reshape((-1,) + outputs.shape[2:]))


def head_output(ext_out, incoming, gate_out, head_gain):
    head_out = ext_out[..., :DV] + jnp.einsum(
        "thd,hvd->thv", ext_out[..., DV:], incoming, precision=highest
    )
    return rms_scale(head_out, head_gain) * jax.nn.silu(gate_out)


def swiglu(gate_up):
    return jax.nn.silu(gate_up[:, 0]) * gate_up[:, 1]


def pass_states(transfer_mats, offsets, backward):
    step_by = -1 if backward else 1

    def turn(turn_index, carry):
        running, arrived = carry
        arrived = passed_along(running, "seq", step_by)
        running = jnp.einsum("hvj,hjk->hvk", arrived, transfer_mats, precision=highest) + offsets
        return (running, arrived)

    return lax.fori_loop(0, lax.axis_size("seq") - 1, turn, (offsets, jnp.zeros_like(offsets)))[1]


def local(
    tokens,
    mixer_gain,
    mixer_weight,
    rate_weight,
    conv_weight,
    decay_log,
    decay_bias,
    head_gain,
    output_weight,
    feed_gain,
    gate_up_weight,
    down_weight,
    doc_starts,
    cotangent,
):
    resid = tokens.astype(jnp.float32)
    norm_one, norm_one_back = jax.vjp(rms_scale, resid, mixer_gain)
    normed = norm_one.astype(jnp.bfloat16)
    gathered = lax.all_gather(normed, "head", axis=0, tiled=True)
    tok_count = gathered.shape[0]
    head_count = mixer_weight.shape[1]
    conv_width = 2 * DK + DV
    projected = jnp.dot(
        gathered, mixer_weight.reshape(D, head_count * MIXW), preferred_element_type=jnp.float32
    ).reshape(tok_count, head_count, MIXW)
    rate_proj = jnp.einsum("td,dgh->tgh", gathered, rate_weight, preferred_element_type=jnp.float32)
    pre_conv = projected[..., :conv_width].astype(jnp.bfloat16)
    gate_out = projected[..., conv_width:]
    rim_rows = passed_along(pre_conv[tok_count - KCONV + 1 :], "seq", 1)
    padded = jnp.concatenate([rim_rows, pre_conv]).astype(jnp.float32)
    first_pos = lax.axis_index("seq") * tok_count
    positions = first_pos + jnp.arange(-(KCONV - 1), tok_count, dtype=jnp.int32)
    doc_pad = doc_index(doc_starts, positions)
    prev_docs = doc_pad[KCONV - 2 : KCONV - 2 + tok_count : GROUP]

    def mixer_local(padded_in, rate_in, conv_in, decay_in, bias_in):
        query_vecs, key_vecs, val_vecs, strength, log_decay = mixer_inputs(
            padded_in, doc_pad, rate_in, conv_in, decay_in, bias_in
        )
        extended = jnp.concatenate(
            [val_vecs, jnp.zeros((tok_count, head_count, DK), jnp.float32)], axis=2
        )
        start_state = jnp.concatenate(
            [
                jnp.zeros((head_count, DV, DK), jnp.float32),
                jnp.broadcast_to(jnp.eye(DK, dtype=jnp.float32), (head_count, DK, DK)),
            ],
            axis=1,
        )
        final, ext_out = run_groups(
            start_state,
            query_vecs,
            key_vecs,
            extended,
            strength,
            log_decay,
            doc_pad[KCONV - 1 :],
            prev_docs,
        )
        return (ext_out, final)

    (ext_out, final), mixer_back = jax.vjp(
        mixer_local, padded, rate_proj, conv_weight.astype(jnp.float32), decay_log, decay_bias
    )
    offsets = final[:, :DV]
    transfer_mats = final[:, DV:]
    incoming = pass_states(transfer_mats, offsets, False)
    gated, head_back = jax.vjp(head_output, ext_out, incoming, gate_out, head_gain)
    gated_low = gated.astype(jnp.bfloat16)
    gated_flat = gated_low.reshape(tok_count, head_count * DV)
    out_flat = output_weight.reshape(head_count * DV, D)
    mixed = lax.psum_scatter(
        jnp.dot(gated_flat, out_flat, preferred_element_type=jnp.float32),
        "head",
        scatter_dimension=0,
        tiled=True,
    )
    hidden = resid + mixed
    norm_two, norm_two_back = jax.vjp(rms_scale, hidden, feed_gain)
    normed_two = norm_two.astype(jnp.bfloat16)
    gathered_two, cot_rows = (
        lax.all_gather(normed_two, "head", axis=0, tiled=True),
        lax.all_gather(cotangent, "head", axis=0, tiled=True),
    )
    gate_up = jnp.einsum(
        "td,dgf->tgf", gathered_two, gate_up_weight, preferred_element_type=jnp.float32
    )
    middle, swiglu_back = jax.vjp(swiglu, gate_up)
    middle_low = middle.astype(jnp.bfloat16)
    feed_sum = lax.psum_scatter(
        jnp.dot(middle_low, down_weight, preferred_element_type=jnp.float32).astype(jnp.bfloat16),
        "head",
        scatter_dimension=0,
        tiled=True,
    ).astype(jnp.float32)
    layer_out = (hidden + feed_sum).astype(jnp.bfloat16)
    d_middle = jnp.einsum("td,fd->tf", cot_rows, down_weight, preferred_element_type=jnp.float32)
    grad_down = jnp.einsum("tf,td->fd", middle_low, cot_rows, preferred_element_type=jnp.float32)
    d_gate_up = swiglu_back(d_middle)[0].astype(jnp.bfloat16)
    grad_gate_up = jnp.einsum(
        "td,tgf->dgf", gathered_two, d_gate_up, preferred_element_type=jnp.float32
    )
    piece = d_gate_up
    d_normed_two = lax.psum_scatter(
        jnp.einsum("tgf,dgf->td", piece, gate_up_weight, preferred_element_type=jnp.float32).astype(
            jnp.bfloat16
        ),
        "head",
        scatter_dimension=0,
        tiled=True,
    ).astype(jnp.float32)
    d_hidden_norm, grad_feed_gain = norm_two_back(d_normed_two)
    d_hidden = cotangent.astype(jnp.float32) + d_hidden_norm
    d_mixed = lax.all_gather(d_hidden.astype(jnp.bfloat16), "head", axis=0, tiled=True)
    d_gated = jnp.einsum("td,hvd->thv", d_mixed, output_weight, preferred_element_type=jnp.float32)
    grad_output = jnp.einsum("thv,td->hvd", gated_low, d_mixed, preferred_element_type=jnp.float32)
    d_ext, d_incoming, d_gate_out, grad_head_gain = head_back(d_gated)
    later = pass_states(jnp.swapaxes(transfer_mats, 1, 2), d_incoming, True)
    d_final = jnp.concatenate(
        [later, jnp.einsum("hvj,hvk->hjk", incoming, later, precision=highest)], axis=1
    )
    d_padded, d_rate_proj, grad_conv, grad_decay_log, grad_decay_bias = mixer_back((d_ext, d_final))
    returned = passed_along(d_padded[: KCONV - 1], "seq", -1)
    d_pre_conv = d_padded[KCONV - 1 :] + jnp.concatenate(
        [jnp.zeros((tok_count - KCONV + 1, head_count, conv_width), jnp.float32), returned]
    )
    d_projected = jnp.concatenate([d_pre_conv, d_gate_out], axis=2).astype(jnp.bfloat16)
    d_rate_low = d_rate_proj.astype(jnp.bfloat16)
    grad_mixer = jnp.einsum(
        "td,thw->dhw", gathered, d_projected, preferred_element_type=jnp.float32
    )
    grad_rate = jnp.einsum("td,tgh->dgh", gathered, d_rate_low, preferred_element_type=jnp.float32)
    piece = d_projected
    main_part = jnp.einsum("thw,dhw->td", piece, mixer_weight, preferred_element_type=jnp.float32)
    d_normed = lax.psum_scatter(
        (
            main_part
            + jnp.einsum("tgh,dgh->td", d_rate_low, rate_weight, preferred_element_type=jnp.float32)
        ).astype(jnp.bfloat16),
        "head",
        scatter_dimension=0,
        tiled=True,
    ).astype(jnp.float32)
    d_resid, grad_mixer_gain = norm_one_back(d_normed)
    grad_tokens = d_hidden + d_resid
    grad_mixer, grad_rate, grad_output, grad_gate_up, grad_down = (
        lax.psum_scatter(
            grad_mixer.astype(jnp.bfloat16), "seq", scatter_dimension=0, tiled=True
        ).astype(jnp.float32),
        lax.psum_scatter(
            grad_rate.astype(jnp.bfloat16), "seq", scatter_dimension=0, tiled=True
        ).astype(jnp.float32),
        lax.psum_scatter(
            grad_output.astype(jnp.bfloat16), "seq", scatter_dimension=2, tiled=True
        ).astype(jnp.float32),
        lax.psum_scatter(
            grad_gate_up.astype(jnp.bfloat16), "seq", scatter_dimension=0, tiled=True
        ).astype(jnp.float32),
        lax.psum_scatter(
            grad_down.astype(jnp.bfloat16), "seq", scatter_dimension=1, tiled=True
        ).astype(jnp.float32),
    )
    grad_conv, grad_decay_log, grad_decay_bias = lax.psum(
        (grad_conv, grad_decay_log, grad_decay_bias), "seq"
    )
    grad_mixer_gain, grad_feed_gain, grad_head_gain = lax.psum(
        (grad_mixer_gain, grad_feed_gain, grad_head_gain), ("seq", "head")
    )
    return (
        layer_out,
        grad_tokens,
        grad_mixer_gain,
        grad_mixer,
        grad_rate,
        grad_conv,
        grad_decay_log,
        grad_decay_bias,
        grad_head_gain,
        grad_output,
        grad_feed_gain,
        grad_gate_up,
        grad_down,
    )


def solution(mesh):
    return jax.shard_map(
        local,
        mesh=mesh,
        in_specs=(
            P(("seq", "head"), None),
            P(),
            P(None, "head", None),
            P(None, None, "head"),
            P(None, "head", None),
            P("head"),
            P("head"),
            P(),
            P("head", None, None),
            P(),
            P(None, None, "head"),
            P("head", None),
            P(),
            P(("seq", "head"), None),
        ),
        out_specs=(
            P(("seq", "head"), None),
            P(("seq", "head"), None),
            P(),
            P("seq", "head", None),
            P("seq", None, "head"),
            P(None, "head", None),
            P("head"),
            P("head"),
            P(),
            P("head", None, "seq"),
            P(),
            P("seq", None, "head"),
            P("head", "seq"),
        ),
        check_vma=False,
    )
```

profile of v0, /device:TPU:1, one launch (start us, length us, event | category | flops | bytes accessed | tf_op | source)
XLA Modules:
  0.0 1731.2 jit_solution(7716297149072949579)
XLA Ops:
  29.7 10.7 all-gather.5.cloned.1.call-done
  66.7 272.9 %while.122 = (s32[]{:T(128)}, f32[2,384,128]{2,1,0:T(8,128)S(1)}, f32[8,64,2,384]{3,1,0,2:T(8,128)}, pred[8,2,64,64]{3,2,1,0:T(32,128)(4,1)}, f32[8,2,64,64]{3,2...) while((s32[]{:T(128)}, f32[2,384,128]{2,1,0:T(8,128)S(1)}, ...), condition=%wide.region_6.7_spmd.clone, body=%wide.region_4.6_spmd.clone.sunk | while | flops 327877120 | bytes 6835273 | solution.py:106
  69.9 9.8 custom-call.53
  104.0 9.8 custom-call.53
  138.1 9.8 custom-call.53
  172.1 9.8 custom-call.53
  206.2 9.8 custom-call.53
  240.4 9.8 custom-call.53
  274.5 9.8 custom-call.53
  308.7 9.8 custom-call.53
  341.8 172.7 %while.120 = (s32[]{:T(128)}, f32[2,256,128]{2,1,0:T(8,128)}, f32[2,256,128]{2,1,0:T(8,128)}, f32[2,128,128]{2,1,0:T(8,128)}, f32[2,256,128]{2,1,0:T(8,128)S(1)}, /*index=5*/s32[]{:T(128)}) while((s32[]{:T(128)}, f32[2,256,128]{2,1,0:T(8,128)}, f32[2,256,128]{2,1,0:T(8,128)}, f32[2,128,128]{2,1,0:T(8,128)}, f32[2,256,128]{2,1,0:T(8,128)S(1)}, ...), condition=%wide.region_8.9_spmd, body=%wide.region_7.8_spmd.sunk | while | flops 100728832 | bytes 3014793 | solution.py:130
  524.1 60.3 %reduce-scatter.18.cloned.1.call-done = f32[64,2048]{1,0:T(8,128)} async-done(((f32[512,2048]{1,0:T(8,128)}), f32[64,2048]{1,0:T(8,128)}) %reduce-scatter.18.cloned.1.call-update) | async-done | bytes 524304 | tf_op jit(solution)/shard_map/reduce_scatter | solution.py:205
  587.4 26.9 %all-gather.7.cloned.1.call-done = bf16[512,2048]{1,0:T(8,128)(2,1)} async-done(((bf16[64,2048]{1,0:T(8,128)(2,1)}), bf16[512,2048]{1,0:T(8,128)(2,1)}) %all-gather.7.cloned.1.call-update) | async-done | bytes 2097168 | tf_op jit(solution)/shard_map/all_gather | solution.py:215
  622.2 19.1 %all-gather.9.cloned.1.call-done = bf16[512,2048]{1,0:T(8,128)(2,1)} async-done(((bf16[64,2048]{1,0:T(8,128)(2,1)}), bf16[512,2048]{1,0:T(8,128)(2,1)}) %all-gather.9.cloned.1.call-update) | async-done | bytes 2097168 | tf_op jit(solution)/shard_map/all_gather | solution.py:216
  655.6 30.7 %reduce-scatter.22.cloned.1.call-done = bf16[64,2048]{1,0:T(8,128)(2,1)} async-done(((bf16[512,2048]{1,0:T(8,128)(2,1)}), bf16[64,2048]{1,0:T(8,128)(2,1)}) %reduce-scatter.22.cloned.1.call-update) | async-done | bytes 262160 | tf_op jit(solution)/shard_map/reduce_scatter | solution.py:237
  700.9 16.6 all-gather.11.cloned.1.call-done
  732.0 188.6 %while.121 = (s32[]{:T(128)}, f32[2,256,128]{2,1,0:T(8,128)}, f32[2,256,128]{2,1,0:T(8,128)}, f32[2,128,128]{2,1,0:T(8,128)S(1)}, f32[2,256,128]{2,1,0:T(8,128)}, /*index=5*/s32[]{:T(128)}) while((s32[]{:T(128)}, f32[2,256,128]{2,1,0:T(8,128)}, f32[2,256,128]{2,1,0:T(8,128)}, f32[2,128,128]{2,1,0:T(8,128)S(1)}, f32[2,256,128]{2,1,0:T(8,128)}, ...), condition=%wide.region_17.18_spmd, body=%wide.region_16.17_spmd.sunk | while | flops 100728832 | bytes 3014793 | solution.py:130
  733.5 11.0 collective-permute-done.1
  747.8 10.5 collective-permute-done.1
  865.4 10.5 collective-permute-done.1
  879.3 11.8 collective-permute-done.1
  894.6 10.6 collective-permute-done.1
  908.6 9.9 collective-permute-done.1
  927.5 382.1 %while.123 = (s32[]{:T(128)}, f32[2,384,128]{2,1,0:T(8,128)S(1)}, f32[8,64,2,128]{3,1,0,2:T(8,128)}, f32[8,64,2,128]{3,1,0,2:T(8,128)}, f32[8,64,2,384]{3,1,0,2:...) while((s32[]{:T(128)}, f32[2,384,128]{2,1,0:T(8,128)S(1)}, ...), condition=%wide.region_28.29_spmd.clone, body=%wide.region_18.28_spmd.clone.sunk | while | flops 662155712 | bytes 10552401 | solution.py:106
  931.9 9.8 custom-call.54
  979.6 9.8 custom-call.54
  1386.1 60.7 %all-reduce.23 = (f32[4,2,512]{2,1,0:T(2,128)}, f32[2]{0:T(128)}, f32[2]{0:T(128)}) all-reduce(f32[4,2,512]{2,1,0:T(2,128)S(1)} %pad_add_fusion.3, f32[2]{0:T(128)S(1)} %negate_multiply_fusion, f32[2]{0:T(128)S(1)} %get-tuple-element.2074), channel_id=1, replica_groups=mesh['seq'=16,'head'=8] {'seq'}, use_global_device_ids=true, to_apply=%region_41.42 | all-reduce | flops 4100 | bytes 32800 | tf_op jit(solution)/shard_map/psum | solution.py:296
  1448.1 43.0 %reduce-scatter.32.cloned.1.call-done = bf16[128,1376]{1,0:T(8,128)(2,1)} async-done(((bf16[2048,1376]{1,0:T(8,128)(2,1)}), bf16[128,1376]{1,0:T(8,128)(2,1)}) %reduce-scatter.32.cloned.1.call-update) | async-done | bytes 352272
  1494.9 72.9 %reduce-scatter.30.cloned.1.call-done = bf16[128,512]{1,0:T(8,128)(2,1)} async-done(((bf16[2048,512]{1,0:T(8,128)(2,1)}), bf16[128,512]{1,0:T(8,128)(2,1)}) %reduce-scatter.30.cloned.1.call-update) | async-done | bytes 131088
  1571.1 30.5 %reduce-scatter.24.cloned.1.call-done = bf16[64,2048]{1,0:T(8,128)(2,1)} async-done(((bf16[512,2048]{1,0:T(8,128)(2,1)}), bf16[64,2048]{1,0:T(8,128)(2,1)}) %reduce-scatter.24.cloned.1.call-update) | async-done | bytes 262160 | tf_op jit(solution)/shard_map/reduce_scatter | solution.py:268
  1603.0 68.8 %all-reduce.22 = (f32[2048]{0:T(1024)}, f32[256]{0:T(256)}, f32[2048]{0:T(1024)}) all-reduce(f32[2048]{0:T(1024)S(1)} %get-tuple-element.2072, f32[256]{0:T(256)S(1)} %copy-done.62, f32[2048]{0:T(1024)S(1)} %copy-done.42), channel_id=1, replica_groups=mesh['seq'=16,'head'=8] {'seq','head'}, use_global_device_ids=true, to_apply=%region_34.35 | all-reduce | flops 4352 | bytes 34816 | tf_op jit(solution)/shard_map/psum | solution.py:299
  1674.4 47.8 %reduce-scatter.26.cloned.1.call-done = bf16[128,2,768]{2,0,1:T(8,128)(2,1)} async-done(((bf16[2048,2,768]{2,0,1:T(8,128)(2,1)}), bf16[128,2,768]{2,0,1:T(8,128)(2,1)}) %reduce-scatter.26.cloned.1.call-update) | async-done | bytes 393232 | tf_op jit(solution)/shard_map/reduce_scatter | solution.py:280
  (954 shorter events, 1064.0 us)
Async XLA Ops:
  7.2 33.2 %all-gather.5.cloned.1.call-start = ((), (), s32[]{:S(2)}) async-start(), calls=%async_computation.9 | async-start | bytes 2359296 | tf_op jit(solution)/shard_map/all_gather | solution.py:152
  11.5 572.9 %reduce-scatter.18.cloned.1.call-start = ((), (), s32[]{:S(2)}) async-start(), calls=%async_computation.10 | async-start | bytes 4718592 | tf_op jit(solution)/shard_map/reduce_scatter | solution.py:205
  391.6 9.7 collective-permute-start
  403.4 9.4 collective-permute-start
  414.9 9.4 collective-permute-start
  437.9 9.5 collective-permute-start
  449.5 10.9 collective-permute-start
  462.5 12.3 collective-permute-start
  477.0 12.5 collective-permute-start
  491.5 10.2 collective-permute-start
  524.0 90.2 %all-gather.7.cloned.1.call-start = ((), (), s32[]{:S(2)}) async-start(), calls=%async_computation.11 | async-start | bytes 2359296 | tf_op jit(solution)/shard_map/all_gather | solution.py:215
  586.6 54.8 %all-gather.9.cloned.1.call-start = ((), (), s32[]{:S(2)}) async-start(), calls=%async_computation.13 | async-start | bytes 2359296 | tf_op jit(solution)/shard_map/all_gather | solution.py:216
  587.1 99.2 %reduce-scatter.22.cloned.1.call-start = ((), (), s32[]{:S(2)}) async-start(), calls=%async_computation.14 | async-start | bytes 2359296 | tf_op jit(solution)/shard_map/reduce_scatter | solution.py:237
  655.6 61.9 %all-gather.11.cloned.1.call-start = ((), (), s32[]{:S(2)}) async-start(), calls=%async_computation.15 | async-start | bytes 2359296 | tf_op jit(solution)/shard_map/all_gather | solution.py:247
  690.0 691.7 %reduce-scatter.34.cloned.1.call-start = ((), (), s32[]{:S(2)}) async-start(), calls=%async_computation.21 | async-start | bytes 3342336
  700.8 745.9 %reduce-scatter.28.cloned.1.call-start = ((), (), s32[]{:S(2)}) async-start(), calls=%async_computation.18 | async-start | bytes 557056
  732.2 12.3 collective-permute-start.1
  746.5 11.7 collective-permute-start.1
  760.4 10.0 collective-permute-start.1
  772.6 10.3 collective-permute-start.1
  828.6 9.4 collective-permute-start.1
  840.2 9.4 collective-permute-start.1
  851.7 10.3 collective-permute-start.1
  864.1 11.8 collective-permute-start.1
  878.0 13.1 collective-permute-start.1
  893.3 11.9 collective-permute-start.1
  907.3 11.2 collective-permute-start.1
  1315.6 175.5 %reduce-scatter.32.cloned.1.call-start = ((), (), s32[]{:S(2)}) async-start(), calls=%async_computation.20 | async-start | bytes 6127616
  1331.7 236.0 %reduce-scatter.30.cloned.1.call-start = ((), (), s32[]{:S(2)}) async-start(), calls=%async_computation.19 | async-start | bytes 2228224
  1346.5 255.1 %reduce-scatter.24.cloned.1.call-start = ((), (), s32[]{:S(2)}) async-start(), calls=%async_computation.16 | async-start | bytes 2359296 | tf_op jit(solution)/shard_map/reduce_scatter | solution.py:268
  1368.3 303.5 %reduce-scatter.20.cloned.1.call-start = ((), (), s32[]{:S(2)}) async-start(), calls=%async_computation.12 | async-start | bytes 2359296 | tf_op jit(solution)/shard_map/reduce_scatter | solution.py:223
  1372.6 349.6 %reduce-scatter.26.cloned.1.call-start = ((), (), s32[]{:S(2)}) async-start(), calls=%async_computation.17 | async-start | bytes 6684672 | tf_op jit(solution)/shard_map/reduce_scatter | solution.py:280
  (114 other events, 3971.6 us)
Sparse Core Ops, SparseCore 0:
  11.6 28.7 all-gather.4
  524.1 60.1 reduce-scatter.17
  586.7 27.5 all-gather.6
  615.8 25.4 all-gather.8
  655.7 30.5 reduce-scatter.21
  690.1 27.2 all-gather.10
  720.8 77.1 reduce-scatter.33
  1315.8 91.3 reduce-scatter.27
  1411.0 80.0 reduce-scatter.31
  1494.6 73.1 reduce-scatter.29
  1570.2 31.3 reduce-scatter.23
  1603.9 32.8 reduce-scatter.19
  1640.2 81.9 reduce-scatter.25
where the time goes:
time: 1750 us; the launch traced here: 1730 us
  waiting for transfers between devices  562 us (32%)
  matrix products  429 us (25%)
  other arithmetic  302 us (17%)
  local copies, waits for them, and re-layouts  187 us (11%)
  blocking collectives  129 us (7%)
  starting transfers between devices  104 us (6%)
    ppermute x32, waiting for transfers between devices, passed_along(): return lax.ppermute(shard, axis, pairs)  203 us
    another operation x72, other arithmetic, solve_lower(): jax.scipy.linalg.solve_triangular(system, rhs_vals, lower=True, unit_diag...  166 us
    unnamed x17, waiting for transfers between devices  117 us
    ppermute x32, starting transfers between devices, passed_along(): return lax.ppermute(shard, axis, pairs)  103 us
    psum x1, blocking collectives, local(): lax.psum((grad_mixer_gain, grad_feed_gain, grad_head_gain), ('seq', 'head'))  68.8 us
    dot_general x30, matrix products, turn(): jnp.einsum('hvj,hjk->hvk', arrived, transfer_mats, precision=highest)  62.9 us
    psum x1, blocking collectives, local(): lax.psum((grad_conv, grad_decay_log, grad_decay_bias), 'seq')  60.7 us
    reduce_scatter x1, waiting for transfers between devices, local(): lax.psum_scatter(jnp.dot(gated_flat, out_flat, preferred_element_type=jnp...  60.3 us
  transfers between devices with their start and end apart: 45, of which 41 were waited for; matrix products, arithmetic and copies ran while one was open for 32% of the time, Pallas kernels for 0%

commit v1 on v0

v1 whole, which is shorter than its diff:
```python
import functools

import jax
import jax.numpy as jnp
from jax import lax
from jax.experimental import pallas as pl
from jax.experimental.pallas import tpu as pltpu
from jax.sharding import PartitionSpec as P

D = 2048
DK = 128
DV = 256
KCONV = 4
MIXW = 768
CONVW = 512
NB = 4
BLK = 256
PAD = 8
F32 = jnp.float32
BF16 = jnp.bfloat16

VMEM = pl.BlockSpec(memory_space=pltpu.VMEM)
SMEM = pl.BlockSpec(memory_space=pltpu.SMEM)


def dot(a, b, form="nn"):
    dims = {"nn": ((1,), (0,)), "nt": ((1,), (1,)), "tn": ((0,), (0,))}[form]
    return lax.dot_general(a.astype(BF16), b.astype(BF16), (dims, ((), ())), preferred_element_type=F32)


def halves(a):
    hi = a.astype(BF16)
    return hi, (a - hi.astype(F32)).astype(BF16)


def dot3(a, b, form="nn"):
    ah, al = halves(a)
    bh, bl = halves(b)
    return dot(ah, bh, form) + (dot(ah, bl, form) + dot(al, bh, form))


def dot_exact_left(a, b, form="nn"):
    b1, rest = halves(b)
    rest = b - b1.astype(F32)
    b2 = rest.astype(BF16)
    b3 = (rest - b2.astype(F32)).astype(BF16)
    return dot(a, b1, form) + (dot(a, b2, form) + dot(a, b3, form))


def iota(shape, axis):
    return lax.broadcasted_iota(jnp.int32, shape, axis)


def doc_of(info, pos):
    count = jnp.zeros(pos.shape, jnp.int32)
    for i in range(NB):
        count = count + jnp.where(pos >= info[i], 1, 0)
    return jnp.where(pos < 0, -1, count)


def sigmoid(v):
    return 1.0 / (1.0 + jnp.exp(-v))


def softplus(v):
    return jnp.maximum(v, 0.0) + jnp.log1p(jnp.exp(-jnp.abs(v)))


def unit_lower_inverse(low):
    n = low.shape[0]
    row, col = iota((n, n), 0), iota((n, n), 1)
    eye = jnp.where(row == col, 1.0, 0.0)

    def same(b):
        return row // b == col // b

    x = jnp.where(same(8), -low, 0.0)
    inv = eye + x
    x = dot3(x, x)
    inv = inv + dot3(inv, x)
    x = dot3(x, x)
    inv = inv + dot3(inv, x)
    b = 8
    while b < n:
        off = jnp.where(same(2 * b) & jnp.logical_not(same(b)), low, 0.0)
        inv = inv - dot3(inv, dot3(off, inv))
        b *= 2
    return inv


def valid_column(info, rows, back):
    pos = info[NB] + iota((rows, 1), 0)
    return jnp.where(doc_of(info, pos) == doc_of(info, pos - back), 1.0, 0.0)


def vectors(conv):
    act = conv * sigmoid(conv)
    qa, ka, va = act[:, :DK], act[:, DK : 2 * DK], act[:, 2 * DK :]
    rq = lax.rsqrt(jnp.sum(qa * qa, axis=1, keepdims=True) + 1e-06)
    rk = lax.rsqrt(jnp.sum(ka * ka, axis=1, keepdims=True) + 1e-06)
    return qa, ka, va, rq, rk


def rates(rate_ref, dlog_ref, dbias_ref):
    heads = dlog_ref.shape[1]
    pre = rate_ref[:, :heads] + dbias_ref[...]
    log_decay = -jnp.exp(dlog_ref[...]) * softplus(pre)
    return sigmoid(rate_ref[:, heads:]), log_decay, pre


def block_masks(info, c):
    row, col = iota((BLK, BLK), 0), iota((BLK, BLK), 1)
    base = info[NB] + c * BLK
    docs_r, docs_c = doc_of(info, base + row), doc_of(info, base + col)
    keep = (docs_r == docs_c) & (col <= row)
    column = doc_of(info, base + iota((BLK, 1), 0))
    first = jnp.where(column == doc_of(info, base - 1 + iota((BLK, 1), 0) * 0), 1.0, 0.0)
    last = jnp.where(column == doc_of(info, base + BLK - 1 + iota((BLK, 1), 0) * 0), 1.0, 0.0)
    tri = jnp.where(col <= row, 1.0, 0.0)
    strict = jnp.where(col < row, 1.0, 0.0)
    return keep, first, last, tri, strict


def decays(g, first, last, tri):
    cum = dot_exact_left(tri, jnp.broadcast_to(g, (BLK, DK)))[:, :1]
    carry = first * jnp.exp(cum)
    to_end = last * jnp.exp(cum[BLK - 1 :, :] - cum)
    return carry, to_end


def fwd_prep(info, proj, halo, rate, convw, dlog, dbias, conv_o, dec_o, inv_o, wu_o, qe_o, ol_o, step_o, ab_o, xpad):
    rows = proj.shape[0]
    heads = dlog.shape[1]
    blocks = rows // BLK
    strength, log_decay, _ = rates(rate, dlog, dbias)
    valid = [valid_column(info, rows, KCONV - 1 - j) for j in range(KCONV)]
    for h in range(heads):
        src, dst = pl.ds(h * MIXW, CONVW), pl.ds(h * CONVW, CONVW)
        xpad[:PAD, :] = halo[:, dst]
        xpad[PAD:, :] = proj[:, src].astype(BF16).astype(F32)
        conv = jnp.zeros((rows, CONVW), F32)
        for j in range(KCONV):
            lo = PAD - (KCONV - 1) + j
            conv = conv + convw[j : j + 1, dst].astype(F32) * xpad[lo : lo + rows, :] * valid[j]
        conv_o[:, dst] = conv
    for c in range(blocks):
        keep, first, last, tri, strict = block_masks(info, c)
        here = pl.ds(c * BLK, BLK)
        for h in range(heads):
            qa, ka, va, rq, rk = vectors(conv_o[here, pl.ds(h * CONVW, CONVW)])
            q, k = qa * (rq * DK**-0.5), ka * rk
            beta = strength[c * BLK : (c + 1) * BLK, h : h + 1]
            g = log_decay[c * BLK : (c + 1) * BLK, h : h + 1]
            spread = dot_exact_left(tri, g * strict)
            dec = jnp.where(keep, jnp.exp(jnp.where(keep, spread, 0.0)), 0.0)
            carry, to_end = decays(g, first, last, tri)
            low = strict * (beta * dec * dot(k, k, "nt"))
            inv = unit_lower_inverse(low)
            u = h * blocks + c
            dec_o[u] = dec
            inv_o[u] = inv.astype(BF16)
            rhs = jnp.concatenate([(beta * carry) * k, beta * va], axis=1)
            wu = dot(inv, rhs)
            wu_o[u] = wu
            out = dot(dec * dot(q, k, "nt"), wu)
            qe_o[here, pl.ds(h * DK, DK)] = carry * q - out[:, :DK]
            ol_o[here, pl.ds(h * DV, DV)] = out[:, DK:]
            step = dot(wu, to_end * k, "tn")
            eye = jnp.where(iota((DK, DK), 0) == iota((DK, DK), 1), 1.0, 0.0)
            step_o[u, :DK] = carry[BLK - 1 :, :] * eye - step[:DK]
            step_o[u, DK:] = step[DK:]
    for h in range(heads):
        ab = step_o[h * blocks]
        for c in range(1, blocks):
            nxt = step_o[h * blocks + c]
            ab = dot3(ab, nxt[:DK])
            ab_o_tail = nxt[DK:]
            ab = jnp.concatenate([ab[:DK], ab[DK:] + ab_o_tail], axis=0)
        ab_o[h] = ab.astype(ab_o.dtype)


def fwd_out(info, all_ab, step, qe, ol, proj, gain, states_o, head_o, gated_o):
    rows = qe.shape[0]
    heads = all_ab.shape[1]
    blocks = rows // BLK
    me = info[NB + 1]

    def chain(j, held):
        return tuple(
            dot_left2(held[h], all_ab[j, h, :DK, :]) + all_ab[j, h, DK:, :].astype(F32) for h in range(heads)
        )

    start = lax.fori_loop(0, me, chain, tuple(jnp.zeros((DV, DK), F32) for _ in range(heads)))
    for h in range(heads):
        state = start[h]
        for c in range(blocks):
            u = h * blocks + c
            here = pl.ds(c * BLK, BLK)
            states_o[u] = state
            out = ol[here, pl.ds(h * DV, DV)] + dot(qe[here, pl.ds(h * DK, DK)], state, "nt")
            head_o[here, pl.ds(h * DV, DV)] = out
            gate = proj[here, pl.ds(h * MIXW + CONVW, DV)]
            scale = lax.rsqrt(jnp.mean(out * out, axis=1, keepdims=True) + 1e-05)
            gated_o[here, pl.ds(h * DV, DV)] = (out * scale * gain[...] * (gate * sigmoid(gate))).astype(BF16)
            if c + 1 < blocks:
                state = dot3(state, step[u, :DK, :]) + step[u, DK:, :]


def dot_left2(a, b, form="nn"):
    ah, al = halves(a)
    return dot(ah, b, form) + dot(al, b, form)


def bwd_head(d_gated, head_out, proj, gain, qe, step, d_out_o, d_gate_o, d_gain_o, y_o, inc_o):
    rows = qe.shape[0]
    blocks = rows // BLK
    heads = qe.shape[1] // DK
    total = jnp.zeros((1, DV), F32)
    for h in range(heads):
        cols = pl.ds(h * DV, DV)
        for c in range(blocks):
            here = pl.ds(c * BLK, BLK)
            dg, out = d_gated[here, cols], head_out[here, cols]
            gate = proj[here, pl.ds(h * MIXW + CONVW, DV)]
            s = sigmoid(gate)
            silu = gate * s
            scale = lax.rsqrt(jnp.mean(out * out, axis=1, keepdims=True) + 1e-05)
            n = out * scale
            dn = dg * n
            d_gate_o[here, cols] = (dn * gain[...] * (s * (1.0 + gate * (1.0 - s)))).astype(BF16)
            total = total + jnp.sum(dn * silu, axis=0, keepdims=True)
            f = dg * gain[...] * silu
            d_out = scale * f - out * (scale * scale * scale) * jnp.mean(f * out, axis=1, keepdims=True)
            d_out_o[here, cols] = d_out
            y_o[h * blocks + c] = dot(d_out, qe[here, pl.ds(h * DK, DK)], "tn")
        inc = y_o[h * blocks + blocks - 1]
        for c in range(blocks - 2, -1, -1):
            inc = y_o[h * blocks + c] + dot3(inc, step[h * blocks + c, :DK, :], "nt")
        inc_o[h] = inc.astype(inc_o.dtype)
    d_gain_o[...] = total


def bwd_mix(
    info, all_ab, all_inc, conv, dec, inv, wu, states, step, y, d_out, rate, proj, halo, convw, dlog, dbias,
    d_pre_o, d_edge_o, d_rate_o, d_convw_o, d_decay_o, xpad, dpad, dsend, cols_s
):
    rows = d_out.shape[0]
    heads = all_ab.shape[1]
    blocks = rows // BLK
    me = info[NB + 1]
    last_dev = all_ab.shape[0] - 1
    strength, log_decay, pre = rates(rate, dlog, dbias)
    valid = [valid_column(info, rows, KCONV - 1 - j) for j in range(KCONV)]

    def chain(i, held):
        j = last_dev - i
        return tuple(
            dot_left2(held[h], all_ab[j, h, :DK, :], "nt") + all_inc[j, h].astype(F32) for h in range(heads)
        )

    later = lax.fori_loop(0, last_dev - me, chain, tuple(jnp.zeros((DV, DK), F32) for _ in range(heads)))
    for h in range(heads):
        grad = later[h]
        for c in range(blocks - 1, -1, -1):
            u = h * blocks + c
            dsend[u] = grad
            if c:
                grad = dot3(grad, step[u, :DK, :], "nt") + y[u]
    for c in range(blocks):
        keep, first, last, tri, strict = block_masks(info, c)
        here = pl.ds(c * BLK, BLK)
        for h in range(heads):
            u = h * blocks + c
            cv = conv[here, pl.ds(h * CONVW, CONVW)]
            sg = sigmoid(cv)
            qa, ka, va, rq, rk = vectors(cv)
            rqs = rq * DK**-0.5
            q, k = qa * rqs, ka * rk
            beta = strength[c * BLK : (c + 1) * BLK, h : h + 1]
            g = log_decay[c * BLK : (c + 1) * BLK, h : h + 1]
            carry, to_end = decays(g, first, last, tri)
            dm = dec[u]
            sc = dm * dot(q, k, "nt")
            gm = dm * dot(k, k, "nt") * strict
            state, d_end = states[u], dsend[u]
            do = d_out[here, pl.ds(h * DV, DV)]
            ks = dot(k, state, "nt")
            qs = dot(q, state, "nt")
            fresh = wu[u, :, DK:] - dot(wu[u, :, :DK], state, "nt")
            kd = to_end * k
            d_fresh = dot(sc, do, "tn") + dot(kd, d_end, "nt")
            d_rhs = dot(inv[u], d_fresh, "tn")
            d_low = -dot(d_rhs, fresh, "nt")
            d_sc = dot(do, fresh, "nt")
            d_val = beta * d_rhs
            ebar = d_low * gm
            d_beta = jnp.sum(d_rhs * (va - carry * ks), axis=1, keepdims=True) + jnp.sum(ebar, axis=1, keepdims=True)
            e = d_sc * sc + beta * ebar
            d_scd = d_sc * dm
            d_gm = (beta * d_low) * (dm * strict)
            d_kd = dot(fresh, d_end)
            d_q = dot(d_scd, k) + carry * dot(do, state)
            d_k = (
                dot(d_scd, q, "tn")
                - (beta * carry) * dot(d_rhs, state)
                + to_end * d_kd
                + dot(d_gm, k)
                + dot(d_gm, k, "tn")
            )
            hcol = carry * jnp.sum(do * qs - beta * d_rhs * ks, axis=1, keepdims=True)
            fcol = jnp.sum(kd * d_kd, axis=1, keepdims=True)
            tail = carry[BLK - 1 :, :] * jnp.sum(
                jnp.sum(state * d_end, axis=1, keepdims=True), axis=0, keepdims=True
            )
            lane = iota((BLK, DK), 1)
            d_g = (
                jnp.sum(dot_exact_left(tri, e, "tn") * strict, axis=1, keepdims=True)
                + dot_exact_left(tri, jnp.where(lane == 0, hcol, 0.0), "tn")[:, :1]
                + dot_exact_left(strict, jnp.where(lane == 0, fcol, 0.0))[:, :1]
                + tail
            )
            cols_s[here, h : h + 1] = d_g
            cols_s[here, heads + h : heads + h + 1] = d_beta
            d_qa = rqs * d_q - qa * (rqs * rq * rq * jnp.sum(d_q * qa, axis=1, keepdims=True))
            d_ka = rk * d_k - ka * (rk * rk * rk * jnp.sum(d_k * ka, axis=1, keepdims=True))
            d_act = jnp.concatenate([d_qa, d_ka, d_val], axis=1)
            d_pre_o[here, pl.ds(h * CONVW, CONVW)] = d_act * (sg * (1.0 + cv * (1.0 - sg)))
    d_g, d_beta = cols_s[:, :heads], cols_s[:, heads : 2 * heads]
    d_bias = -d_g * jnp.exp(dlog[...]) * sigmoid(pre)
    d_rate_o[:, :heads] = d_bias
    d_rate_o[:, heads:] = d_beta * strength * (1.0 - strength)
    d_decay_o[:, :heads] = jnp.sum(d_g * log_decay, axis=0, keepdims=True)
    d_decay_o[:, heads:] = jnp.sum(d_bias, axis=0, keepdims=True)
    for h in range(heads):
        src, dst = pl.ds(h * MIXW, CONVW), pl.ds(h * CONVW, CONVW)
        xpad[:PAD, :] = halo[:, dst]
        xpad[PAD:, :] = proj[:, src].astype(BF16).astype(F32)
        dpad[...] = jnp.zeros_like(dpad)
        d_conv = d_pre_o[:, dst]
        for j in range(KCONV):
            lo = PAD - (KCONV - 1) + j
            masked = d_conv * valid[j]
            d_convw_o[j : j + 1, dst] = jnp.sum(masked * xpad[lo : lo + rows, :], axis=0, keepdims=True)
            dpad[lo : lo + rows, :] += convw[j : j + 1, dst].astype(F32) * masked
        d_edge_o[:, dst] = dpad[:PAD, :]
        d_pre_o[:, dst] = dpad[PAD:, :]


def call(kernel, outs, scratch, limit, *args, flops=2_000_000_000, nbytes=16_000_000):
    def spec(a):
        return SMEM if a.dtype == jnp.int32 else VMEM

    return pl.pallas_call(
        kernel,
        out_shape=outs,
        in_specs=[spec(a) for a in args],
        out_specs=[VMEM for _ in outs],
        scratch_shapes=scratch,
        compiler_params=pltpu.CompilerParams(vmem_limit_bytes=limit << 20),
        cost_estimate=pl.CostEstimate(flops=flops, bytes_accessed=nbytes, transcendentals=0),
    )(*args)


def sds(shape, dtype=F32):
    return jax.ShapeDtypeStruct(shape, dtype)


def passed_along(shard, axis, by):
    length = lax.axis_size(axis)
    pairs = [(i, i + by) for i in range(length) if 0 <= i + by < length]
    return lax.ppermute(shard, axis, pairs)


def rms_scale(values, gain):
    return values * lax.rsqrt(jnp.mean(values * values, axis=-1, keepdims=True) + 1e-05) * gain


def swiglu(gate_up):
    return jax.nn.silu(gate_up[:, 0]) * gate_up[:, 1]


def local(
    tokens, mixer_gain, mixer_weight, rate_weight, conv_weight, decay_log, decay_bias, head_gain,
    output_weight, feed_gain, gate_up_weight, down_weight, doc_starts, cotangent,
):
    resid = tokens.astype(F32)
    norm_one, norm_one_back = jax.vjp(rms_scale, resid, mixer_gain)
    normed = norm_one.astype(BF16)
    gathered = lax.all_gather(normed, "head", axis=0, tiled=True)
    rows = gathered.shape[0]
    heads = mixer_weight.shape[1]
    blocks = rows // BLK
    units = heads * blocks
    seq = lax.axis_size("seq")
    mixer_flat = mixer_weight.reshape(D, heads * MIXW)
    projected = jnp.dot(gathered, mixer_flat, preferred_element_type=F32)
    rate_proj = jnp.einsum("td,dgh->tgh", gathered, rate_weight, preferred_element_type=F32).reshape(rows, 2 * heads)
    rim = projected[rows - PAD :].reshape(PAD, heads, MIXW)[:, :, :CONVW].reshape(PAD, heads * CONVW).astype(BF16)
    halo = passed_along(rim, "seq", 1).astype(F32)
    convw = conv_weight.reshape(KCONV, heads * CONVW)
    info = jnp.concatenate(
        [doc_starts, jnp.stack([lax.axis_index("seq") * rows, lax.axis_index("seq")]).astype(jnp.int32)]
    )
    dlog, dbias = decay_log.reshape(1, heads), decay_bias.reshape(1, heads)
    gain = head_gain.reshape(1, DV)

    conv, dec, inv, wu, qe, ol, step, ab = call(
        fwd_prep,
        [
            sds((rows, heads * CONVW)), sds((units, BLK, BLK)), sds((units, BLK, BLK), BF16),
            sds((units, BLK, DK + DV)), sds((rows, heads * DK)), sds((rows, heads * DV)),
            sds((units, DK + DV, DK)), sds((heads, DK + DV, DK), BF16),
        ],
        [pltpu.VMEM((PAD + rows, CONVW), F32)],
        56, info, projected, halo, rate_proj, convw, dlog, dbias,
    )
    all_ab = lax.all_gather(ab, "seq", axis=0)
    states, head_out, gated = call(
        fwd_out,
        [sds((units, DV, DK)), sds((rows, heads * DV)), sds((rows, heads * DV), BF16)],
        [], 48, info, all_ab, step, qe, ol, projected, gain,
    )
    out_flat = output_weight.reshape(heads * DV, D)
    mixed = lax.psum_scatter(
        jnp.dot(gated, out_flat, preferred_element_type=F32), "head", scatter_dimension=0, tiled=True
    )
    hidden = resid + mixed
    norm_two, norm_two_back = jax.vjp(rms_scale, hidden, feed_gain)
    normed_two = norm_two.astype(BF16)
    gathered_two = lax.all_gather(normed_two, "head", axis=0, tiled=True)
    cot_rows = lax.all_gather(cotangent, "head", axis=0, tiled=True)
    gate_up = jnp.einsum("td,dgf->tgf", gathered_two, gate_up_weight, preferred_element_type=F32)
    middle, swiglu_back = jax.vjp(swiglu, gate_up)
    middle_low = middle.astype(BF16)
    feed_sum = lax.psum_scatter(
        jnp.dot(middle_low, down_weight, preferred_element_type=F32).astype(BF16),
        "head", scatter_dimension=0, tiled=True,
    ).astype(F32)
    layer_out = (hidden + feed_sum).astype(BF16)
    d_middle = jnp.einsum("td,fd->tf", cot_rows, down_weight, preferred_element_type=F32)
    grad_down = jnp.einsum("tf,td->fd", middle_low, cot_rows, preferred_element_type=F32)
    d_gate_up = swiglu_back(d_middle)[0].astype(BF16)
    grad_gate_up = jnp.einsum("td,tgf->dgf", gathered_two, d_gate_up, preferred_element_type=F32)
    d_normed_two = lax.psum_scatter(
        jnp.einsum("tgf,dgf->td", d_gate_up, gate_up_weight, preferred_element_type=F32).astype(BF16),
        "head", scatter_dimension=0, tiled=True,
    ).astype(F32)
    d_hidden_norm, grad_feed_gain = norm_two_back(d_normed_two)
    d_hidden = cotangent.astype(F32) + d_hidden_norm
    d_mixed = lax.all_gather(d_hidden.astype(BF16), "head", axis=0, tiled=True)
    d_gated = jnp.einsum("td,vd->tv", d_mixed, out_flat, preferred_element_type=F32)
    grad_output = jnp.einsum("tv,td->vd", gated, d_mixed, preferred_element_type=F32)
    d_out, d_gate, grad_head_gain, y, inc = call(
        bwd_head,
        [
            sds((rows, heads * DV)), sds((rows, heads * DV), BF16), sds((1, DV)),
            sds((units, DV, DK)), sds((heads, DV, DK), BF16),
        ],
        [], 48, d_gated, head_out, projected, gain, qe, step,
    )
    all_inc = lax.all_gather(inc, "seq", axis=0)
    d_pre, d_edge, d_rate, d_convw, d_decay = call(
        bwd_mix,
        [
            sds((rows, heads * CONVW)), sds((PAD, heads * CONVW)), sds((rows, 2 * heads)),
            sds((KCONV, heads * CONVW)), sds((1, 2 * heads)),
        ],
        [
            pltpu.VMEM((PAD + rows, CONVW), F32), pltpu.VMEM((PAD + rows, CONVW), F32),
            pltpu.VMEM((units, DV, DK), F32), pltpu.VMEM((rows, DK), F32),
        ],
        60, info, all_ab, all_inc, conv, dec, inv, wu, states, step, y, d_out, rate_proj, projected, halo, convw,
        dlog, dbias,
    )
    returned = passed_along(d_edge, "seq", -1)
    d_pre = d_pre.at[rows - PAD :].add(returned).reshape(rows, heads, CONVW)
    d_projected = jnp.concatenate([d_pre.astype(BF16), d_gate.reshape(rows, heads, DV)], axis=2).reshape(
        rows, heads * MIXW
    )
    d_rate_low = d_rate.astype(BF16)
    grad_mixer = jnp.einsum("td,tw->dw", gathered, d_projected, preferred_element_type=F32)
    grad_rate = jnp.einsum("td,tg->dg", gathered, d_rate_low, preferred_element_type=F32)
    d_normed = lax.psum_scatter(
        (
            jnp.einsum("tw,dw->td", d_projected, mixer_flat, preferred_element_type=F32)
            + jnp.einsum("tg,dg->td", d_rate_low, rate_weight.reshape(D, 2 * heads), preferred_element_type=F32)
        ).astype(BF16),
        "head", scatter_dimension=0, tiled=True,
    ).astype(F32)
    d_resid, grad_mixer_gain = norm_one_back(d_normed)
    grad_tokens = d_hidden + d_resid

    def over_seq(grad, dim):
        return lax.psum_scatter(grad.astype(BF16), "seq", scatter_dimension=dim, tiled=True).astype(F32)

    grad_mixer = over_seq(grad_mixer, 0).reshape(D // seq, heads, MIXW)
    grad_rate = over_seq(grad_rate, 0).reshape(D // seq, 2, heads)
    grad_output = over_seq(grad_output, 1).reshape(heads, DV, D // seq)
    grad_gate_up = over_seq(grad_gate_up, 0)
    grad_down = over_seq(grad_down, 1)
    d_convw, d_decay = lax.psum((d_convw, d_decay), "seq")
    grad_conv = d_convw.reshape(KCONV, heads, CONVW)
    grad_decay_log, grad_decay_bias = d_decay[0, :heads], d_decay[0, heads:]
    grad_mixer_gain, grad_feed_gain, grad_head_gain = lax.psum(
        (grad_mixer_gain, grad_feed_gain, grad_head_gain[0]), ("seq", "head")
    )
    return (
        layer_out, grad_tokens, grad_mixer_gain, grad_mixer, grad_rate, grad_conv, grad_decay_log, grad_decay_bias,
        grad_head_gain, grad_output, grad_feed_gain, grad_gate_up, grad_down,
    )


def solution(mesh):
    rows = P(("seq", "head"), None)
    return jax.shard_map(
        local,
        mesh=mesh,
        in_specs=(
            rows, P(), P(None, "head", None), P(None, None, "head"), P(None, "head", None), P("head"), P("head"),
            P(), P("head", None, None), P(), P(None, None, "head"), P("head", None), P(), rows,
        ),
        out_specs=(
            rows, rows, P(), P("seq", "head", None), P("seq", None, "head"), P(None, "head", None), P("head"),
            P("head"), P(), P("head", None, "seq"), P(), P("seq", None, "head"), P("head", "seq"),
        ),
        check_vma=False,
    )
```

time: 1750 us -> 847 us (0.48)
  matrix products: 429 us -> 75.8 us
  other arithmetic: 302 us -> 21.3 us
  local copies, waits for them, and re-layouts: 187 us -> 50.7 us
  starting transfers between devices: 104 us -> 5.64 us
  waiting for transfers between devices: 562 us -> 491 us
  Pallas kernels: 0 us -> 56.3 us
    dot_general x199 -> x13, matrix products: 380 us -> 59.9 us  [the longest x1 8.18 us: local(): jnp.einsum('td,tw->dw', gathered, d_projected, preferred_element_type=F32)]
    ppermute x32 -> x2, waiting for transfers between devices: 203 us -> 3.75 us  [passed_along(): return lax.ppermute(shard, axis, pairs)]
    another operation x112 -> x0, other arithmetic: 181 us -> none  [the longest x72 166 us: solve_lower(): jax.scipy.linalg.solve_triangular(system, rhs_vals, lower=True, unit_diag...]
    ppermute x32 -> x2, starting transfers between devices: 103 us -> 4.84 us  [passed_along(): return lax.ppermute(shard, axis, pairs)]
    all_gather x3 -> x5, waiting for transfers between devices: 62.6 us -> 140 us  [the longest x1 48.6 us: local(): all_ab = lax.all_gather(ab, 'seq', axis=0)]
    unnamed x17 -> x19, waiting for transfers between devices: 117 us -> 180 us
    dynamic_update_slice x64 -> x0, local copies, waits for them, and re-layouts: 57.2 us -> none  [run_groups(): final, outputs = lax.scan(advance, start_state, pieces)]
    pallas_call x0 -> x4, Pallas kernels: none -> 56.3 us  [call(): pl.pallas_call(kernel, out_shape=outs, in_specs=[spec(a) for a in args],...]
  transfers between devices with their start and end apart: 45 -> 17, of which waited for: 41 -> 15; matrix products, arithmetic and copies ran while one was open for 32% -> 12% of each run, Pallas kernels for 0% -> 3%
where the time goes in v1:
time: 847 us; the launch traced here: 842 us
  waiting for transfers between devices  491 us (58%)
  blocking collectives  127 us (15%)
  matrix products  75.8 us (9%)
  Pallas kernels  56.3 us (7%)
  local copies, waits for them, and re-layouts  50.7 us (6%)
  other arithmetic  21.3 us (3%)
  between operations  14.8 us (2%)
    unnamed x19, waiting for transfers between devices  180 us
    psum x1, blocking collectives, local(): lax.psum((grad_mixer_gain, grad_feed_gain, grad_head_gain[0]), ('seq', 'h...  68.8 us
    psum x1, blocking collectives, local(): d_convw, d_decay = lax.psum((d_convw, d_decay), 'seq')  57.9 us
    pallas_call x4, Pallas kernels, call(): pl.pallas_call(kernel, out_shape=outs, in_specs=[spec(a) for a in args],...  56.3 us
    all_gather x1, waiting for transfers between devices, local(): all_ab = lax.all_gather(ab, 'seq', axis=0)  48.6 us
    reduce_scatter x1, waiting for transfers between devices, over_seq(): lax.psum_scatter(grad.astype(BF16), 'seq', scatter_dimension=dim, tiled=T...  47.1 us
    unnamed x77, local copies, waits for them, and re-layouts  43.5 us
    reduce_scatter x1, waiting for transfers between devices, local(): lax.psum_scatter(jnp.dot(gated, out_flat, preferred_element_type=F32), 'h...  37.2 us
  transfers between devices with their start and end apart: 17, of which 15 were waited for; matrix products, arithmetic and copies ran while one was open for 12% of the time, Pallas kernels for 3%

profile of v1, /device:TPU:1, one launch (start us, length us, event | category | flops | bytes accessed | tf_op | source)
XLA Modules:
  0.0 842.3 jit_solution(10286413031158679501)
XLA Ops:
  11.7 6.8 copy.55
  19.1 20.1 %all-gather.9.cloned.1.call-done = bf16[512,2048]{1,0:T(8,128)(2,1)} async-done(((bf16[64,2048]{1,0:T(8,128)(2,1)}), bf16[512,2048]{1,0:T(8,128)(2,1)}) %all-gather.9.cloned.1.call-update) | async-done | bytes 2097168 | tf_op jit(solution)/shard_map/all_gather | solution.py:389
  39.2 6.9 fusion.31.proj
  53.3 25.7 %shard_map.237 = (f32[512,1024]{1,0:T(8,128)}, f32[4,256,256]{2,1,0:T(8,128)}, bf16[4,256,256]{2,1,0:T(8,128)(2,1)}, f32[4,256,384]{2,1,0:T(8,128)}, f32[512,256...) custom-call(s32[6]{0:T(128)} %pad_add_fusion.info, ...), custom_call_target="tpu_custom_call" | custom-call | flops 2000000000 | bytes 16000000 | tf_op jit(solution)/shard_map/pallas_call | solution.py:353
  79.1 48.6 %all-gather.17.cloned.1.call-done = bf16[32,384,128]{2,1,0:T(8,128)(2,1)} async-done(((bf16[2,384,128]{2,1,0:T(8,128)(2,1)}), bf16[32,384,128]{2,1,0:T(8,128)(2,1)}) %all-gather.17.cloned.1.call-update) | async-done | bytes 3145744 | tf_op jit(solution)/shard_map/all_gather | solution.py:417
  141.0 37.2 %reduce-scatter.18.cloned.1.call-done = f32[64,2048]{1,0:T(8,128)} async-done(((f32[512,2048]{1,0:T(8,128)}), f32[64,2048]{1,0:T(8,128)}) %reduce-scatter.18.cloned.1.call-update) | async-done | bytes 524304 | tf_op jit(solution)/shard_map/reduce_scatter | solution.py:424
  181.0 26.9 %all-gather.11.cloned.1.call-done = bf16[512,2048]{1,0:T(8,128)(2,1)} async-done(((bf16[64,2048]{1,0:T(8,128)(2,1)}), bf16[512,2048]{1,0:T(8,128)(2,1)}) %all-gather.11.cloned.1.call-update) | async-done | bytes 2097168 | tf_op jit(solution)/shard_map/all_gather | solution.py:430
  207.9 7.9 fusion.4
  215.9 19.1 %all-gather.13.cloned.1.call-done = bf16[512,2048]{1,0:T(8,128)(2,1)} async-done(((bf16[64,2048]{1,0:T(8,128)(2,1)}), bf16[512,2048]{1,0:T(8,128)(2,1)}) %all-gather.13.cloned.1.call-update) | async-done | bytes 2097168 | tf_op jit(solution)/shard_map/all_gather | solution.py:431
  235.0 5.5 multiply_bitcast_fusion
  242.0 7.3 bitcast_convert_fusion
  249.4 30.7 %reduce-scatter.22.cloned.1.call-done = bf16[64,2048]{1,0:T(8,128)(2,1)} async-done(((bf16[512,2048]{1,0:T(8,128)(2,1)}), bf16[64,2048]{1,0:T(8,128)(2,1)}) %reduce-scatter.22.cloned.1.call-update) | async-done | bytes 262160 | tf_op jit(solution)/shard_map/reduce_scatter | solution.py:444
  283.5 27.1 %all-gather.15.cloned.1.call-done = bf16[512,2048]{1,0:T(8,128)(2,1)} async-done(((bf16[64,2048]{1,0:T(8,128)(2,1)}), bf16[512,2048]{1,0:T(8,128)(2,1)}) %all-gather.15.cloned.1.call-update) | async-done | bytes 2097168 | tf_op jit(solution)/shard_map/all_gather | solution.py:450
  314.3 4.3 shard_map.239
  321.3 5.0 convolution_convert_fusion.2
  326.3 4.6 copy.49
  331.0 8.0 convolution_convert_fusion.1
  338.9 8.3 copy.51
  347.3 18.3 %all-gather.19.cloned.1.call-done = bf16[32,256,128]{2,1,0:T(8,128)(2,1)} async-done(((bf16[2,256,128]{2,1,0:T(8,128)(2,1)}), bf16[32,256,128]{2,1,0:T(8,128)(2,1)}) %all-gather.19.cloned.1.call-update) | async-done | bytes 2097168 | tf_op jit(solution)/shard_map/all_gather | solution.py:461
  365.5 22.4 %shard_map.240 = (f32[512,1024]{1,0:T(8,128)}, f32[8,1024]{1,0:T(8,128)}, f32[512,4]{1,0:T(8,128)}, f32[4,1024]{1,0:T(4,128)}, f32[1,4]{1,0:T(1,128)}) custom-call(s32[6]{0:T(128)} %pad_add_fusion.info, bf16[16,2,384,128]{3,2,1,0:T(8,128)(2,1)} %bitcast.103, bf16[16,2,256,128]{3,2,1,0:T(8,128)(2,1)} %bitcast.110, f32[512,1024]{1,0:T(8,128)} %get-tuple-element.53.conv, ...), custom_call_target="tpu_custom_call" | custom-call | flops 2000000000 | bytes 16000000 | tf_op jit(solution)/shard_map/pallas_call | solution.py:353
  391.2 4.2 convolution_convert_fusion.3
  408.9 6.8 fusion
  417.8 4.3 convolution_convert_fusion.4
  424.8 8.2 convolution_convert_fusion
  433.0 10.3 %reduce-scatter.34.cloned.1.call-done = bf16[128,688]{1,0:T(8,128)(2,1)} async-done(((bf16[2048,688]{1,0:T(8,128)(2,1)}), bf16[128,688]{1,0:T(8,128)(2,1)}) %reduce-scatter.34.cloned.1.call-update) | async-done | bytes 176144
  445.2 81.4 %reduce-scatter.32.cloned.1.call-done = bf16[128,1376]{1,0:T(8,128)(2,1)} async-done(((bf16[2048,1376]{1,0:T(8,128)(2,1)}), bf16[128,1376]{1,0:T(8,128)(2,1)}) %reduce-scatter.32.cloned.1.call-update) | async-done | bytes 352272
  531.0 57.9 %all-reduce.3 = (f32[4,2,512]{2,1,0:T(2,128)}, f32[1,4]{1,0:T(1,128)S(1)}) all-reduce(f32[4,2,512]{2,1,0:T(2,128)S(1)} %reshape.166, f32[1,4]{1,0:T(1,128)} %get-tuple-element.65), channel_id=1, replica_groups=mesh['seq'=16,'head'=8] {'seq'}, use_global_device_ids=true, to_apply=%region_12.13 | all-reduce | flops 4100 | bytes 32800 | tf_op jit(solution)/shard_map/psum | solution.py:501
  589.6 11.8 %reduce-scatter.28.cloned.1.call-done = bf16[128,4]{1,0:T(8,128)(2,1)} async-done(((bf16[2048,4]{1,0:T(8,128)(2,1)}), bf16[128,4]{1,0:T(8,128)(2,1)}) %reduce-scatter.28.cloned.1.call-update) | async-done | bytes 1040
  602.8 75.8 %reduce-scatter.30.cloned.1.call-done = bf16[128,512]{1,0:T(8,128)(2,1)} async-done(((bf16[2048,512]{1,0:T(8,128)(2,1)}), bf16[128,512]{1,0:T(8,128)(2,1)}) %reduce-scatter.30.cloned.1.call-update) | async-done | bytes 131088
  680.4 32.0 %reduce-scatter.24.cloned.1.call-done = bf16[64,2048]{1,0:T(8,128)(2,1)} async-done(((bf16[512,2048]{1,0:T(8,128)(2,1)}), bf16[64,2048]{1,0:T(8,128)(2,1)}) %reduce-scatter.24.cloned.1.call-update) | async-done | bytes 262160 | tf_op jit(solution)/shard_map/reduce_scatter | solution.py:483
  713.8 68.8 %all-reduce.2 = (f32[2048]{0:T(1024)}, f32[256]{0:T(256)}, f32[2048]{0:T(1024)}) all-reduce(f32[2048]{0:T(1024)S(1)} %get-tuple-element.69, f32[256]{0:T(256)S(1)} %bitcast.101, f32[2048]{0:T(1024)S(1)} %get-tuple-element.67), channel_id=1, replica_groups=mesh['seq'=16,'head'=8] {'seq','head'}, use_global_device_ids=true, to_apply=%region_9.10 | all-reduce | flops 4352 | bytes 34816 | tf_op jit(solution)/shard_map/psum | solution.py:504
  785.8 47.1 %reduce-scatter.26.cloned.1.call-done = bf16[128,1536]{1,0:T(8,128)(2,1)} async-done(((bf16[2048,1536]{1,0:T(8,128)(2,1)}), bf16[128,1536]{1,0:T(8,128)(2,1)}) %reduce-scatter.26.cloned.1.call-update) | async-done | bytes 393232 | tf_op jit(solution)/shard_map/reduce_scatter | solution.py:494
  (145 shorter events, 78.1 us)
Async XLA Ops:
  7.2 227.8 %copy-start = (bf16[688,2048]{1,0:T(8,128)(2,1)S(1)}, bf16[688,2048]{1,0:T(8,128)(2,1)}, u32[]{:S(2)}) copy-start(bf16[688,2048]{1,0:T(8,128)(2,1)} %param.27) | copy-start | bytes 8454148
  7.2 32.0 %all-gather.9.cloned.1.call-start = ((), (), s32[]{:S(2)}) async-start(), calls=%async_computation.9 | async-start | bytes 2359296 | tf_op jit(solution)/shard_map/all_gather | solution.py:389
  8.5 10.0 %copy-start.28 = (f32[64]{0:T(128)}, f32[64]{0:T(128)S(1)}, u32[]{:S(2)}) copy-start(f32[64]{0:T(128)S(1)} %fusion.22) | copy-start | bytes 772
  10.3 117.4 %all-gather.17.cloned.1.call-start = ((), (), s32[]{:S(2)}) async-start(), calls=%async_computation.18 | async-start | bytes 3342336 | tf_op jit(solution)/shard_map/all_gather | solution.py:417
  11.7 6.8 copy-start.29
  39.2 11.9 %copy-start.21 = (bf16[512,2048]{1,0:T(8,128)(2,1)S(1)}, bf16[512,2048]{1,0:T(8,128)(2,1)}, u32[]{:S(2)}) copy-start(bf16[512,2048]{1,0:T(8,128)(2,1)} %all-gather.9.cloned.1.call-done) | copy-start | bytes 6291460
  39.2 11.9 %copy-start.26 = (bf16[2048,2,2]{0,2,1:T(2,128)(2,1)S(1)}, bf16[2048,2,2]{0,2,1:T(2,128)(2,1)}, u32[]{:S(2)}) copy-start(bf16[2048,2,2]{0,2,1:T(2,128)(2,1)} %param.19) | copy-start | bytes 49156
  47.8 4.9 collective-permute-start
  53.3 74.4 %copy-start.13 = (s32[6]{0:T(128)S(1)}, s32[6]{0:T(128)}, u32[]{:S(2)}) copy-start(s32[6]{0:T(128)} %pad_add_fusion.info) | copy-start | bytes 76
  53.3 74.4 %copy-start.14 = (f32[256]{0:T(256)S(1)}, f32[256]{0:T(256)}, u32[]{:S(2)}) copy-start(f32[256]{0:T(256)} %param.23) | copy-start | bytes 3076
  79.1 99.1 %reduce-scatter.18.cloned.1.call-start = ((), (), s32[]{:S(2)}) async-start(), calls=%async_computation.10 | async-start | bytes 4718592 | tf_op jit(solution)/shard_map/reduce_scatter | solution.py:424
  140.9 38.6 %copy-start.24 = (f32[2048]{0:T(1024)S(1)}, f32[2048]{0:T(1024)}, u32[]{:S(2)}) copy-start(f32[2048]{0:T(1024)} %param.25) | copy-start | bytes 24580
  140.9 67.0 %all-gather.11.cloned.1.call-start = ((), (), s32[]{:S(2)}) async-start(), calls=%async_computation.11 | async-start | bytes 2359296 | tf_op jit(solution)/shard_map/all_gather | solution.py:430
  179.5 101.8 %copy-start.17 = (f32[64,2048]{1,0:T(8,128)}, f32[64,2048]{1,0:T(8,128)S(1)}, u32[]{:S(2)}) copy-start(f32[64,2048]{1,0:T(8,128)S(1)} %get-tuple-element.77) | copy-start | bytes 1572868
  180.4 54.6 %all-gather.13.cloned.1.call-start = ((), (), s32[]{:S(2)}) async-start(), calls=%async_computation.13 | async-start | bytes 2359296 | tf_op jit(solution)/shard_map/all_gather | solution.py:431
  181.0 99.1 %reduce-scatter.22.cloned.1.call-start = ((), (), s32[]{:S(2)}) async-start(), calls=%async_computation.14 | async-start | bytes 2359296 | tf_op jit(solution)/shard_map/reduce_scatter | solution.py:444
  249.3 61.4 %all-gather.15.cloned.1.call-start = ((), (), s32[]{:S(2)}) async-start(), calls=%async_computation.15 | async-start | bytes 2359296 | tf_op jit(solution)/shard_map/all_gather | solution.py:450
  281.3 33.0 %copy-start.27 = (f32[64]{0:T(128)}, f32[64]{0:T(128)S(1)}, u32[]{:S(2)}) copy-start(f32[64]{0:T(128)S(1)} %multiply_multiply_fusion.1) | copy-start | bytes 772
  283.3 31.0 %copy-start.7 = (f32[512,256]{1,0:T(8,128)S(1)}, f32[512,256]{1,0:T(8,128)}, u32[]{:S(2)}) copy-start(f32[512,256]{1,0:T(8,128)} %get-tuple-element.48.qe) | copy-start | bytes 1572868
  283.3 82.3 %all-gather.19.cloned.1.call-start = ((), (), s32[]{:S(2)}) async-start(), calls=%async_computation.19 | async-start | bytes 2228224 | tf_op jit(solution)/shard_map/all_gather | solution.py:461
  321.2 122.1 %reduce-scatter.34.cloned.1.call-start = ((), (), s32[]{:S(2)}) async-start(), calls=%async_computation.23 | async-start | bytes 3342336
  330.9 195.6 %reduce-scatter.32.cloned.1.call-start = ((), (), s32[]{:S(2)}) async-start(), calls=%async_computation.22 | async-start | bytes 6127616
  347.2 254.2 %reduce-scatter.28.cloned.1.call-start = ((), (), s32[]{:S(2)}) async-start(), calls=%async_computation.20 | async-start | bytes 557056
  391.1 287.5 %reduce-scatter.30.cloned.1.call-start = ((), (), s32[]{:S(2)}) async-start(), calls=%async_computation.21 | async-start | bytes 2228224
  399.4 313.0 %reduce-scatter.24.cloned.1.call-start = ((), (), s32[]{:S(2)}) async-start(), calls=%async_computation.16 | async-start | bytes 2359296 | tf_op jit(solution)/shard_map/reduce_scatter | solution.py:483
  400.2 5.3 collective-permute-start.1
  408.8 6.9 copy-start.20
  408.9 6.9 copy-start.23
  417.8 365.5 %reduce-scatter.20.cloned.1.call-start = ((), (), s32[]{:S(2)}) async-start(), calls=%async_computation.12 | async-start | bytes 2359296 | tf_op jit(solution)/shard_map/reduce_scatter | solution.py:435
  422.2 410.7 %reduce-scatter.26.cloned.1.call-start = ((), (), s32[]{:S(2)}) async-start(), calls=%async_computation.17 | async-start | bytes 6684672 | tf_op jit(solution)/shard_map/reduce_scatter | solution.py:494
  433.0 279.5 %copy-start.25 = (f32[2048]{0:T(1024)S(1)}, f32[2048]{0:T(1024)}, u32[]{:S(2)}) copy-start(f32[2048]{0:T(1024)} %param.17) | copy-start | bytes 24580
  433.0 350.3 %copy-start.18 = (f32[64,2048]{1,0:T(8,128)S(1)}, f32[64,2048]{1,0:T(8,128)}, u32[]{:S(2)}) copy-start(f32[64,2048]{1,0:T(8,128)} %copy-done.17) | copy-start | bytes 1572868
  (18 other events, 32.8 us)
Sparse Core Ops, SparseCore 0:
  10.4 28.7 all-gather.8
  79.2 48.4 all-gather.16
  141.1 37.0 reduce-scatter.17
  180.5 27.3 all-gather.10
  209.5 25.4 all-gather.12
  249.4 30.5 reduce-scatter.21
  283.4 27.2 all-gather.14
  321.4 44.1 all-gather.18
  368.9 74.3 reduce-scatter.33
  446.6 79.9 reduce-scatter.31
  530.3 71.0 reduce-scatter.27
  604.9 73.7 reduce-scatter.29
  681.1 31.3 reduce-scatter.23
  714.7 32.8 reduce-scatter.19
  750.9 82.0 reduce-scatter.25

commit v2 on v1

--- a/solution.py
+++ b/solution.py
@@ -179,18 +179,10 @@
         ab_o[h] = ab.astype(ab_o.dtype)
 
 
-def fwd_out(info, all_ab, step, qe, ol, proj, gain, states_o, head_o, gated_o):
+def fwd_out(start, step, qe, ol, proj, gain, states_o, head_o, gated_o):
     rows = qe.shape[0]
-    heads = all_ab.shape[1]
+    heads = start.shape[0]
     blocks = rows // BLK
-    me = info[NB + 1]
-
-    def chain(j, held):
-        return tuple(
-            dot_left2(held[h], all_ab[j, h, :DK, :]) + all_ab[j, h, DK:, :].astype(F32) for h in range(heads)
-        )
-
-    start = lax.fori_loop(0, me, chain, tuple(jnp.zeros((DV, DK), F32) for _ in range(heads)))
     for h in range(heads):
         state = start[h]
         for c in range(blocks):
@@ -241,24 +233,14 @@
 
 
 def bwd_mix(
-    info, all_ab, all_inc, conv, dec, inv, wu, states, step, y, d_out, rate, proj, halo, convw, dlog, dbias,
-    d_pre_o, d_edge_o, d_rate_o, d_convw_o, d_decay_o, xpad, dpad, dsend, cols_s
+    info, later, conv, dec, inv, wu, states, step, y, d_out, d_gate, rate, proj, halo, convw, dlog, dbias,
+    d_proj_o, d_tail_o, d_edge_o, d_rate_o, d_convw_o, d_decay_o, xpad, dpad, dsend, cols_s, d_pre_o
 ):
     rows = d_out.shape[0]
-    heads = all_ab.shape[1]
+    heads = later.shape[0]
     blocks = rows // BLK
-    me = info[NB + 1]
-    last_dev = all_ab.shape[0] - 1
     strength, log_decay, pre = rates(rate, dlog, dbias)
     valid = [valid_column(info, rows, KCONV - 1 - j) for j in range(KCONV)]
-
-    def chain(i, held):
-        j = last_dev - i
-        return tuple(
-            dot_left2(held[h], all_ab[j, h, :DK, :], "nt") + all_inc[j, h].astype(F32) for h in range(heads)
-        )
-
-    later = lax.fori_loop(0, last_dev - me, chain, tuple(jnp.zeros((DV, DK), F32) for _ in range(heads)))
     for h in range(heads):
         grad = later[h]
         for c in range(blocks - 1, -1, -1):
@@ -343,7 +325,9 @@
             d_convw_o[j : j + 1, dst] = jnp.sum(masked * xpad[lo : lo + rows, :], axis=0, keepdims=True)
             dpad[lo : lo + rows, :] += convw[j : j + 1, dst].astype(F32) * masked
         d_edge_o[:, dst] = dpad[:PAD, :]
-        d_pre_o[:, dst] = dpad[PAD:, :]
+        d_tail_o[:, dst] = dpad[rows:, :]
+        d_proj_o[:, src] = dpad[PAD:, :].astype(BF16)
+        d_proj_o[:, pl.ds(h * MIXW + CONVW, DV)] = d_gate[:, pl.ds(h * DV, DV)]
 
 
 def call(kernel, outs, scratch, limit, *args, flops=2_000_000_000, nbytes=16_000_000):
@@ -363,6 +347,349 @@
 
 def sds(shape, dtype=F32):
     return jax.ShapeDtypeStruct(shape, dtype)
+CHIPS = 4
+LANES = 128
+
+
+def cp(src, dst, send, recv, dev):
+    return pltpu.make_async_remote_copy(
+        src_ref=src, dst_ref=dst, send_sem=send, recv_sem=recv, device_id=dev, device_id_type=pl.DeviceIdType.MESH
+    )
+
+
+def greet(devices):
+    barrier = pltpu.get_barrier_semaphore()
+    for dev in devices:
+        pl.semaphore_signal(barrier, inc=1, device_id=dev, device_id_type=pl.DeviceIdType.MESH)
+    pl.semaphore_wait(barrier, len(devices))
+
+
+def head_place():
+    me = lax.axis_index("head")
+    chip, core = me // 2, me % 2
+    seq = lax.axis_index("seq")
+
+    def dev(step, flip=False):
+        c = lax.rem(chip + step, CHIPS)
+        return (seq, c * 2 + (1 - core if flip else core))
+
+    return me, chip, core, dev
+
+
+def head_peers():
+    dev = head_place()[3]
+    return [dev(0, True)] + [dev(d) for d in range(1, CHIPS)]
+
+
+def gather_over_head(x, o, ssem, rsem, lsem):
+    rows = x.shape[0]
+    me, chip, core, dev = head_place()
+
+    def at(step, flip=False):
+        return o.at[pl.ds(pl.multiple_of(dev(step, flip)[1] * rows, rows), rows)]
+
+    own = pltpu.make_async_copy(x, at(0), lsem)
+    own.start()
+    out = [cp(x, at(0), ssem.at[d], rsem.at[d], dev(d)) for d in (1, 3, 2)]
+    out.append(cp(x, at(0), ssem.at[0], rsem.at[0], dev(0, True)))
+    for s in out:
+        s.start()
+    for d in (1, 3, 2):
+        cp(x, at(CHIPS - d), ssem.at[d], rsem.at[d], dev(d)).wait_recv()
+        fwd = cp(at(CHIPS - d), at(CHIPS - d), ssem.at[CHIPS + d], rsem.at[CHIPS + d], dev(0, True))
+        fwd.start()
+        out.append(fwd)
+    own.wait()
+    cp(x, at(0, True), ssem.at[0], rsem.at[0], dev(0, True)).wait_recv()
+    for d in range(1, CHIPS):
+        cp(x, at(CHIPS - d, True), ssem.at[CHIPS + d], rsem.at[CHIPS + d], dev(0, True)).wait_recv()
+    for s in out:
+        s.wait_send()
+
+
+def reduce_over_head(x, total, pair, got, mid, ssem, rsem):
+    rows = total.shape[0]
+    me, chip, core, dev = head_place()
+    partner = dev(0, True)
+
+    def at(step, flip=False):
+        return x.at[pl.ds(pl.multiple_of(dev(step, flip)[1] * rows, rows), rows)]
+
+    order = (2, 1, 3, 0)
+    first = [cp(at(d, True), pair.at[d], ssem.at[d], rsem.at[d], partner) for d in order]
+    for s in first:
+        s.start()
+    second = []
+    for s, d in zip(first, order):
+        s.wait_recv()
+        both = at(d)[...].astype(F32) + pair[d].astype(F32)
+        if d:
+            mid[d] = both.astype(BF16)
+            t = cp(mid.at[d], got.at[d], ssem.at[CHIPS + d], rsem.at[CHIPS + d], dev(d))
+            t.start()
+            second.append(t)
+        else:
+            total[...] = both
+    for s in (second[1], second[2], second[0]):
+        s.wait_recv()
+    total[...] = total[...] + ((got[1].astype(F32) + got[3].astype(F32)) + got[2].astype(F32))
+    for s in first + second:
+        s.wait_send()
+
+
+def mean_scale(v):
+    return lax.rsqrt(jnp.mean(v * v, axis=1, keepdims=True) + 1e-05)
+
+
+def norm_back(v, gain, d_norm):
+    r = mean_scale(v)
+    e = d_norm * gain
+    d_v = r * e - v * (r * r * r * jnp.mean(e * v, axis=1, keepdims=True))
+    return d_v, jnp.sum(d_norm * v * r, axis=0, keepdims=True)
+
+
+def mid_forward(x, tokens, gain, all_o, hidden_o, total, block, pair, got, mid, s1, r1, s2, r2, ls):
+    greet(head_peers())
+    reduce_over_head(x, total, pair, got, mid, s1, r1)
+    hidden = tokens[...].astype(F32) + total[...]
+    hidden_o[...] = hidden
+    block[...] = (hidden * mean_scale(hidden) * gain[...]).astype(BF16)
+    gather_over_head(block, all_o, s2, r2, ls)
+
+
+def mid_backward(x, hidden, cot, gain, all_o, d_hidden_o, d_gain_o, total, block, pair, got, mid, s1, r1, s2, r2, ls):
+    greet(head_peers())
+    reduce_over_head(x, total, pair, got, mid, s1, r1)
+    d_norm, d_gain = norm_back(hidden[...], gain[...], total[...])
+    d_hidden = cot[...].astype(F32) + d_norm
+    d_hidden_o[...] = d_hidden
+    d_gain_o[...] = d_gain
+    block[...] = d_hidden.astype(BF16)
+    gather_over_head(block, all_o, s2, r2, ls)
+
+
+def last_backward(x, tokens, d_hidden, gain, d_tokens_o, d_gain_o, total, pair, got, mid, s1, r1):
+    greet(head_peers())
+    reduce_over_head(x, total, pair, got, mid, s1, r1)
+    d_norm, d_gain = norm_back(tokens[...].astype(F32), gain[...], total[...])
+    d_tokens_o[...] = d_hidden[...] + d_norm
+    d_gain_o[...] = d_gain
+
+
+def reach(kernel, outs, scratch, cid, limit, *args, anywhere=(), nbytes=12_000_000):
+    return pl.pallas_call(
+        kernel,
+        out_shape=outs,
+        in_specs=[pl.BlockSpec(memory_space=pl.ANY) if i in anywhere else VMEM for i in range(len(args))],
+        out_specs=[VMEM for _ in outs],
+        scratch_shapes=scratch,
+        compiler_params=pltpu.CompilerParams(
+            collective_id=cid, has_side_effects=True, vmem_limit_bytes=limit << 20
+        ),
+        cost_estimate=pl.CostEstimate(flops=0, bytes_accessed=nbytes, transcendentals=0),
+    )(*args)
+
+
+def sems(n):
+    return pltpu.SemaphoreType.DMA((n,))
+
+
+def reduce_scratch(rows, cols):
+    return [pltpu.VMEM((CHIPS, rows, cols), BF16) for _ in range(3)] + [sems(2 * CHIPS), sems(2 * CHIPS)]
+
+
+def gather_scratch():
+    return [sems(2 * CHIPS), sems(2 * CHIPS), pltpu.SemaphoreType.DMA]
+
+
+SIDE = 4
+
+
+def seq_place():
+    me = lax.axis_index("seq")
+    z, y = me // SIDE, me % SIDE
+    head = lax.axis_index("head")
+
+    def dev(dz, dy):
+        return (lax.rem(z + dz, SIDE) * SIDE + lax.rem(y + dy, SIDE), head)
+
+    return me, z, y, dev
+
+
+def side_peers():
+    dev = seq_place()[3]
+    return [dev(0, d) for d in range(1, SIDE)] + [dev(d, 0) for d in range(1, SIDE)]
+
+
+def share(src, got, place, to, ssem, rsem):
+    got[place] = src[...]
+    out = [cp(src, got.at[place], ssem.at[d], rsem.at[d], to(d)) for d in range(1, SIDE)]
+    for s in out:
+        s.start()
+    for d in range(1, SIDE):
+        back = lax.rem(place + SIDE - d, SIDE)
+        cp(src, got.at[back], ssem.at[d], rsem.at[d], to(d)).wait_recv()
+    return out
+
+
+def unit_top():
+    return jnp.where(iota((DK + DV, DK), 0) == iota((DK + DV, DK), 1), 1.0, 0.0)
+
+
+def add_low(pair, low):
+    return jnp.concatenate([pair[:DK], pair[DK:] + low], axis=0)
+
+
+def states_forward(ab, start_o, ga_o, ta_o, got1, tot, got2, s1, r1, s2, r2):
+    me, z, y, dev = seq_place()
+    heads = ab.shape[0]
+    greet(side_peers())
+    out = share(ab, got1, y, lambda d: dev(0, d), s1, r1)
+    before = []
+    for h in range(heads):
+        whole = got1[0, h].astype(F32)
+        prefix = jnp.where(y > 0, whole, unit_top())
+        for j in range(1, SIDE):
+            a, b = got1[j, h, :DK, :], got1[j, h, DK:, :].astype(F32)
+            whole = add_low(dot_left2(whole, a), b)
+            if j < SIDE - 1:
+                prefix = jnp.where(y > j, whole, prefix)
+        tot[h] = whole.astype(BF16)
+        before.append(prefix)
+        for j in range(SIDE):
+            ga_o[j, h] = got1[j, h, :DK, :]
+    out += share(tot, got2, z, lambda d: dev(d, 0), s2, r2)
+    for h in range(heads):
+        held = jnp.zeros((DV, DK), F32)
+        for j in range(SIDE - 1):
+            held = jnp.where(
+                z > j, dot_left2(held, got2[j, h, :DK, :]) + got2[j, h, DK:, :].astype(F32), held
+            )
+        start_o[h] = dot3(held, before[h][:DK]) + before[h][DK:]
+        for j in range(SIDE):
+            ta_o[j, h] = got2[j, h, :DK, :]
+    for s in out:
+        s.wait_send()
+
+
+def states_backward(inc, ga, ta, later_o, got1, tot, got2, s1, r1, s2, r2):
+    me, z, y, dev = seq_place()
+    heads = inc.shape[0]
+    greet(side_peers())
+    out = share(inc, got1, y, lambda d: dev(0, d), s1, r1)
+    after = []
+    for h in range(heads):
+        whole = add_low(dot(unit_top(), ga[SIDE - 1, h], "nt"), got1[SIDE - 1, h].astype(F32))
+        suffix = jnp.where(y < SIDE - 1, whole, unit_top())
+        for j in range(SIDE - 2, -1, -1):
+            whole = add_low(dot_left2(whole, ga[j, h], "nt"), got1[j, h].astype(F32))
+            if j:
+                suffix = jnp.where(y < j, whole, suffix)
+        tot[h] = whole[DK:].astype(BF16)
+        after.append(suffix)
+    out += share(tot, got2, z, lambda d: dev(d, 0), s2, r2)
+    for h in range(heads):
+        held = jnp.zeros((DV, DK), F32)
+        for j in range(SIDE - 1, 0, -1):
+            held = jnp.where(z < j, dot_left2(held, ta[j, h], "nt") + got2[j, h].astype(F32), held)
+        later_o[h] = dot3(held, after[h][:DK]) + after[h][DK:]
+    for s in out:
+        s.wait_send()
+
+
+def reduce_over_seq(x, o, got1, mid, got2, own, ssem, rsem, lsem):
+    half, rows, cols = o.shape
+    me, z, y, dev = seq_place()
+    greet(side_peers())
+    ways = (lambda a, b: dev(b, a), lambda a, b: dev(a, b))
+
+    def piece(i, a, b):
+        owner = ways[i](a, b)[0]
+        return x.at[pl.ds(pl.multiple_of(owner * rows, rows), rows), pl.ds(i * cols, cols)]
+
+    sends, second, kept = [], [], {}
+    for a in (2, 1, 3):
+        for i in range(2):
+            for b in (2, 1, 3, 0):
+                k = (i * SIDE + a) * SIDE + b
+                s = cp(piece(i, a, b), got1.at[i, a, b], ssem.at[k], rsem.at[k], ways[i](a, 0))
+                s.start()
+                sends.append(s)
+    for i in range(2):
+        for b in range(SIDE):
+            kept[i, b] = pltpu.make_async_copy(piece(i, 0, b), own.at[i, b], lsem.at[i * SIDE + b])
+            kept[i, b].start()
+    for b in (2, 1, 3, 0):
+        for i in range(2):
+            kept[i, b].wait()
+            for a in (1, 3, 2):
+                k = (i * SIDE + a) * SIDE + b
+                cp(piece(i, a, b), got1.at[i, a, b], ssem.at[k], rsem.at[k], ways[i](a, 0)).wait_recv()
+            total = own[i, b].astype(F32) + (
+                (got1[i, 1, b].astype(F32) + got1[i, 3, b].astype(F32)) + got1[i, 2, b].astype(F32)
+            )
+            if b:
+                mid[i, b] = total.astype(BF16)
+                k = 2 * SIDE * SIDE + i * SIDE + b
+                s = cp(mid.at[i, b], got2.at[i, b], ssem.at[k], rsem.at[k], ways[i](0, b))
+                s.start()
+                second.append(s)
+            else:
+                o[i] = total
+    for s in second:
+        s.wait_recv()
+    for i in range(2):
+        o[i] = o[i] + ((got2[i, 1].astype(F32) + got2[i, 3].astype(F32)) + got2[i, 2].astype(F32))
+    for s in sends + second:
+        s.wait_send()
+
+
+def small_sums(gains, convs, rate, gains_o, convs_o, rate_o, gbuf, sbuf, rbuf, s1, r1, s2, r2):
+    me, z, y, dev = seq_place()
+    head = lax.axis_index("head")
+    heads, seqs = gbuf.shape[0], rbuf.shape[0]
+    g = gains.shape[0]
+    c = convs.shape[0]
+    across = [(me, lax.rem(head + d, heads)) for d in range(1, heads)]
+    along = [(lax.rem(me + d, seqs), head) for d in range(1, seqs)]
+    greet(across + along)
+    gbuf[head] = gains[...]
+    out = [cp(gains, gbuf.at[head], s1.at[d], r1.at[d], across[d - 1]) for d in range(1, heads)]
+    for s in out:
+        s.start()
+    for d in range(1, heads):
+        cp(gains, gbuf.at[lax.rem(head + heads - d, heads)], s1.at[d], r1.at[d], across[d - 1]).wait_recv()
+    total = gbuf[0]
+    for i in range(1, heads):
+        total = total + gbuf[i]
+    for j in range(seqs):
+        sbuf[j, :g] = total
+        sbuf[j, g : g + c] = convs[...]
+        sbuf[j, g + c :] = rate[j]
+    rbuf[me] = sbuf[me]
+    for d in range(1, seqs):
+        s = cp(sbuf.at[lax.rem(me + d, seqs)], rbuf.at[me], s2.at[d], r2.at[d], along[d - 1])
+        s.start()
+        out.append(s)
+    for d in range(1, seqs):
+        cp(sbuf.at[0], rbuf.at[lax.rem(me + seqs - d, seqs)], s2.at[d], r2.at[d], along[d - 1]).wait_recv()
+    total = rbuf[0]
+    for i in range(1, seqs):
+        total = total + rbuf[i]
+    gains_o[...] = total[:g]
+    convs_o[...] = total[g : g + c]
+    rate_o[...] = total[g + c :]
+    for s in out:
+        s.wait_send()
+
+
+def weight_grads(d_gu, middle, gated, n2, cot, d_mixed, o):
+    a, b = d_gu.shape[0], middle.shape[0]
+    for lo, left, right in ((0, d_gu, n2), (a, middle, cot), (a + b, gated, d_mixed)):
+        out = dot(left[...], right[...]).astype(BF16)
+        n = left.shape[0]
+        o[0, lo : lo + n] = out[:, :LANES]
+        o[1, lo : lo + n] = out[:, LANES:]
 
 
 def passed_along(shard, axis, by):
@@ -373,10 +700,6 @@
 
 def rms_scale(values, gain):
     return values * lax.rsqrt(jnp.mean(values * values, axis=-1, keepdims=True) + 1e-05) * gain
-
-
-def swiglu(gate_up):
-    return jax.nn.silu(gate_up[:, 0]) * gate_up[:, 1]
 
 
 def local(
@@ -384,15 +707,17 @@
     output_weight, feed_gain, gate_up_weight, down_weight, doc_starts, cotangent,
 ):
     resid = tokens.astype(F32)
-    norm_one, norm_one_back = jax.vjp(rms_scale, resid, mixer_gain)
-    normed = norm_one.astype(BF16)
+    normed = rms_scale(resid, mixer_gain).astype(BF16)
     gathered = lax.all_gather(normed, "head", axis=0, tiled=True)
+    heads = mixer_weight.shape[1]
+    gathered, cot_own, mixer_flat = lax.optimization_barrier(
+        (gathered, cotangent, mixer_weight.reshape(D, heads * MIXW))
+    )
+    cot_rows = lax.all_gather(cot_own, "head", axis=0, tiled=True)
     rows = gathered.shape[0]
-    heads = mixer_weight.shape[1]
     blocks = rows // BLK
     units = heads * blocks
     seq = lax.axis_size("seq")
-    mixer_flat = mixer_weight.reshape(D, heads * MIXW)
     projected = jnp.dot(gathered, mixer_flat, preferred_element_type=F32)
     rate_proj = jnp.einsum("td,dgh->tgh", gathered, rate_weight, preferred_element_type=F32).reshape(rows, 2 * heads)
     rim = projected[rows - PAD :].reshape(PAD, heads, MIXW)[:, :, :CONVW].reshape(PAD, heads * CONVW).astype(BF16)
@@ -414,43 +739,75 @@
         [pltpu.VMEM((PAD + rows, CONVW), F32)],
         56, info, projected, halo, rate_proj, convw, dlog, dbias,
     )
-    all_ab = lax.all_gather(ab, "seq", axis=0)
+    start, ga, ta = reach(
+        states_forward,
+        [sds((heads, DV, DK)), sds((SIDE, heads, DK, DK), BF16), sds((SIDE, heads, DK, DK), BF16)],
+        [
+            pltpu.VMEM((SIDE, heads, DK + DV, DK), BF16), pltpu.VMEM((heads, DK + DV, DK), BF16),
+            pltpu.VMEM((SIDE, heads, DK + DV, DK), BF16), sems(SIDE), sems(SIDE), sems(SIDE), sems(SIDE),
+        ],
+        1, 40, ab,
+    )
     states, head_out, gated = call(
         fwd_out,
         [sds((units, DV, DK)), sds((rows, heads * DV)), sds((rows, heads * DV), BF16)],
-        [], 48, info, all_ab, step, qe, ol, projected, gain,
+        [], 48, start, step, qe, ol, projected, gain,
     )
     out_flat = output_weight.reshape(heads * DV, D)
-    mixed = lax.psum_scatter(
-        jnp.dot(gated, out_flat, preferred_element_type=F32), "head", scatter_dimension=0, tiled=True
-    )
-    hidden = resid + mixed
-    norm_two, norm_two_back = jax.vjp(rms_scale, hidden, feed_gain)
-    normed_two = norm_two.astype(BF16)
-    gathered_two = lax.all_gather(normed_two, "head", axis=0, tiled=True)
-    cot_rows = lax.all_gather(cotangent, "head", axis=0, tiled=True)
-    gate_up = jnp.einsum("td,dgf->tgf", gathered_two, gate_up_weight, preferred_element_type=F32)
-    middle, swiglu_back = jax.vjp(swiglu, gate_up)
-    middle_low = middle.astype(BF16)
-    feed_sum = lax.psum_scatter(
-        jnp.dot(middle_low, down_weight, preferred_element_type=F32).astype(BF16),
-        "head", scatter_dimension=0, tiled=True,
-    ).astype(F32)
+    own = tokens.shape[0]
+    mixed = jnp.dot(gated, out_flat, preferred_element_type=F32).astype(BF16)
+    feed_row = feed_gain.reshape(1, D)
+    gathered_two, hidden = reach(
+        mid_forward,
+        [sds((rows, D), BF16), sds((own, D))],
+        [pltpu.VMEM((own, D), F32), pltpu.VMEM((own, D), BF16)] + reduce_scratch(own, D) + gather_scratch(),
+        2, 48, mixed, tokens, feed_row,
+    )
+    hid = down_weight.shape[0]
+    gu_t = gate_up_weight.transpose(1, 2, 0).reshape(2 * hid, D)
+    by_last = (((1,), (1,)), ((), ()))
+    by_first = (((0,), (0,)), ((), ()))
+    d_middle = lax.dot_general(down_weight, cot_rows, by_last, preferred_element_type=F32)
+    gate_up = lax.dot_general(gu_t, gathered_two, by_last, preferred_element_type=F32)
+    gate, up = gate_up[:hid], gate_up[hid:]
+    s = jax.nn.sigmoid(gate)
+    middle = (gate * s * up).astype(BF16)
+    d_gate_up = jnp.concatenate([d_middle * up * (s * (1.0 + gate * (1.0 - s))), d_middle * gate * s]).astype(BF16)
+    d_two = lax.dot_general(d_gate_up, gu_t, by_first, preferred_element_type=F32).astype(BF16)
+    d_mixed, d_hidden, g_feed_gain = reach(
+        mid_backward,
+        [sds((rows, D), BF16), sds((own, D)), sds((1, D))],
+        [pltpu.VMEM((own, D), F32), pltpu.VMEM((own, D), BF16)] + reduce_scratch(own, D) + gather_scratch(),
+        3, 48, d_two, hidden, cotangent, feed_row,
+    )
+    d_mixed, middle = lax.optimization_barrier((d_mixed, middle))
+    feed = lax.dot_general(middle, down_weight, by_first, preferred_element_type=F32).astype(BF16)
+    feed_sum = lax.psum_scatter(feed, "head", scatter_dimension=0, tiled=True).astype(F32)
     layer_out = (hidden + feed_sum).astype(BF16)
-    d_middle = jnp.einsum("td,fd->tf", cot_rows, down_weight, preferred_element_type=F32)
-    grad_down = jnp.einsum("tf,td->fd", middle_low, cot_rows, preferred_element_type=F32)
-    d_gate_up = swiglu_back(d_middle)[0].astype(BF16)
-    grad_gate_up = jnp.einsum("td,tgf->dgf", gathered_two, d_gate_up, preferred_element_type=F32)
-    d_normed_two = lax.psum_scatter(
-        jnp.einsum("tgf,dgf->td", d_gate_up, gate_up_weight, preferred_element_type=F32).astype(BF16),
-        "head", scatter_dimension=0, tiled=True,
-    ).astype(F32)
-    d_hidden_norm, grad_feed_gain = norm_two_back(d_normed_two)
-    d_hidden = cotangent.astype(F32) + d_hidden_norm
-    d_mixed = lax.all_gather(d_hidden.astype(BF16), "head", axis=0, tiled=True)
+    d_mixed, feed = lax.optimization_barrier((d_mixed, feed))
+    wide = 3 * hid + heads * DV
+    right = pl.BlockSpec((rows, 2 * LANES), lambda j: (0, j))
+
+    def whole(a):
+        return pl.BlockSpec(a.shape, lambda j: (0, 0))
+
+    gated_t = gated.T
+    grads = pl.pallas_call(
+        weight_grads,
+        grid=(seq // 2,),
+        out_shape=sds((seq, wide, LANES), BF16),
+        in_specs=[whole(d_gate_up), whole(middle), whole(gated_t), right, right, right],
+        out_specs=pl.BlockSpec((2, wide, LANES), lambda j: (j, 0, 0)),
+        compiler_params=pltpu.CompilerParams(vmem_limit_bytes=48 << 20),
+        cost_estimate=pl.CostEstimate(flops=2 * wide * rows * D, bytes_accessed=24_000_000, transcendentals=0),
+    )(d_gate_up, middle, gated_t, gathered_two, cot_rows, d_mixed)
+    d_mixed, grads = lax.optimization_barrier((d_mixed, grads))
+    grads = lax.psum_scatter(grads.reshape(seq * wide, LANES), "seq", scatter_dimension=0, tiled=True).astype(F32)
+    grad_gate_up = grads[: 2 * hid].reshape(2, hid, LANES).transpose(2, 0, 1)
+    grad_down = grads[2 * hid : 3 * hid]
+    grad_output = grads[3 * hid :].reshape(heads, DV, LANES)
     d_gated = jnp.einsum("td,vd->tv", d_mixed, out_flat, preferred_element_type=F32)
-    grad_output = jnp.einsum("tv,td->vd", gated, d_mixed, preferred_element_type=F32)
-    d_out, d_gate, grad_head_gain, y, inc = call(
+    d_out, d_gate, g_head_gain, y, inc = call(
         bwd_head,
         [
             sds((rows, heads * DV)), sds((rows, heads * DV), BF16), sds((1, DV)),
@@ -458,52 +815,85 @@
         ],
         [], 48, d_gated, head_out, projected, gain, qe, step,
     )
-    all_inc = lax.all_gather(inc, "seq", axis=0)
-    d_pre, d_edge, d_rate, d_convw, d_decay = call(
+    (later,) = reach(
+        states_backward,
+        [sds((heads, DV, DK))],
+        [
+            pltpu.VMEM((SIDE, heads, DV, DK), BF16), pltpu.VMEM((heads, DV, DK), BF16),
+            pltpu.VMEM((SIDE, heads, DV, DK), BF16), sems(SIDE), sems(SIDE), sems(SIDE), sems(SIDE),
+        ],
+        4, 40, inc, ga, ta,
+    )
+    d_projected, d_tail, d_edge, d_rate, d_convw, d_decay = call(
         bwd_mix,
         [
-            sds((rows, heads * CONVW)), sds((PAD, heads * CONVW)), sds((rows, 2 * heads)),
-            sds((KCONV, heads * CONVW)), sds((1, 2 * heads)),
+            sds((rows, heads * MIXW), BF16), sds((PAD, heads * CONVW)), sds((PAD, heads * CONVW)),
+            sds((rows, 2 * heads)), sds((KCONV, heads * CONVW)), sds((1, 2 * heads)),
         ],
         [
             pltpu.VMEM((PAD + rows, CONVW), F32), pltpu.VMEM((PAD + rows, CONVW), F32),
-            pltpu.VMEM((units, DV, DK), F32), pltpu.VMEM((rows, DK), F32),
+            pltpu.VMEM((units, DV, DK), F32), pltpu.VMEM((rows, DK), F32), pltpu.VMEM((rows, heads * CONVW), F32),
         ],
-        60, info, all_ab, all_inc, conv, dec, inv, wu, states, step, y, d_out, rate_proj, projected, halo, convw,
+        60, info, later, conv, dec, inv, wu, states, step, y, d_out, d_gate, rate_proj, projected, halo, convw,
         dlog, dbias,
     )
-    returned = passed_along(d_edge, "seq", -1)
-    d_pre = d_pre.at[rows - PAD :].add(returned).reshape(rows, heads, CONVW)
-    d_projected = jnp.concatenate([d_pre.astype(BF16), d_gate.reshape(rows, heads, DV)], axis=2).reshape(
-        rows, heads * MIXW
-    )
+    tail = (d_tail + passed_along(d_edge, "seq", -1)).astype(BF16)
+    for h in range(heads):
+        d_projected = lax.dynamic_update_slice(
+            d_projected, tail[:, h * CONVW : (h + 1) * CONVW], (rows - PAD, h * MIXW)
+        )
     d_rate_low = d_rate.astype(BF16)
-    grad_mixer = jnp.einsum("td,tw->dw", gathered, d_projected, preferred_element_type=F32)
+    d_normed = (
+        jnp.einsum("tw,dw->td", d_projected, mixer_flat, preferred_element_type=F32)
+        + jnp.einsum("tg,dg->td", d_rate_low, rate_weight.reshape(D, 2 * heads), preferred_element_type=F32)
+    ).astype(BF16)
     grad_rate = jnp.einsum("td,tg->dg", gathered, d_rate_low, preferred_element_type=F32)
-    d_normed = lax.psum_scatter(
-        (
-            jnp.einsum("tw,dw->td", d_projected, mixer_flat, preferred_element_type=F32)
-            + jnp.einsum("tg,dg->td", d_rate_low, rate_weight.reshape(D, 2 * heads), preferred_element_type=F32)
-        ).astype(BF16),
-        "head", scatter_dimension=0, tiled=True,
-    ).astype(F32)
-    d_resid, grad_mixer_gain = norm_one_back(d_normed)
-    grad_tokens = d_hidden + d_resid
-
-    def over_seq(grad, dim):
-        return lax.psum_scatter(grad.astype(BF16), "seq", scatter_dimension=dim, tiled=True).astype(F32)
-
-    grad_mixer = over_seq(grad_mixer, 0).reshape(D // seq, heads, MIXW)
-    grad_rate = over_seq(grad_rate, 0).reshape(D // seq, 2, heads)
-    grad_output = over_seq(grad_output, 1).reshape(heads, DV, D // seq)
-    grad_gate_up = over_seq(grad_gate_up, 0)
-    grad_down = over_seq(grad_down, 1)
-    d_convw, d_decay = lax.psum((d_convw, d_decay), "seq")
-    grad_conv = d_convw.reshape(KCONV, heads, CONVW)
-    grad_decay_log, grad_decay_bias = d_decay[0, :heads], d_decay[0, heads:]
-    grad_mixer_gain, grad_feed_gain, grad_head_gain = lax.psum(
-        (grad_mixer_gain, grad_feed_gain, grad_head_gain[0]), ("seq", "head")
-    )
+    grad_tokens, g_mixer_gain = reach(
+        last_backward,
+        [sds((own, D)), sds((1, D))],
+        [pltpu.VMEM((own, D), F32)] + reduce_scratch(own, D),
+        5, 48, d_normed, tokens, d_hidden, mixer_gain.reshape(1, D),
+    )
+    grad_mixer = jnp.einsum("td,tw->dw", gathered, d_projected, preferred_element_type=F32).astype(BF16)
+    half = heads * MIXW // 2
+    part = D // seq
+    (grad_mixer,) = reach(
+        reduce_over_seq,
+        [sds((2, part, half))],
+        [
+            pltpu.VMEM((2, SIDE, SIDE, part, half), BF16), pltpu.VMEM((2, SIDE, part, half), BF16),
+            pltpu.VMEM((2, SIDE, part, half), BF16), pltpu.VMEM((2, SIDE, part, half), BF16),
+            sems(2 * SIDE * SIDE + 2 * SIDE), sems(2 * SIDE * SIDE + 2 * SIDE), sems(2 * SIDE),
+        ],
+        6, 56, grad_mixer, anywhere=(0,), nbytes=40_000_000,
+    )
+    grad_mixer = grad_mixer.transpose(1, 0, 2)
+
+    def packed(*arrays):
+        flat = jnp.concatenate([a.reshape(-1) for a in arrays])
+        size = -(-flat.size // (8 * LANES)) * 8 * LANES
+        return jnp.pad(flat, (0, size - flat.size)).reshape(-1, LANES)
+
+    gains = packed(g_mixer_gain, g_feed_gain, g_head_gain)
+    convs = packed(d_convw, d_decay)
+    rate_own = jnp.pad(grad_rate.reshape(seq, -1, LANES), ((0, 0), (0, 8 - 2 * heads), (0, 0)))
+    n_gain, n_conv = gains.shape[0], convs.shape[0]
+    gains, convs, rate_own = reach(
+        small_sums,
+        [sds((n_gain, LANES)), sds((n_conv, LANES)), sds((8, LANES))],
+        [
+            pltpu.VMEM((lax.axis_size("head"), n_gain, LANES), F32),
+            pltpu.VMEM((seq, n_gain + n_conv + 8, LANES), F32), pltpu.VMEM((seq, n_gain + n_conv + 8, LANES), F32),
+            sems(8), sems(8), sems(16), sems(16),
+        ],
+        7, 40, gains, convs, rate_own, nbytes=1_000_000,
+    )
+    gains, convs = gains.reshape(-1), convs.reshape(-1)
+    grad_mixer_gain, grad_feed_gain, grad_head_gain = gains[:D], gains[D : 2 * D], gains[2 * D : 2 * D + DV]
+    n = KCONV * heads * CONVW
+    grad_conv = convs[:n].reshape(KCONV, heads, CONVW)
+    grad_decay_log, grad_decay_bias = convs[n : n + heads], convs[n + heads : n + 2 * heads]
+    grad_rate = rate_own[: 2 * heads].reshape(part, 2, heads)
     return (
         layer_out, grad_tokens, grad_mixer_gain, grad_mixer, grad_rate, grad_conv, grad_decay_log, grad_decay_bias,
         grad_head_gain, grad_output, grad_feed_gain, grad_gate_up, grad_down,

time: 847 us -> 414 us (0.49)
  waiting for transfers between devices: 491 us -> 22.1 us
  Pallas kernels: 56.3 us -> 266 us
  blocking collectives: 127 us -> 0 us
  matrix products: 75.8 us -> 53.3 us
  other arithmetic: 21.3 us -> 7.67 us
  local copies, waits for them, and re-layouts: 50.7 us -> 41.1 us
    pallas_call x0 -> x8, Pallas kernels: none -> 218 us  [the longest x7 207 us: reach(): pl.pallas_call(kernel, out_shape=outs, in_specs=[pl.BlockSpec(memory_spac...]
    unnamed x19 -> x5, waiting for transfers between devices: 180 us -> 0.07 us
    reduce_scatter x5 -> x1, waiting for transfers between devices: 147 us -> 0.01 us  [local(): lax.psum_scatter(feed, 'head', scatter_dimension=0, tiled=True).astype(F32)]
    all_gather x5 -> x1, waiting for transfers between devices: 140 us -> 0.01 us  [local(): cot_rows = lax.all_gather(cot_own, 'head', axis=0, tiled=True)]
    psum x2 -> x0, blocking collectives: 127 us -> none  [the longest x1 68.8 us: local(): lax.psum((grad_mixer_gain, grad_feed_gain, grad_head_gain[0]), ('seq', 'h...]
    dot_general x8 -> x5, matrix products: 45.5 us -> 20.7 us  [the longest x1 7.05 us: local(): lax.dot_general(d_gate_up, gu_t, by_first, preferred_element_type=F32)]
    unnamed x77 -> x106, local copies, waits for them, and re-layouts: 43.5 us -> 30.3 us
  transfers between devices with their start and end apart: 17 -> 6, of which waited for: 15 -> 1; matrix products, arithmetic and copies ran while one was open for 12% -> 14% of each run, Pallas kernels for 3% -> 57%
where the time goes in v2:
time: 414 us; the launch traced here: 410 us
  Pallas kernels  266 us (64%)
  matrix products  53.3 us (13%)
  local copies, waits for them, and re-layouts  41.1 us (10%)
  waiting for transfers between devices  22.1 us (5%)
  between operations  14.6 us (4%)
  other arithmetic  7.67 us (2%)
  starting transfers between devices  4.72 us (1%)
    pallas_call x7, Pallas kernels, reach(): pl.pallas_call(kernel, out_shape=outs, in_specs=[pl.BlockSpec(memory_spac...  207 us
    pallas_call x4, Pallas kernels, call(): pl.pallas_call(kernel, out_shape=outs, in_specs=[spec(a) for a in args],...  48.1 us
    unnamed x106, local copies, waits for them, and re-layouts  30.3 us
    all_gather x1, waiting for transfers between devices, local(): gathered = lax.all_gather(normed, 'head', axis=0, tiled=True)  22 us
    pallas_call x1, Pallas kernels, local(): pl.pallas_call(weight_grads, grid=(seq // 2,), out_shape=sds((seq, wide,...  11.3 us
    dot_general x1, matrix products, local(): jnp.einsum('td,tw->dw', gathered, d_projected, preferred_element_type=F32)  8.49 us
    dot_general x1, matrix products, local(): jnp.einsum('tw,dw->td', d_projected, mixer_flat, preferred_element_type=F32)  8.29 us
  transfers between devices with their start and end apart: 6, of which 1 were waited for; matrix products, arithmetic and copies ran while one was open for 14% of the time, Pallas kernels for 57%

profile of v2, /device:TPU:1, one launch (start us, length us, event | category | flops | bytes accessed | tf_op | source)
XLA Modules:
  0.0 409.8 jit_solution(12552655590816313235)
XLA Ops:
  8.5 1.8 fusion.4
  10.4 6.8 %copy.45 = bf16[256,8,2,768]{3,1,2,0:T(8,128)(2,1)} copy(bf16[256,8,2,768]{3,2,1,0:T(2,128)(2,1)} %bitcast.86) | data formatting | bytes 12582912
  17.2 22.0 %all-gather.3.cloned.1.call-done = bf16[512,2048]{1,0:T(8,128)(2,1)} async-done(((bf16[64,2048]{1,0:T(8,128)(2,1)}), bf16[512,2048]{1,0:T(8,128)(2,1)}) %all-gather.3.cloned.1.call-update) | async-done | bytes 2097168 | tf_op jit(solution)/shard_map/all_gather | solution.py:711
  40.5 6.9 %fusion.12.proj = f32[512,1536]{1,0:T(8,128)S(1)} fusion(bf16[512,2048]{1,0:T(8,128)(2,1)} %all-gather.3.cloned.1.call-done, bf16[2048,1536]{1,0:T(8,128)(2,1)} %bitcast.87), kind=kOutput, calls=%fused_computation.42 | convolution fusion | flops 3221225472 | bytes 11534336 | tf_op jit(solution)/shard_map/dot_general | solution.py:721
  47.4 1.6 copy-done.37
  49.1 3.3 collective-permute-start
  54.5 25.6 %shard_map.237 = (f32[512,1024]{1,0:T(8,128)}, f32[4,256,256]{2,1,0:T(8,128)}, bf16[4,256,256]{2,1,0:T(8,128)(2,1)}, f32[4,256,384]{2,1,0:T(8,128)}, f32[512,256...) custom-call(s32[6]{0:T(128)} %pad_add_fusion.info, ...), custom_call_target="tpu_custom_call" | custom-call | flops 2000000000 | bytes 16000000 | tf_op jit(solution)/shard_map/pallas_call | solution.py:337
  81.0 24.4 %shard_map.238 = (f32[2,256,128]{2,1,0:T(8,128)S(1)}, bf16[4,2,128,128]{3,2,1,0:T(8,128)(2,1)S(1)}, bf16[4,2,128,128]{3,2,1,0:T(8,128)(2,1)S(1)}) custom-call(bf16[2,384,128]{2,1,0:T(8,128)(2,1)S(1)} %copy-done.21), custom_call_target="tpu_custom_call" | custom-call | bytes 12000000 | tf_op jit(solution)/shard_map/pallas_call | solution.py:480
  109.5 2.9 shard_map.239
  114.8 36.5 %shard_map.240 = (bf16[512,2048]{1,0:T(8,128)(2,1)S(1)}, f32[64,2048]{1,0:T(8,128)S(1)}) custom-call(bf16[512,2048]{1,0:T(8,128)(2,1)S(1)} %convolution_convert_fusion.2.x, bf16[64,2048]{1,0:T(8,128)(2,1)S(1)} %copy-done.2, f32[1,2048]{1,0:T(1,128)S(1)} %bitcast.76), custom_call_target="tpu_custom_call" | custom-call | bytes 12000000 | tf_op jit(solution)/shard_map/pallas_call | solution.py:480
  152.1 4.6 %convolution_bitcast_fusion = f32[1376,512]{1,0:T(8,128)} fusion(bf16[512,2048]{1,0:T(8,128)(2,1)S(1)} %get-tuple-element.66.n2, bf16[1376,2048]{1,0:T(8,128)(2,1)S(1)} %bitcast.107), kind=kOutput, calls=%fused_computation.2 | convolution fusion | flops 2885681152 | bytes 10551296 | tf_op jit(solution)/shard_map/dot_general | solution.py:771
  158.1 4.6 %multiply_convert_fusion.2 = (bf16[688,512]{1,0:T(8,128)(2,1)S(1)}, bf16[688,512]{1,0:T(8,128)(2,1)S(1)}, bf16[688,512]{1,0:T(8,128)(2,1)S(1)}) fusion(f32[1376,512]{1,0:T(8,128)} %convolution_bitcast_fusion, bf16[512,2048]{1,0:T(8,128)(2,1)} %all-gather.5.cloned.1.call-done.cot, bf16[688,2048]{1,0:T(8,128)(2,1)S(1)} %copy-done), kind=kOutput, calls=%fused_computation.12 | convolution fusion | flops 1448476672 | bytes 9846784 | tf_op jit(solution)/shard_map/dot_general | solution.py:770
  162.7 7.1 %convolution_convert_fusion.3.x = bf16[512,2048]{1,0:T(8,128)(2,1)S(1)} fusion(bf16[1376,2048]{1,0:T(8,128)(2,1)} %bitcast.104, bf16[688,512]{1,0:T(8,128)(2,1)S(1)} %get-tuple-element.139, bf16[688,512]{1,0:T(8,128)(2,1)S(1)} %get-tuple-element.138), kind=kOutput, calls=%fused_computation.5 | convolution fusion | flops 2889547776 | bytes 9142272 | tf_op jit(solution)/shard_map/dot_general | solution.py:776
  169.8 33.4 %shard_map.241 = (bf16[512,2048]{1,0:T(8,128)(2,1)S(1)}, f32[64,2048]{1,0:T(8,128)S(1)}, f32[1,2048]{1,0:T(1,128)S(1)}) custom-call(bf16[512,2048]{1,0:T(8,128)(2,1)S(1)} %convolution_convert_fusion.3.x, f32[64,2048]{1,0:T(8,128)S(1)} %copy-done.4, bf16[64,2048]{1,0:T(8,128)(2,1)S(1)} %copy-done.8, f32[1,2048]{1,0:T(1,128)S(1)} %bitcast.77), custom_call_target="tpu_custom_call" | custom-call | bytes 12000000 | tf_op jit(solution)/shard_map/pallas_call | solution.py:480
  205.3 3.2 convolution_convert_fusion.1
  212.9 11.3 %shard_map.242 = bf16[16,2576,128]{2,1,0:T(8,128)(2,1)} custom-call(bf16[1376,512]{1,0:T(8,128)(2,1)S(1)} %pad_maximum_fusion.d_gu, bf16[688,512]{1,0:T(8,128)(2,1)S(1)} %copy-done.29, bf16[512,512]{1,0:T(8,128)(2,1)S(1)} %bitcast.75, bf16[512,2048]{1,0:T(8,128)(2,1)S(1)} %copy-done.25, bf16[512,2048]{1,0:T(8,128)(2,1)} %all-gather.5.cloned.1.call-done.cot, ...), custom_call_target="tpu_custom_call" | custom-call | flops 5402263552 | bytes 24000000 | tf_op jit(solution)/shard_map/pallas_call | solution.py:795
  224.4 3.7 fusion.13.d_gated
  228.1 3.6 shard_map.243
  233.5 19.5 %shard_map.244.later = f32[2,256,128]{2,1,0:T(8,128)S(1)} custom-call(bf16[2,256,128]{2,1,0:T(8,128)(2,1)S(1)} %get-tuple-element.73.inc, bf16[4,2,128,128]{3,2,1,0:T(8,128)(2,1)S(1)} %get-tuple-element.74.ga, bf16[4,2,128,128]{3,2,1,0:T(8,128)(2,1)S(1)} %copy-done.20), custom_call_target="tpu_custom_call" | custom-call | bytes 12000000 | tf_op jit(solution)/shard_map/pallas_call | solution.py:480
  253.8 16.0 %shard_map.245 = (bf16[512,1536]{1,0:T(8,128)(2,1)}, f32[8,1024]{1,0:T(8,128)}, f32[8,1024]{1,0:T(8,128)}, f32[512,4]{1,0:T(8,128)}, f32[4,1024]{1,0:T(4,128)}, /*index=5*/f32[1,4]{1,0:T(1,128)}) custom-call(s32[6]{0:T(128)} %pad_add_fusion.info, f32[2,256,128]{2,1,0:T(8,128)} %copy-done.7, f32[512,1024]{1,0:T(8,128)} %get-tuple-element.76.conv, ...), custom_call_target="tpu_custom_call" | custom-call | flops 2000000000 | bytes 16000000 | tf_op jit(solution)/shard_map/pallas_call | solution.py:337
  271.1 3.8 fusion.7
  277.6 8.3 %add_convert_fusion.x = bf16[512,2048]{1,0:T(8,128)(2,1)S(1)} fusion(f32[512,2048]{1,0:T(8,128)} %fusion.7, bf16[512,1536]{1,0:T(8,128)(2,1)} %slice_dynamic-update-slice_fusion, bf16[2048,1536]{1,0:T(8,128)(2,1)} %bitcast.88), kind=kOutput, calls=%fused_computation.1 | convolution fusion | flops 3223322624 | bytes 14155776 | tf_op jit(solution)/shard_map/tw,dw->td/dot_general | solution.py:847
  285.9 18.1 %shard_map.246 = (f32[64,2048]{1,0:T(8,128)S(1)}, f32[1,2048]{1,0:T(1,128)S(1)}) custom-call(bf16[512,2048]{1,0:T(8,128)(2,1)S(1)} %add_convert_fusion.x, bf16[64,2048]{1,0:T(8,128)(2,1)S(1)} %copy-done.2, f32[64,2048]{1,0:T(8,128)S(1)} %copy-done.18, f32[1,2048]{1,0:T(1,128)S(1)} %bitcast.78), custom_call_target="tpu_custom_call" | custom-call | bytes 12000000 | tf_op jit(solution)/shard_map/pallas_call | solution.py:480
  304.9 21.6 %shard_map.247 = (f32[40,128]{1,0:T(8,128)S(1)}, f32[40,128]{1,0:T(8,128)S(1)}, f32[8,128]{1,0:T(8,128)S(1)}) custom-call(f32[40,128]{1,0:T(8,128)S(1)} %get-tuple-element.146.gains, f32[40,128]{1,0:T(8,128)S(1)} %get-tuple-element.145.convs, f32[16,8,128]{2,1,0:T(8,128)S(1)} %pad.14.rate), custom_call_target="tpu_custom_call" | custom-call | bytes 1000000 | tf_op jit(solution)/shard_map/pallas_call | solution.py:480
  328.0 8.5 %convolution_convert_fusion.x = bf16[2048,1536]{1,0:T(8,128)(2,1)} fusion(bf16[512,2048]{1,0:T(8,128)(2,1)} %all-gather.3.cloned.1.call-done, bf16[512,1536]{1,0:T(8,128)(2,1)} %slice_dynamic-update-slice_fusion), kind=kOutput, calls=%fused_computation | convolution fusion | flops 3224371200 | bytes 9961472 | tf_op jit(solution)/shard_map/td,tw->dw/dot_general | solution.py:857
  336.5 53.3 %shard_map.248 = f32[2,128,768]{2,1,0:T(8,128)} custom-call(bf16[2048,1536]{1,0:T(8,128)(2,1)} %convolution_convert_fusion.x), custom_call_target="tpu_custom_call" | custom-call | bytes 40000000 | tf_op jit(solution)/shard_map/pallas_call | solution.py:480
  389.8 2.6 copy.42
  394.2 1.9 add_convert_fusion.1
  396.0 1.6 slice.87
  397.7 1.7 slice.89
  399.3 1.9 slice.88
  401.2 1.9 copy.53
  (144 shorter events, 31.2 us)
Async XLA Ops:
  7.2 150.9 %copy-start = (bf16[688,2048]{1,0:T(8,128)(2,1)S(1)}, bf16[688,2048]{1,0:T(8,128)(2,1)}, u32[]{:S(2)}) copy-start(bf16[688,2048]{1,0:T(8,128)(2,1)} %param.25) | copy-start | bytes 8454148
  7.2 32.0 %all-gather.3.cloned.1.call-start = ((), (), s32[]{:S(2)}) async-start(), calls=%async_computation.2 | async-start | bytes 2359296 | tf_op jit(solution)/shard_map/all_gather | solution.py:711
  10.3 147.8 %all-gather.5.cloned.1.call-start = ((), (), s32[]{:S(2)}) async-start(), calls=%async_computation.3 | async-start | bytes 2359296 | tf_op jit(solution)/shard_map/all_gather | solution.py:716
  10.4 28.9 %copy-start.44 = (bf16[4,2,512]{2,1,0:T(2,128)(2,1)S(1)}, bf16[4,2,512]{2,1,0:T(2,128)(2,1)}, u32[]{:S(2)}) copy-start(bf16[4,2,512]{2,1,0:T(2,128)(2,1)} %param.18) | copy-start | bytes 24580
  10.4 29.5 %copy-start.46 = (s32[4]{0:T(128)S(1)}, s32[4]{0:T(128)}, u32[]{:S(2)}) copy-start(s32[4]{0:T(128)} %param.26) | copy-start | bytes 52
  39.3 354.9 %reduce-scatter.5.cloned.1.call-start = ((), (), s32[]{:S(2)}) async-start(), calls=%async_computation.4 | async-start | bytes 2359296 | tf_op jit(solution)/shard_map/reduce_scatter | solution.py:785
  40.5 11.8 %copy-start.35 = (bf16[512,2048]{1,0:T(8,128)(2,1)S(1)}, bf16[512,2048]{1,0:T(8,128)(2,1)}, u32[]{:S(2)}) copy-start(bf16[512,2048]{1,0:T(8,128)(2,1)} %all-gather.3.cloned.1.call-done) | copy-start | bytes 6291460
  40.5 11.8 %copy-start.42 = (bf16[2048,2,2]{0,2,1:T(2,128)(2,1)S(1)}, bf16[2048,2,2]{0,2,1:T(2,128)(2,1)}, u32[]{:S(2)}) copy-start(bf16[2048,2,2]{0,2,1:T(2,128)(2,1)} %param.17) | copy-start | bytes 49156
  49.1 4.8 %collective-permute-start = (bf16[8,1024]{1,0:T(8,128)(2,1)S(1)}, bf16[8,1024]{1,0:T(8,128)(2,1)S(1)}, u32[]{:S(2)}, u32[]{:S(2)}) collective-permute-start(bf16[8,1024]{1,0:T(8,128)(2,1)S(1)} %bitcast.97), channel_id=1, source_target_pairs={{0,8},{8,16},{16,24},{24,32},{32,40},{40,48},{48,56},{56,64},{64,7... | collective-permute-start | bytes 49160 | tf_op jit(solution)/shard_map/ppermute | solution.py:698
  54.5 51.6 %copy-start.27 = (f32[256]{0:T(256)S(1)}, f32[256]{0:T(256)}, u32[]{:S(2)}) copy-start(f32[256]{0:T(256)} %param.21) | copy-start | bytes 3076
  109.5 3.9 copy-start.47
  109.5 42.6 %slice-start = ((s8[5636096]{0:T(1024)(128)(4,1)}), s8[4194304]{0:T(1024)(128)(4,1)S(1)}, s32[]{:S(2)}) async-start(s8[5636096]{0:T(1024)(128)(4,1)} %bitcast.105), calls=%async_computation.6 | async-start | bytes 8388608
  113.5 38.6 %slice-start.1 = ((s8[5636096]{0:T(1024)(128)(4,1)}), s8[1441792]{0:T(1024)(128)(4,1)S(1)}, s32[]{:S(2)}) async-start(s8[5636096]{0:T(1024)(128)(4,1)} %bitcast.105), calls=%async_computation.7 | async-start | bytes 2883584
  162.7 7.1 %copy-start.39 = (bf16[688,512]{1,0:T(8,128)(2,1)}, bf16[688,512]{1,0:T(8,128)(2,1)S(1)}, u32[]{:S(2)}) copy-start(bf16[688,512]{1,0:T(8,128)(2,1)S(1)} %get-tuple-element.138) | copy-start | bytes 2113540
  162.7 7.1 %copy-start.40 = (bf16[688,512]{1,0:T(8,128)(2,1)}, bf16[688,512]{1,0:T(8,128)(2,1)S(1)}, u32[]{:S(2)}) copy-start(bf16[688,512]{1,0:T(8,128)(2,1)S(1)} %get-tuple-element.139) | copy-start | bytes 2113540
  162.7 42.7 %copy-start.28 = (bf16[688,512]{1,0:T(8,128)(2,1)}, bf16[688,512]{1,0:T(8,128)(2,1)S(1)}, u32[]{:S(2)}) copy-start(bf16[688,512]{1,0:T(8,128)(2,1)S(1)} %get-tuple-element.68.middle) | copy-start | bytes 2113540
  162.7 7.1 %copy-start.4 = (f32[64,2048]{1,0:T(8,128)S(1)}, f32[64,2048]{1,0:T(8,128)}, u32[]{:S(2)}) copy-start(f32[64,2048]{1,0:T(8,128)} %copy-done.3) | copy-start | bytes 1572868
  162.7 7.1 %copy-start.8 = (bf16[64,2048]{1,0:T(8,128)(2,1)S(1)}, bf16[64,2048]{1,0:T(8,128)(2,1)}, u32[]{:S(2)}) copy-start(bf16[64,2048]{1,0:T(8,128)(2,1)} %cot.1) | copy-start | bytes 786436
  208.6 187.4 %reduce-scatter.7.cloned.1.call-start = ((), (), s32[]{:S(2)}) async-start(), calls=%async_computation.5 | async-start | bytes 11210752
  224.3 3.8 copy-start.10
  224.4 3.7 copy-start.31
  224.4 3.7 copy-start.33
  228.1 5.4 %copy-start.20 = (bf16[4,2,128,128]{3,2,1,0:T(8,128)(2,1)S(1)}, bf16[4,2,128,128]{3,2,1,0:T(8,128)(2,1)}, u32[]{:S(2)}) copy-start(bf16[4,2,128,128]{3,2,1,0:T(8,128)(2,1)} %copy-done.19) | copy-start | bytes 786436
  233.5 19.6 %copy-start.12 = (bf16[512,512]{1,0:T(8,128)(2,1)}, bf16[512,512]{1,0:T(8,128)(2,1)S(1)}, u32[]{:S(2)}) copy-start(bf16[512,512]{1,0:T(8,128)(2,1)S(1)} %get-tuple-element.83.d_gate) | copy-start | bytes 1572868
  269.8 6.5 %collective-permute-start.1 = (f32[8,1024]{1,0:T(8,128)}, f32[8,1024]{1,0:T(8,128)S(1)}, u32[]{:S(2)}, u32[]{:S(2)}) collective-permute-start(f32[8,1024]{1,0:T(8,128)} %get-tuple-element.86), channel_id=1, source_target_pairs={{8,0},{16,8},{24,16},{32,24},{40,32},{48,40},{56,48},{64,56},{72,6... | collective-permute-start | bytes 98312 | tf_op jit(solution)/shard_map/ppermute | solution.py:698
  271.1 3.8 copy-start.36
  271.1 3.8 copy-start.38
  277.6 8.3 %copy-start.18 = (f32[64,2048]{1,0:T(8,128)S(1)}, f32[64,2048]{1,0:T(8,128)}, u32[]{:S(2)}) copy-start(f32[64,2048]{1,0:T(8,128)} %copy-done.17) | copy-start | bytes 1572868
  277.6 8.3 %copy-start.23 = (f32[2048]{0:T(1024)S(1)}, f32[2048]{0:T(1024)}, u32[]{:S(2)}) copy-start(f32[2048]{0:T(1024)} %param.15) | copy-start | bytes 24580
  285.9 18.9 %copy-start.45 = (f32[1,4]{1,0:T(1,128)S(1)}, f32[1,4]{1,0:T(1,128)}, u32[]{:S(2)}) copy-start(f32[1,4]{1,0:T(1,128)} %get-tuple-element.94) | copy-start | bytes 52
  336.5 57.7 %copy-start.5 = (f32[64,2048]{1,0:T(8,128)S(1)}, f32[64,2048]{1,0:T(8,128)}, u32[]{:S(2)}) copy-start(f32[64,2048]{1,0:T(8,128)} %copy-done.3) | copy-start | bytes 1572868
  394.2 8.9 %copy-start.1 = (bf16[688,2048]{1,0:T(8,128)(2,1)S(1)}, bf16[688,2048]{1,0:T(8,128)(2,1)}, u32[]{:S(2)}) copy-start(bf16[688,2048]{1,0:T(8,128)(2,1)} %param.25) | copy-start | bytes 8454148
  (24 other events, 26.8 us)
Sparse Core Ops, SparseCore 0:
  10.4 28.7 all-gather.2
  40.9 25.4 all-gather.4
  208.7 28.5 reduce-scatter.4
  240.6 127.2 reduce-scatter.6

commit v3 on v2

--- a/solution.py
+++ b/solution.py
@@ -325,7 +325,7 @@
             d_convw_o[j : j + 1, dst] = jnp.sum(masked * xpad[lo : lo + rows, :], axis=0, keepdims=True)
             dpad[lo : lo + rows, :] += convw[j : j + 1, dst].astype(F32) * masked
         d_edge_o[:, dst] = dpad[:PAD, :]
-        d_tail_o[:, dst] = dpad[rows:, :]
+        d_tail_o[:, dst] = dpad[rows - PAD :, :]
         d_proj_o[:, src] = dpad[PAD:, :].astype(BF16)
         d_proj_o[:, pl.ds(h * MIXW + CONVW, DV)] = d_gate[:, pl.ds(h * DV, DV)]
 
@@ -466,14 +466,6 @@
     d_gain_o[...] = d_gain
     block[...] = d_hidden.astype(BF16)
     gather_over_head(block, all_o, s2, r2, ls)
-
-
-def last_backward(x, tokens, d_hidden, gain, d_tokens_o, d_gain_o, total, pair, got, mid, s1, r1):
-    greet(head_peers())
-    reduce_over_head(x, total, pair, got, mid, s1, r1)
-    d_norm, d_gain = norm_back(tokens[...].astype(F32), gain[...], total[...])
-    d_tokens_o[...] = d_hidden[...] + d_norm
-    d_gain_o[...] = d_gain
 
 
 def reach(kernel, outs, scratch, cid, limit, *args, anywhere=(), nbytes=12_000_000):
@@ -597,89 +589,181 @@
         s.wait_send()
 
 
-def reduce_over_seq(x, o, got1, mid, got2, own, ssem, rsem, lsem):
-    half, rows, cols = o.shape
-    me, z, y, dev = seq_place()
-    greet(side_peers())
-    ways = (lambda a, b: dev(b, a), lambda a, b: dev(a, b))
-
-    def piece(i, a, b):
-        owner = ways[i](a, b)[0]
-        return x.at[pl.ds(pl.multiple_of(owner * rows, rows), rows), pl.ds(i * cols, cols)]
-
-    sends, second, kept = [], [], {}
-    for a in (2, 1, 3):
-        for i in range(2):
-            for b in (2, 1, 3, 0):
-                k = (i * SIDE + a) * SIDE + b
-                s = cp(piece(i, a, b), got1.at[i, a, b], ssem.at[k], rsem.at[k], ways[i](a, 0))
-                s.start()
-                sends.append(s)
-    for i in range(2):
-        for b in range(SIDE):
-            kept[i, b] = pltpu.make_async_copy(piece(i, 0, b), own.at[i, b], lsem.at[i * SIDE + b])
-            kept[i, b].start()
-    for b in (2, 1, 3, 0):
-        for i in range(2):
-            kept[i, b].wait()
-            for a in (1, 3, 2):
-                k = (i * SIDE + a) * SIDE + b
-                cp(piece(i, a, b), got1.at[i, a, b], ssem.at[k], rsem.at[k], ways[i](a, 0)).wait_recv()
-            total = own[i, b].astype(F32) + (
-                (got1[i, 1, b].astype(F32) + got1[i, 3, b].astype(F32)) + got1[i, 2, b].astype(F32)
-            )
-            if b:
-                mid[i, b] = total.astype(BF16)
-                k = 2 * SIDE * SIDE + i * SIDE + b
-                s = cp(mid.at[i, b], got2.at[i, b], ssem.at[k], rsem.at[k], ways[i](0, b))
-                s.start()
-                second.append(s)
-            else:
-                o[i] = total
-    for s in second:
-        s.wait_recv()
-    for i in range(2):
-        o[i] = o[i] + ((got2[i, 1].astype(F32) + got2[i, 3].astype(F32)) + got2[i, 2].astype(F32))
-    for s in sends + second:
-        s.wait_send()
-
-
-def small_sums(gains, convs, rate, gains_o, convs_o, rate_o, gbuf, sbuf, rbuf, s1, r1, s2, r2):
+def pair_sends(x, pair, ssem, rsem, steps):
+    rows = pair.shape[1]
+    dev = head_place()[3]
+    out = {}
+    for d in steps:
+        owner = dev(d, True)[1]
+        src = x.at[pl.ds(pl.multiple_of(owner * rows, rows), rows)]
+        out[d] = cp(src, pair.at[d], ssem.at[d], rsem.at[d], dev(0, True))
+        out[d].start()
+    return out
+
+
+def chip_sends(x, first, total, pair, got, mid, ssem, rsem, steps):
+    rows = pair.shape[1]
+    dev = head_place()[3]
+    out = {}
+    for d in steps:
+        first[d].wait_recv()
+        owner = dev(d)[1]
+        both = x[pl.ds(pl.multiple_of(owner * rows, rows), rows), :].astype(F32) + pair[d].astype(F32)
+        if d:
+            mid[d] = both.astype(BF16)
+            out[d] = cp(mid.at[d], got.at[d], ssem.at[CHIPS + d], rsem.at[CHIPS + d], dev(d))
+            out[d].start()
+        else:
+            total[...] = both
+    return out
+
+
+def chip_sum(second, total, got):
+    for d in (1, 3, 2):
+        second[d].wait_recv()
+    return total[...] + ((got[1].astype(F32) + got[3].astype(F32)) + got[2].astype(F32))
+
+
+FAR = (2, 1, 3, 0)
+
+
+def finish(
+    dproj, normed, w, d_rate, rate_w, d_tail, d_edge, feed, hidden, tokens, d_hidden, gain, convs, decay, g_feed, g_head,
+    layer_o, d_tokens_o, g_mixer_o, gains_o, convs_o, rate_o,
+    dp, wv, edge, g, got1, mid, got2, dn, ta, pa, ga, ma, tb, pb, gb, mb, gains, gbuf, sbuf, rbuf,
+    es, er, ls, s1, r1, sa, ra, sb, rb, sg, rg, ss, rs
+):
     me, z, y, dev = seq_place()
     head = lax.axis_index("head")
     heads, seqs = gbuf.shape[0], rbuf.shape[0]
-    g = gains.shape[0]
-    c = convs.shape[0]
+    rows = dp.shape[0]
+    part, half = g_mixer_o.shape[1], g_mixer_o.shape[2]
     across = [(me, lax.rem(head + d, heads)) for d in range(1, heads)]
     along = [(lax.rem(me + d, seqs), head) for d in range(1, seqs)]
+    load_p = pltpu.make_async_copy(dproj, dp, ls.at[0])
+    load_p.start()
+    load_w = pltpu.make_async_copy(w, wv, ls.at[1])
+    load_w.start()
     greet(across + along)
+    back = cp(d_edge, edge, es, er, (lax.rem(me + seqs - 1, seqs), head))
+    back.start()
+    feed_one = pair_sends(feed, pa, sa, ra, FAR)
+    load_p.wait()
+    back.wait_recv()
+    there = jnp.where(me < seqs - 1, edge[...], 0.0)
+    tail = jnp.concatenate([d_tail[:PAD, :], d_tail[PAD:, :] + there], axis=0).astype(BF16)
+    wide = half - DV
+    for i in range(2):
+        dp[rows - 2 * PAD :, pl.ds(i * half, wide)] = tail[:, i * wide : (i + 1) * wide]
+
+    ways = (lambda a, b: dev(b, a), lambda a, b: dev(a, b))
+
+    def piece(i, owner):
+        return g.at[i, owner]
+
+    first, second = {}, {}
+    places = [(dz, dy) for dz in FAR for dy in FAR]
+    for dz, dy in places:
+        owner = dev(dz, dy)[0]
+        left = normed[:, pl.ds(pl.multiple_of(owner * part, part), part)]
+        for i in range(2):
+            a, b = (dy, dz) if i == 0 else (dz, dy)
+            g[i, owner] = dot(left, dp[:, i * half : (i + 1) * half], "tn").astype(BF16)
+            if a:
+                k = (i * SIDE + a) * SIDE + b
+                first[i, a, b] = cp(piece(i, owner), got1.at[i, a, b], s1.at[k], r1.at[k], ways[i](a, 0))
+                first[i, a, b].start()
+    feed_two = chip_sends(feed, feed_one, ta, pa, ga, ma, sa, ra, FAR)
+    rates_t = dot(d_rate[:, :PAD], normed[...], "tn")
+
+    load_w.wait()
+    low = rows // CHIPS
+    hp = head_place()[3]
+    dn_one = {}
+    for d in FAR:
+        chip = hp(d)[1] // 2
+        here = pl.ds(pl.multiple_of(chip * low, low), low)
+        dn[here, :] = (dot(dp[here, :], wv[...], "nt") + dot(d_rate[here, :], rate_w[...], "nt")).astype(BF16)
+        dn_one.update(pair_sends(dn, pb, sb, rb, (d,)))
+    dn_two = chip_sends(dn, dn_one, tb, pb, gb, mb, sb, rb, FAR)
+    layer_o[...] = (hidden[...] + chip_sum(feed_two, ta, ga)).astype(BF16)
+    d_norm, d_gain = norm_back(tokens[...].astype(F32), gain[...], chip_sum(dn_two, tb, gb))
+    d_tokens_o[...] = d_hidden[...] + d_norm
+
+    ng = gains.shape[0]
+    n_row = D // LANES
+    gains[...] = jnp.zeros_like(gains)
+    for r in range(n_row):
+        at = slice(r * LANES, (r + 1) * LANES)
+        gains[r : r + 1, :] = d_gain[:, at]
+        gains[n_row + r : n_row + r + 1, :] = g_feed[:, at]
+    for r in range(DV // LANES):
+        gains[2 * n_row + r : 2 * n_row + r + 1, :] = g_head[:, r * LANES : (r + 1) * LANES]
     gbuf[head] = gains[...]
-    out = [cp(gains, gbuf.at[head], s1.at[d], r1.at[d], across[d - 1]) for d in range(1, heads)]
-    for s in out:
+    g_out = [cp(gains, gbuf.at[head], sg.at[d], rg.at[d], across[d - 1]) for d in range(1, heads)]
+    for s in g_out:
         s.start()
+    taps, wide_c = convs.shape
+    c_row = wide_c // LANES
+    nc = taps * c_row
+    for j in range(seqs):
+        for t in range(taps):
+            for r in range(c_row):
+                lo = ng + t * c_row + r
+                if j == 0:
+                    sbuf[0, lo : lo + 1, :] = convs[t : t + 1, r * LANES : (r + 1) * LANES]
+        if j == 0:
+            sbuf[0, ng + nc : ng + nc + PAD, :] = jnp.zeros((PAD, LANES), F32)
+            sbuf[0, ng + nc : ng + nc + 1, :] = decay[...]
+        else:
+            sbuf[j, ng : ng + nc + PAD, :] = sbuf[0, ng : ng + nc + PAD, :]
+        sbuf[j, ng + nc + PAD :, :] = rates_t[:, j * LANES : (j + 1) * LANES]
     for d in range(1, heads):
-        cp(gains, gbuf.at[lax.rem(head + heads - d, heads)], s1.at[d], r1.at[d], across[d - 1]).wait_recv()
+        cp(gains, gbuf.at[lax.rem(head + heads - d, heads)], sg.at[d], rg.at[d], across[d - 1]).wait_recv()
     total = gbuf[0]
     for i in range(1, heads):
         total = total + gbuf[i]
     for j in range(seqs):
-        sbuf[j, :g] = total
-        sbuf[j, g : g + c] = convs[...]
-        sbuf[j, g + c :] = rate[j]
+        sbuf[j, :ng, :] = total
     rbuf[me] = sbuf[me]
+    s_out = []
     for d in range(1, seqs):
-        s = cp(sbuf.at[lax.rem(me + d, seqs)], rbuf.at[me], s2.at[d], r2.at[d], along[d - 1])
+        s = cp(sbuf.at[lax.rem(me + d, seqs)], rbuf.at[me], ss.at[d], rs.at[d], along[d - 1])
         s.start()
-        out.append(s)
+        s_out.append(s)
+
+    for b in FAR:
+        for i in range(2):
+            for a in (1, 3, 2):
+                first[i, a, b].wait_recv()
+            mine = g[i, ways[i](0, b)[0]].astype(F32)
+            both = mine + (
+                (got1[i, 1, b].astype(F32) + got1[i, 3, b].astype(F32)) + got1[i, 2, b].astype(F32)
+            )
+            if b:
+                mid[i, b] = both.astype(BF16)
+                k = 2 * SIDE * SIDE + i * SIDE + b
+                second[i, b] = cp(mid.at[i, b], got2.at[i, b], s1.at[k], r1.at[k], ways[i](0, b))
+                second[i, b].start()
+            else:
+                g_mixer_o[i] = both
     for d in range(1, seqs):
-        cp(sbuf.at[0], rbuf.at[lax.rem(me + seqs - d, seqs)], s2.at[d], r2.at[d], along[d - 1]).wait_recv()
+        cp(sbuf.at[0], rbuf.at[lax.rem(me + seqs - d, seqs)], ss.at[d], rs.at[d], along[d - 1]).wait_recv()
     total = rbuf[0]
     for i in range(1, seqs):
         total = total + rbuf[i]
-    gains_o[...] = total[:g]
-    convs_o[...] = total[g : g + c]
-    rate_o[...] = total[g + c :]
-    for s in out:
+    gains_o[...] = total[:ng]
+    convs_o[...] = total[ng : ng + nc + PAD]
+    rate_o[...] = total[ng + nc + PAD :]
+    for i in range(2):
+        for b in (1, 3, 2):
+            second[i, b].wait_recv()
+        g_mixer_o[i] = g_mixer_o[i] + (
+            (got2[i, 1].astype(F32) + got2[i, 3].astype(F32)) + got2[i, 2].astype(F32)
+        )
+    done = list(first.values()) + list(second.values()) + g_out + s_out + [back]
+    done += list(feed_one.values()) + list(feed_two.values()) + list(dn_one.values()) + list(dn_two.values())
+    for s in done:
         s.wait_send()
 
 
@@ -780,11 +864,6 @@
         [pltpu.VMEM((own, D), F32), pltpu.VMEM((own, D), BF16)] + reduce_scratch(own, D) + gather_scratch(),
         3, 48, d_two, hidden, cotangent, feed_row,
     )
-    d_mixed, middle = lax.optimization_barrier((d_mixed, middle))
-    feed = lax.dot_general(middle, down_weight, by_first, preferred_element_type=F32).astype(BF16)
-    feed_sum = lax.psum_scatter(feed, "head", scatter_dimension=0, tiled=True).astype(F32)
-    layer_out = (hidden + feed_sum).astype(BF16)
-    d_mixed, feed = lax.optimization_barrier((d_mixed, feed))
     wide = 3 * hid + heads * DV
     right = pl.BlockSpec((rows, 2 * LANES), lambda j: (0, j))
 
@@ -801,7 +880,8 @@
         compiler_params=pltpu.CompilerParams(vmem_limit_bytes=48 << 20),
         cost_estimate=pl.CostEstimate(flops=2 * wide * rows * D, bytes_accessed=24_000_000, transcendentals=0),
     )(d_gate_up, middle, gated_t, gathered_two, cot_rows, d_mixed)
-    d_mixed, grads = lax.optimization_barrier((d_mixed, grads))
+    d_mixed, grads, middle = lax.optimization_barrier((d_mixed, grads, middle))
+    feed = lax.dot_general(middle, down_weight, by_first, preferred_element_type=F32).astype(BF16)
     grads = lax.psum_scatter(grads.reshape(seq * wide, LANES), "seq", scatter_dimension=0, tiled=True).astype(F32)
     grad_gate_up = grads[: 2 * hid].reshape(2, hid, LANES).transpose(2, 0, 1)
     grad_down = grads[2 * hid : 3 * hid]
@@ -827,7 +907,7 @@
     d_projected, d_tail, d_edge, d_rate, d_convw, d_decay = call(
         bwd_mix,
         [
-            sds((rows, heads * MIXW), BF16), sds((PAD, heads * CONVW)), sds((PAD, heads * CONVW)),
+            sds((rows, heads * MIXW), BF16), sds((2 * PAD, heads * CONVW)), sds((PAD, heads * CONVW)),
             sds((rows, 2 * heads)), sds((KCONV, heads * CONVW)), sds((1, 2 * heads)),
         ],
         [
@@ -837,63 +917,44 @@
         60, info, later, conv, dec, inv, wu, states, step, y, d_out, d_gate, rate_proj, projected, halo, convw,
         dlog, dbias,
     )
-    tail = (d_tail + passed_along(d_edge, "seq", -1)).astype(BF16)
-    for h in range(heads):
-        d_projected = lax.dynamic_update_slice(
-            d_projected, tail[:, h * CONVW : (h + 1) * CONVW], (rows - PAD, h * MIXW)
-        )
-    d_rate_low = d_rate.astype(BF16)
-    d_normed = (
-        jnp.einsum("tw,dw->td", d_projected, mixer_flat, preferred_element_type=F32)
-        + jnp.einsum("tg,dg->td", d_rate_low, rate_weight.reshape(D, 2 * heads), preferred_element_type=F32)
-    ).astype(BF16)
-    grad_rate = jnp.einsum("td,tg->dg", gathered, d_rate_low, preferred_element_type=F32)
-    grad_tokens, g_mixer_gain = reach(
-        last_backward,
-        [sds((own, D)), sds((1, D))],
-        [pltpu.VMEM((own, D), F32)] + reduce_scratch(own, D),
-        5, 48, d_normed, tokens, d_hidden, mixer_gain.reshape(1, D),
-    )
-    grad_mixer = jnp.einsum("td,tw->dw", gathered, d_projected, preferred_element_type=F32).astype(BF16)
-    half = heads * MIXW // 2
-    part = D // seq
-    (grad_mixer,) = reach(
-        reduce_over_seq,
-        [sds((2, part, half))],
+    part, half, n_head = D // seq, MIXW, lax.axis_size("head")
+    d_rate_low = jnp.pad(d_rate.astype(BF16), ((0, 0), (0, LANES - 2 * heads)))
+    rate_pad = jnp.pad(rate_weight.reshape(D, 2 * heads), ((0, 0), (0, LANES - 2 * heads)))
+    d_decay = jnp.pad(d_decay, ((0, 0), (0, LANES - 2 * heads)))
+    n_gain, n_conv = 40, KCONV * heads * CONVW // LANES + PAD
+    small = n_gain + n_conv + PAD
+    layer_out, grad_tokens, grad_mixer, gains, convs, rate_own = reach(
+        finish,
         [
+            sds((own, D), BF16), sds((own, D)), sds((2, part, half)), sds((n_gain, LANES)), sds((n_conv, LANES)),
+            sds((PAD, LANES)),
+        ],
+        [
+            pltpu.VMEM((rows, heads * MIXW), BF16), pltpu.VMEM((D, heads * MIXW), BF16),
+            pltpu.VMEM((PAD, heads * CONVW), F32), pltpu.VMEM((2, seq, part, half), BF16),
             pltpu.VMEM((2, SIDE, SIDE, part, half), BF16), pltpu.VMEM((2, SIDE, part, half), BF16),
-            pltpu.VMEM((2, SIDE, part, half), BF16), pltpu.VMEM((2, SIDE, part, half), BF16),
-            sems(2 * SIDE * SIDE + 2 * SIDE), sems(2 * SIDE * SIDE + 2 * SIDE), sems(2 * SIDE),
+            pltpu.VMEM((2, SIDE, part, half), BF16), pltpu.VMEM((rows, D), BF16),
+        ]
+        + 2 * ([pltpu.VMEM((own, D), F32)] + [pltpu.VMEM((CHIPS, own, D), BF16) for _ in range(3)])
+        + [
+            pltpu.VMEM((n_gain, LANES), F32), pltpu.VMEM((n_head, n_gain, LANES), F32),
+            pltpu.VMEM((seq, small, LANES), F32), pltpu.VMEM((seq, small, LANES), F32),
+            pltpu.SemaphoreType.DMA, pltpu.SemaphoreType.DMA, sems(2),
+            sems(2 * SIDE * SIDE + 2 * SIDE), sems(2 * SIDE * SIDE + 2 * SIDE),
+            sems(2 * CHIPS), sems(2 * CHIPS), sems(2 * CHIPS), sems(2 * CHIPS),
+            sems(n_head), sems(n_head), sems(seq), sems(seq),
         ],
-        6, 56, grad_mixer, anywhere=(0,), nbytes=40_000_000,
+        5, 62, d_projected, gathered, mixer_flat, d_rate_low, rate_pad, d_tail, d_edge, feed, hidden, tokens,
+        d_hidden, mixer_gain.reshape(1, D), d_convw, d_decay, g_feed_gain, g_head_gain,
+        anywhere=(0, 2), nbytes=40_000_000,
     )
     grad_mixer = grad_mixer.transpose(1, 0, 2)
-
-    def packed(*arrays):
-        flat = jnp.concatenate([a.reshape(-1) for a in arrays])
-        size = -(-flat.size // (8 * LANES)) * 8 * LANES
-        return jnp.pad(flat, (0, size - flat.size)).reshape(-1, LANES)
-
-    gains = packed(g_mixer_gain, g_feed_gain, g_head_gain)
-    convs = packed(d_convw, d_decay)
-    rate_own = jnp.pad(grad_rate.reshape(seq, -1, LANES), ((0, 0), (0, 8 - 2 * heads), (0, 0)))
-    n_gain, n_conv = gains.shape[0], convs.shape[0]
-    gains, convs, rate_own = reach(
-        small_sums,
-        [sds((n_gain, LANES)), sds((n_conv, LANES)), sds((8, LANES))],
-        [
-            pltpu.VMEM((lax.axis_size("head"), n_gain, LANES), F32),
-            pltpu.VMEM((seq, n_gain + n_conv + 8, LANES), F32), pltpu.VMEM((seq, n_gain + n_conv + 8, LANES), F32),
-            sems(8), sems(8), sems(16), sems(16),
-        ],
-        7, 40, gains, convs, rate_own, nbytes=1_000_000,
-    )
     gains, convs = gains.reshape(-1), convs.reshape(-1)
     grad_mixer_gain, grad_feed_gain, grad_head_gain = gains[:D], gains[D : 2 * D], gains[2 * D : 2 * D + DV]
     n = KCONV * heads * CONVW
     grad_conv = convs[:n].reshape(KCONV, heads, CONVW)
     grad_decay_log, grad_decay_bias = convs[n : n + heads], convs[n + heads : n + 2 * heads]
-    grad_rate = rate_own[: 2 * heads].reshape(part, 2, heads)
+    grad_rate = rate_own[: 2 * heads].reshape(2, heads, part).transpose(2, 0, 1)
     return (
         layer_out, grad_tokens, grad_mixer_gain, grad_mixer, grad_rate, grad_conv, grad_decay_log, grad_decay_bias,
         grad_head_gain, grad_output, grad_feed_gain, grad_gate_up, grad_down,

time: 414 us -> 387 us (0.935)
  matrix products: 53.3 us -> 37.7 us
  Pallas kernels: 266 us -> 257 us
    dot_general x4 -> x0, matrix products: 21.3 us -> none  [the longest x1 8.49 us: local(): jnp.einsum('td,tw->dw', gathered, d_projected, preferred_element_type=F32)]
    pallas_call x7 -> x5, Pallas kernels: 207 us -> 197 us  [reach(): pl.pallas_call(kernel, out_shape=outs, in_specs=[pl.BlockSpec(memory_spac...]
    unnamed x106 -> x69, local copies, waits for them, and re-layouts: 30.3 us -> 25.9 us
  transfers between devices with their start and end apart: 6 -> 4, of which waited for: 1 -> 1; matrix products, arithmetic and copies ran while one was open for 14% -> 13% of each run, Pallas kernels for 57% -> 55%
where the time goes in v3:
time: 387 us; the launch traced here: 383 us
  Pallas kernels  257 us (66%)
  local copies, waits for them, and re-layouts  43.6 us (11%)
  matrix products  37.7 us (10%)
  waiting for transfers between devices  22.1 us (6%)
  between operations  14.4 us (4%)
  other arithmetic  5.17 us (1%)
    pallas_call x5, Pallas kernels, reach(): pl.pallas_call(kernel, out_shape=outs, in_specs=[pl.BlockSpec(memory_spac...  197 us
    pallas_call x4, Pallas kernels, call(): pl.pallas_call(kernel, out_shape=outs, in_specs=[spec(a) for a in args],...  48.7 us
    unnamed x69, local copies, waits for them, and re-layouts  25.9 us
    all_gather x1, waiting for transfers between devices, local(): gathered = lax.all_gather(normed, 'head', axis=0, tiled=True)  22.1 us
    pallas_call x1, Pallas kernels, local(): pl.pallas_call(weight_grads, grid=(seq // 2,), out_shape=sds((seq, wide,...  11.3 us
  transfers between devices with their start and end apart: 4, of which 1 were waited for; matrix products, arithmetic and copies ran while one was open for 13% of the time, Pallas kernels for 55%

profile of v3, /device:TPU:1, one launch (start us, length us, event | category | flops | bytes accessed | tf_op | source)
XLA Modules:
  0.0 383.0 jit_solution(8482245042924068870)
XLA Ops:
  8.3 1.8 fusion.4
  10.2 6.8 %copy.41 = bf16[256,8,2,768]{3,1,2,0:T(8,128)(2,1)} copy(bf16[256,8,2,768]{3,2,1,0:T(2,128)(2,1)} %bitcast.68) | data formatting | bytes 12582912
  17.0 22.1 %all-gather.3.cloned.1.call-done.normed = bf16[512,2048]{1,0:T(8,128)(2,1)} async-done(((bf16[64,2048]{1,0:T(8,128)(2,1)}), bf16[512,2048]{1,0:T(8,128)(2,1)}) %all-gather.3.cloned.1.call-update) | async-done | bytes 2097168 | tf_op jit(solution)/shard_map/all_gather | solution.py:795
  40.4 6.9 %fusion.6.proj = f32[512,1536]{1,0:T(8,128)S(1)} fusion(bf16[512,2048]{1,0:T(8,128)(2,1)} %all-gather.3.cloned.1.call-done.normed, bf16[2048,1536]{1,0:T(8,128)(2,1)} %bitcast.65), kind=kOutput, calls=%fused_computation.24 | convolution fusion | flops 3221225472 | bytes 11534336 | tf_op jit(solution)/shard_map/dot_general | solution.py:805
  47.3 1.6 copy-done.25
  48.9 3.3 collective-permute-start
  54.4 25.7 %shard_map.237 = (f32[512,1024]{1,0:T(8,128)}, f32[4,256,256]{2,1,0:T(8,128)}, bf16[4,256,256]{2,1,0:T(8,128)(2,1)}, f32[4,256,384]{2,1,0:T(8,128)}, f32[512,256...) custom-call(s32[6]{0:T(128)} %pad_add_fusion.info, ...), custom_call_target="tpu_custom_call" | custom-call | flops 2000000000 | bytes 16000000 | tf_op jit(solution)/shard_map/pallas_call | solution.py:337
  81.0 24.4 %shard_map.238 = (f32[2,256,128]{2,1,0:T(8,128)S(1)}, bf16[4,2,128,128]{3,2,1,0:T(8,128)(2,1)S(1)}, bf16[4,2,128,128]{3,2,1,0:T(8,128)(2,1)S(1)}) custom-call(bf16[2,384,128]{2,1,0:T(8,128)(2,1)S(1)} %copy-done.11), custom_call_target="tpu_custom_call" | custom-call | bytes 12000000 | tf_op jit(solution)/shard_map/pallas_call | solution.py:472
  108.9 2.8 shard_map.239
  113.7 2.9 convolution_convert_fusion.1.x
  116.7 36.0 %shard_map.240 = (bf16[512,2048]{1,0:T(8,128)(2,1)S(1)}, f32[64,2048]{1,0:T(8,128)S(1)}) custom-call(bf16[512,2048]{1,0:T(8,128)(2,1)S(1)} %convolution_convert_fusion.1.x, bf16[64,2048]{1,0:T(8,128)(2,1)S(1)} %copy-done, f32[1,2048]{1,0:T(1,128)S(1)} %bitcast.61), custom_call_target="tpu_custom_call" | custom-call | bytes 12000000 | tf_op jit(solution)/shard_map/pallas_call | solution.py:472
  152.7 7.4 %convolution_bitcast_fusion = f32[1376,512]{1,0:T(8,128)} fusion(bf16[512,2048]{1,0:T(8,128)(2,1)S(1)} %get-tuple-element.64.n2, bf16[1376,2048]{1,0:T(8,128)(2,1)} %bitcast.84), kind=kOutput, calls=%fused_computation | convolution fusion | flops 2885681152 | bytes 10551296 | tf_op jit(solution)/shard_map/dot_general | solution.py:855
  160.2 1.4 copy-done.15
  161.5 5.4 %multiply_convert_fusion.2 = (bf16[688,512]{1,0:T(8,128)(2,1)S(1)}, bf16[688,512]{1,0:T(8,128)(2,1)S(1)}, bf16[688,512]{1,0:T(8,128)(2,1)S(1)}) fusion(f32[1376,512]{1,0:T(8,128)} %convolution_bitcast_fusion, bf16[512,2048]{1,0:T(8,128)(2,1)} %all-gather.5.cloned.1.call-done.cot, bf16[688,2048]{1,0:T(8,128)(2,1)} %param.25), kind=kOutput, calls=%fused_computation.10 | convolution fusion | flops 1448476672 | bytes 9846784 | tf_op jit(solution)/shard_map/dot_general | solution.py:854
  167.0 6.3 %convolution_convert_fusion.2.x = bf16[512,2048]{1,0:T(8,128)(2,1)S(1)} fusion(bf16[1376,2048]{1,0:T(8,128)(2,1)} %bitcast.85, bf16[688,512]{1,0:T(8,128)(2,1)S(1)} %get-tuple-element.137, bf16[688,512]{1,0:T(8,128)(2,1)S(1)} %get-tuple-element.136), kind=kOutput, calls=%fused_computation.3 | convolution fusion | flops 2889547776 | bytes 9142272 | tf_op jit(solution)/shard_map/dot_general | solution.py:860
  173.4 33.4 %shard_map.241 = (bf16[512,2048]{1,0:T(8,128)(2,1)S(1)}, f32[64,2048]{1,0:T(8,128)S(1)}, f32[1,2048]{1,0:T(1,128)S(1)}) custom-call(bf16[512,2048]{1,0:T(8,128)(2,1)S(1)} %convolution_convert_fusion.2.x, f32[64,2048]{1,0:T(8,128)S(1)} %get-tuple-element.65.hidden, bf16[64,2048]{1,0:T(8,128)(2,1)S(1)} %copy-done.4, f32[1,2048]{1,0:T(1,128)S(1)} %bitcast.62), custom_call_target="tpu_custom_call" | custom-call | bytes 12000000 | tf_op jit(solution)/shard_map/pallas_call | solution.py:472
  208.2 1.3 copy-done.17
  209.5 11.3 %shard_map.242 = bf16[16,2576,128]{2,1,0:T(8,128)(2,1)} custom-call(bf16[1376,512]{1,0:T(8,128)(2,1)S(1)} %pad_maximum_fusion.d_gu, bf16[688,512]{1,0:T(8,128)(2,1)S(1)} %get-tuple-element.84.middle, bf16[512,512]{1,0:T(8,128)(2,1)S(1)} %bitcast.60, bf16[512,2048]{1,0:T(8,128)(2,1)S(1)} %copy-done.16, bf16[512,2048]{1,0:T(8,128)(2,1)} %all-gather.5.cloned.1.call-done.cot, ...), custom_call_target="tpu_custom_call" | custom-call | flops 5402263552 | bytes 24000000 | tf_op jit(solution)/shard_map/pallas_call | solution.py:874
  222.0 1.9 pad.13.rate_w
  224.0 3.1 fusion.7.d_gated
  227.1 4.0 %shard_map.243 = (f32[512,512]{1,0:T(8,128)S(1)}, bf16[512,512]{1,0:T(8,128)(2,1)S(1)}, f32[1,256]{1,0:T(1,128)S(1)}, f32[4,256,128]{2,1,0:T(8,128)S(1)}, bf16[2,256,128]{2,1,0:T(8,128)(2,1)S(1)}) custom-call(f32[512,512]{1,0:T(8,128)S(1)} %fusion.7.d_gated, f32[512,512]{1,0:T(8,128)S(1)} %copy-done.21, f32[512,1536]{1,0:T(8,128)} %copy-done.25, ...), custom_call_target="tpu_custom_call" | custom-call | flops 2000000000 | bytes 16000000 | tf_op jit(solution)/shard_map/pallas_call | solution.py:337
  232.9 28.6 %shard_map.244.later = f32[2,256,128]{2,1,0:T(8,128)S(1)} custom-call(bf16[2,256,128]{2,1,0:T(8,128)(2,1)S(1)} %get-tuple-element.69.inc, bf16[4,2,128,128]{3,2,1,0:T(8,128)(2,1)S(1)} %get-tuple-element.70.ga, bf16[4,2,128,128]{3,2,1,0:T(8,128)(2,1)S(1)} %get-tuple-element.71.ta), custom_call_target="tpu_custom_call" | custom-call | bytes 12000000 | tf_op jit(solution)/shard_map/pallas_call | solution.py:472
  262.2 16.1 %shard_map.245 = (bf16[512,1536]{1,0:T(8,128)(2,1)}, f32[16,1024]{1,0:T(8,128)}, f32[8,1024]{1,0:T(8,128)}, f32[512,4]{1,0:T(8,128)}, f32[4,1024]{1,0:T(4,128)}, /*index=5*/f32[1,4]{1,0:T(1,128)}) custom-call(s32[6]{0:T(128)} %pad_add_fusion.info, f32[2,256,128]{2,1,0:T(8,128)} %copy-done.3, f32[512,1024]{1,0:T(8,128)} %get-tuple-element.72.conv, ...), custom_call_target="tpu_custom_call" | custom-call | flops 2000000000 | bytes 16000000 | tf_op jit(solution)/shard_map/pallas_call | solution.py:337
  281.2 5.0 %convolution_convert_fusion.feed = bf16[512,2048]{1,0:T(8,128)(2,1)} fusion(bf16[688,512]{1,0:T(8,128)(2,1)S(1)} %get-tuple-element.84.middle, bf16[688,2048]{1,0:T(8,128)(2,1)} %param.25), kind=kOutput, calls=%fused_computation.1 | convolution fusion | flops 1443889152 | bytes 5619712 | tf_op jit(solution)/shard_map/dot_general | solution.py:884
  286.2 74.1 %shard_map.246 = (bf16[64,2048]{1,0:T(8,128)(2,1)}, f32[64,2048]{1,0:T(8,128)}, f32[2,128,768]{2,1,0:T(8,128)}, f32[40,128]{1,0:T(8,128)}, f32[40,128]{1,0:T(8,128)}, /*index=5*/f32[8,128]{1,0:T(8,128)}) custom-call(bf16[512,1536]{1,0:T(8,128)(2,1)} %get-tuple-element.80.dproj, bf16[512,2048]{1,0:T(8,128)(2,1)} %all-gather.3.cloned.1.call-done.normed, ...), custom_call_target="tpu_custom_call" | custom-call | bytes 40000000 | tf_op jit(solution)/shard_map/pallas_call | solution.py:472
  360.3 2.7 copy.40
  364.4 1.3 slice.60
  365.6 1.3 fusion.5
  368.2 1.3 slice_bitcast_fusion
  369.5 1.9 slice.78
  371.4 1.7 slice.79
  373.1 1.6 slice.77
  (92 shorter events, 23.0 us)
Async XLA Ops:
  7.2 31.9 %all-gather.3.cloned.1.call-start = ((), (), s32[]{:S(2)}) async-start(), calls=%async_computation.1 | async-start | bytes 2359296 | tf_op jit(solution)/shard_map/all_gather | solution.py:795
  10.2 151.4 %all-gather.5.cloned.1.call-start = ((), (), s32[]{:S(2)}) async-start(), calls=%async_computation.2 | async-start | bytes 2359296 | tf_op jit(solution)/shard_map/all_gather | solution.py:800
  10.2 29.0 %copy-start.30 = (bf16[4,2,512]{2,1,0:T(2,128)(2,1)S(1)}, bf16[4,2,512]{2,1,0:T(2,128)(2,1)}, u32[]{:S(2)}) copy-start(bf16[4,2,512]{2,1,0:T(2,128)(2,1)} %param.18) | copy-start | bytes 24580
  10.2 29.6 %copy-start.31 = (s32[4]{0:T(128)S(1)}, s32[4]{0:T(128)}, u32[]{:S(2)}) copy-start(s32[4]{0:T(128)} %param.26) | copy-start | bytes 52
  39.1 330.4 %reduce-scatter.4.cloned.1.call-start = ((), (), s32[]{:S(2)}) async-start(), calls=%async_computation.3 | async-start | bytes 11210752
  40.4 11.8 %copy-start.26 = (bf16[512,2048]{1,0:T(8,128)(2,1)S(1)}, bf16[512,2048]{1,0:T(8,128)(2,1)}, u32[]{:S(2)}) copy-start(bf16[512,2048]{1,0:T(8,128)(2,1)} %all-gather.3.cloned.1.call-done.normed) | copy-start | bytes 6291460
  40.4 11.8 %copy-start.29 = (bf16[2048,2,2]{0,2,1:T(2,128)(2,1)S(1)}, bf16[2048,2,2]{0,2,1:T(2,128)(2,1)}, u32[]{:S(2)}) copy-start(bf16[2048,2,2]{0,2,1:T(2,128)(2,1)} %param.17) | copy-start | bytes 49156
  47.3 1.6 copy-start.25
  48.9 4.8 %collective-permute-start = (bf16[8,1024]{1,0:T(8,128)(2,1)S(1)}, bf16[8,1024]{1,0:T(8,128)(2,1)S(1)}, u32[]{:S(2)}, u32[]{:S(2)}) collective-permute-start(bf16[8,1024]{1,0:T(8,128)(2,1)S(1)} %bitcast.76), channel_id=1, source_target_pairs={{0,8},{8,16},{16,24},{24,32},{32,40},{40,48},{48,56},{56,64},{64,7... | collective-permute-start | bytes 49160 | tf_op jit(solution)/shard_map/ppermute | solution.py:782
  54.4 51.1 %copy-start.19 = (f32[256]{0:T(256)S(1)}, f32[256]{0:T(256)}, u32[]{:S(2)}) copy-start(f32[256]{0:T(256)} %param.21) | copy-start | bytes 3076
  80.1 0.9 copy-start.11
  105.5 1.1 copy-start.5
  106.6 1.0 copy-start.22
  107.7 1.2 copy-start.24
  111.7 0.8 copy-start.8
  112.5 1.0 copy-start.20
  113.7 3.0 copy-start
  113.7 3.0 copy-start.12
  152.7 20.7 %copy-start.1 = (f32[64,2048]{1,0:T(8,128)}, f32[64,2048]{1,0:T(8,128)S(1)}, u32[]{:S(2)}) copy-start(f32[64,2048]{1,0:T(8,128)S(1)} %get-tuple-element.65.hidden) | copy-start | bytes 1572868
  160.2 1.4 copy-start.15
  167.0 6.4 %copy-start.4 = (bf16[64,2048]{1,0:T(8,128)(2,1)S(1)}, bf16[64,2048]{1,0:T(8,128)(2,1)}, u32[]{:S(2)}) copy-start(bf16[64,2048]{1,0:T(8,128)(2,1)} %cot.1) | copy-start | bytes 786436
  173.4 36.2 %copy-start.16 = (bf16[512,2048]{1,0:T(8,128)(2,1)S(1)}, bf16[512,2048]{1,0:T(8,128)(2,1)}, u32[]{:S(2)}) copy-start(bf16[512,2048]{1,0:T(8,128)(2,1)} %copy-done.15) | copy-start | bytes 6291460
  208.2 1.3 copy-start.17
  220.9 3.1 copy-start.18
  224.0 3.1 copy-start.6
  224.0 3.1 copy-start.21
  224.0 3.2 copy-start.23
  231.1 1.0 copy-start.2
  232.9 28.6 %copy-start.9 = (bf16[512,512]{1,0:T(8,128)(2,1)}, bf16[512,512]{1,0:T(8,128)(2,1)S(1)}, u32[]{:S(2)}) copy-start(bf16[512,512]{1,0:T(8,128)(2,1)S(1)} %get-tuple-element.79.d_gate) | copy-start | bytes 1572868
  232.9 29.3 %copy-start.14 = (f32[1,256]{1,0:T(1,128)}, f32[1,256]{1,0:T(1,128)S(1)}, u32[]{:S(2)}) copy-start(f32[1,256]{1,0:T(1,128)S(1)} %get-tuple-element.89.g_head) | copy-start | bytes 3076
  360.3 14.4 %copy-start.28 = (bf16[64,2048]{1,0:T(8,128)(2,1)S(1)}, bf16[64,2048]{1,0:T(8,128)(2,1)}, u32[]{:S(2)}) copy-start(bf16[64,2048]{1,0:T(8,128)(2,1)} %get-tuple-element.156) | copy-start | bytes 786436
  360.3 15.1 %copy-start.27 = (f32[64,2048]{1,0:T(8,128)S(1)}, f32[64,2048]{1,0:T(8,128)}, u32[]{:S(2)}) copy-start(f32[64,2048]{1,0:T(8,128)} %get-tuple-element.157) | copy-start | bytes 1572868
  (4 other events, 2.9 us)
Sparse Core Ops, SparseCore 0:
  10.3 28.7 all-gather.2
  40.8 25.4 all-gather.4
  221.0 141.0 reduce-scatter.3

commit v4 on v3

--- a/solution.py
+++ b/solution.py
@@ -233,9 +233,18 @@
 
 
 def bwd_mix(
-    info, later, conv, dec, inv, wu, states, step, y, d_out, d_gate, rate, proj, halo, convw, dlog, dbias,
-    d_proj_o, d_tail_o, d_edge_o, d_rate_o, d_convw_o, d_decay_o, xpad, dpad, dsend, cols_s, d_pre_o
+    info, later, conv, dec, inv, wu, states, step, y, d_out, d_gate, rate, proj, halo, convw, dlog, dbias, g_down, g_out,
+    d_proj_o, d_tail_o, d_edge_o, d_rate_o, d_convw_o, d_decay_o, s_down_o, s_out_o,
+    xpad, dpad, dsend, cols_s, d_pre_o, relay_d, relay_o, got_d, got_o, s1, r1
 ):
+    greet(side_peers())
+    grads = (g_down, g_out)
+    spread = Spread(
+        lambda i, owner: grads[i].at[owner], lambda i, b: (relay_d, relay_o)[i].at[b],
+        lambda i, s, b: (got_d, got_o)[i].at[s, b], s1, r1,
+    )
+    for place in PLACES:
+        spread.ready(*place)
     rows = d_out.shape[0]
     heads = later.shape[0]
     blocks = rows // BLK
@@ -307,6 +316,8 @@
             d_ka = rk * d_k - ka * (rk * rk * rk * jnp.sum(d_k * ka, axis=1, keepdims=True))
             d_act = jnp.concatenate([d_qa, d_ka, d_val], axis=1)
             d_pre_o[here, pl.ds(h * CONVW, CONVW)] = d_act * (sg * (1.0 + cv * (1.0 - sg)))
+            if h == 1:
+                spread.relays(c)
     d_g, d_beta = cols_s[:, :heads], cols_s[:, heads : 2 * heads]
     d_bias = -d_g * jnp.exp(dlog[...]) * sigmoid(pre)
     d_rate_o[:, :heads] = d_bias
@@ -328,6 +339,10 @@
         d_tail_o[:, dst] = dpad[rows - PAD :, :]
         d_proj_o[:, src] = dpad[PAD:, :].astype(BF16)
         d_proj_o[:, pl.ds(h * MIXW + CONVW, DV)] = d_gate[:, pl.ds(h * DV, DV)]
+    for i, o in ((0, s_down_o), (1, s_out_o)):
+        for b in FAR:
+            o[b] = spread.total(i, b).astype(BF16)
+    spread.end()
 
 
 def call(kernel, outs, scratch, limit, *args, flops=2_000_000_000, nbytes=16_000_000):
@@ -381,30 +396,51 @@
     return [dev(0, True)] + [dev(d) for d in range(1, CHIPS)]
 
 
-def gather_over_head(x, o, ssem, rsem, lsem):
+def head_rows(o, rows, step, flip=False):
+    owner = head_place()[3](step, flip)[1]
+    return o.at[pl.ds(pl.multiple_of(owner * rows, rows), rows)]
+
+
+def gather_start(x, o, ssem, rsem, lsem):
     rows = x.shape[0]
-    me, chip, core, dev = head_place()
-
-    def at(step, flip=False):
-        return o.at[pl.ds(pl.multiple_of(dev(step, flip)[1] * rows, rows), rows)]
-
-    own = pltpu.make_async_copy(x, at(0), lsem)
-    own.start()
-    out = [cp(x, at(0), ssem.at[d], rsem.at[d], dev(d)) for d in (1, 3, 2)]
-    out.append(cp(x, at(0), ssem.at[0], rsem.at[0], dev(0, True)))
+    dev = head_place()[3]
+    pltpu.make_async_copy(x, head_rows(o, rows, 0), lsem).start()
+    out = [cp(x, head_rows(o, rows, 0), ssem.at[d], rsem.at[d], dev(d)) for d in (2, 1, 3)]
+    out.append(cp(x, head_rows(o, rows, 0), ssem.at[0], rsem.at[0], dev(0, True)))
     for s in out:
         s.start()
+    return out
+
+
+def gather_forward(x, o, ssem, rsem):
+    rows = x.shape[0]
+    dev = head_place()[3]
+    out = []
     for d in (1, 3, 2):
-        cp(x, at(CHIPS - d), ssem.at[d], rsem.at[d], dev(d)).wait_recv()
-        fwd = cp(at(CHIPS - d), at(CHIPS - d), ssem.at[CHIPS + d], rsem.at[CHIPS + d], dev(0, True))
+        there = head_rows(o, rows, CHIPS - d)
+        cp(x, there, ssem.at[d], rsem.at[d], dev(d)).wait_recv()
+        fwd = cp(there, there, ssem.at[CHIPS + d], rsem.at[CHIPS + d], dev(0, True))
         fwd.start()
         out.append(fwd)
-    own.wait()
-    cp(x, at(0, True), ssem.at[0], rsem.at[0], dev(0, True)).wait_recv()
+    return out
+
+
+def gather_end(x, o, ssem, rsem, lsem, sent):
+    rows = x.shape[0]
+    dev = head_place()[3]
+    pltpu.make_async_copy(x, head_rows(o, rows, 0), lsem).wait()
+    cp(x, head_rows(o, rows, 0, True), ssem.at[0], rsem.at[0], dev(0, True)).wait_recv()
     for d in range(1, CHIPS):
-        cp(x, at(CHIPS - d, True), ssem.at[CHIPS + d], rsem.at[CHIPS + d], dev(0, True)).wait_recv()
-    for s in out:
+        there = head_rows(o, rows, CHIPS - d, True)
+        cp(x, there, ssem.at[CHIPS + d], rsem.at[CHIPS + d], dev(0, True)).wait_recv()
+    for s in sent:
         s.wait_send()
+
+
+def gather_over_head(x, o, ssem, rsem, lsem):
+    sent = gather_start(x, o, ssem, rsem, lsem)
+    sent += gather_forward(x, o, ssem, rsem)
+    gather_end(x, o, ssem, rsem, lsem, sent)
 
 
 def reduce_over_head(x, total, pair, got, mid, ssem, rsem):
@@ -457,22 +493,65 @@
     gather_over_head(block, all_o, s2, r2, ls)
 
 
-def mid_backward(x, hidden, cot, gain, all_o, d_hidden_o, d_gain_o, total, block, pair, got, mid, s1, r1, s2, r2, ls):
-    greet(head_peers())
-    reduce_over_head(x, total, pair, got, mid, s1, r1)
-    d_norm, d_gain = norm_back(hidden[...], gain[...], total[...])
+def mid_backward(
+    x, hidden, cot, gain, d_gu, n2, all_o, d_hidden_o, d_gain_o, grad_o,
+    total, block, pair, got, mid, g, relay, seqs_got, part, last_got, s1, r1, s2, r2, ls, s3, r3, s4, r4
+):
+    greet(head_peers() + side_peers())
+    one = pair_sends(x, pair, s1, r1, FAR)
+    spread = Spread(
+        lambda i, owner: g.at[owner, i], lambda i, b: relay.at[i, b], lambda i, s, b: seqs_got.at[i, s, b], s3, r3
+    )
+    settle = Settle(lambda i, b: last_got.at[i, b], s4, r4)
+    dev = seq_place()[3]
+    hid = g.shape[2]
+
+    def make(place):
+        owner = dev(*place)[0]
+        cols = n2[:, pl.ds(pl.multiple_of(owner * LANES, LANES), LANES)]
+        out = dot(d_gu[...], cols).astype(BF16)
+        g[owner, 0] = out[:hid]
+        g[owner, 1] = out[hid:]
+        spread.ready(*place)
+
+    for place in PLACES[:2]:
+        make(place)
+    two = chip_sends(x, one, total, pair, got, mid, s1, r1, FAR)
+    for place in PLACES[2:]:
+        make(place)
+    spread.relays(0)
+    d_norm, d_gain = norm_back(hidden[...], gain[...], chip_sum(two, total, got))
     d_hidden = cot[...].astype(F32) + d_norm
     d_hidden_o[...] = d_hidden
     d_gain_o[...] = d_gain
     block[...] = d_hidden.astype(BF16)
-    gather_over_head(block, all_o, s2, r2, ls)
-
-
-def reach(kernel, outs, scratch, cid, limit, *args, anywhere=(), nbytes=12_000_000):
+    ahead = gather_start(block, all_o, s2, r2, ls)
+    spread.relays(1)
+    ahead += gather_forward(block, all_o, s2, r2)
+    for b in FAR:
+        for i in range(2):
+            both = spread.total(i, b)
+            if b:
+                part[i, b] = both.astype(BF16)
+                settle.send(part.at[i, b], i, b)
+            else:
+                grad_o[i] = both
+    gather_end(block, all_o, s2, r2, ls, ahead)
+    for i in range(2):
+        grad_o[i] = grad_o[i] + settle.others(i)
+    spread.end()
+    settle.end()
+    for s in list(one.values()) + list(two.values()):
+        s.wait_send()
+
+
+def reach(kernel, outs, scratch, cid, limit, *args, anywhere=(), scalars=(), nbytes=12_000_000):
     return pl.pallas_call(
         kernel,
         out_shape=outs,
-        in_specs=[pl.BlockSpec(memory_space=pl.ANY) if i in anywhere else VMEM for i in range(len(args))],
+        in_specs=[
+            pl.BlockSpec(memory_space=pl.ANY) if i in anywhere else SMEM if i in scalars else VMEM for i in range(len(args))
+        ],
         out_specs=[VMEM for _ in outs],
         scratch_shapes=scratch,
         compiler_params=pltpu.CompilerParams(
@@ -513,14 +592,116 @@
     return [dev(0, d) for d in range(1, SIDE)] + [dev(d, 0) for d in range(1, SIDE)]
 
 
-def share(src, got, place, to, ssem, rsem):
+FAR = (2, 1, 3, 0)
+FIRST, OTHER = (2, 1), (3, 0)
+PLACES = (
+    (2, 2), (2, 1), (1, 2), (2, 3), (3, 2), (2, 0), (0, 2), (1, 3), (3, 1), (1, 0), (0, 3), (3, 3), (1, 1), (3, 0), (0, 1),
+    (0, 0),
+)
+
+
+class Spread:
+    def __init__(self, piece, relay, got, ssem, rsem):
+        self.piece, self.relay, self.got, self.ssem, self.rsem = piece, relay, got, ssem, rsem
+        self.dev = seq_place()[3]
+        self.sent = []
+
+    def way(self, i, a, b):
+        return self.dev(b, a) if i == 0 else self.dev(a, b)
+
+    def copy(self, i, a, b, owner):
+        k = (i * SIDE + a) * SIDE + b
+        if a == 2:
+            dst, step = self.relay(i, b), 1 if b in FIRST else 3
+        else:
+            dst, step = self.got(i, 0 if a == 1 else 1, b), a
+        return cp(self.piece(i, owner), dst, self.ssem.at[k], self.rsem.at[k], self.way(i, step, 0))
+
+    def send(self, i, a, b, owner):
+        s = self.copy(i, a, b, owner)
+        s.start()
+        self.sent.append(s)
+
+    def late(self, a, b):
+        return a == 1 and b in FIRST or a == 3 and b in OTHER
+
+    def ready(self, dz, dy):
+        owner = self.dev(dz, dy)[0]
+        for i in range(2):
+            a, b = (dy, dz) if i == 0 else (dz, dy)
+            if a and not self.late(a, b):
+                self.send(i, a, b, owner)
+
+    def relays(self, part=None):
+        for n, b in enumerate(FAR):
+            if part is not None and n // 2 != part:
+                continue
+            for i in range(2):
+                a = 1 if b in FIRST else 3
+                owner = self.way(i, a, b)[0]
+                self.copy(i, 2, b, owner).wait_recv()
+                both = self.piece(i, owner)[...].astype(F32) + self.relay(i, b)[...].astype(F32)
+                self.relay(i, b)[...] = both.astype(BF16)
+                k = (i * SIDE + a) * SIDE + b
+                s = cp(
+                    self.relay(i, b), self.got(i, 0 if a == 1 else 1, b), self.ssem.at[k], self.rsem.at[k],
+                    self.way(i, a, 0),
+                )
+                s.start()
+                self.sent.append(s)
+
+    def total(self, i, b):
+        owner = self.way(i, 0, b)[0]
+        for a in (1, 3):
+            self.copy(i, a, b, owner).wait_recv()
+        return self.piece(i, owner)[...].astype(F32) + (
+            self.got(i, 0, b)[...].astype(F32) + self.got(i, 1, b)[...].astype(F32)
+        )
+
+    def end(self):
+        for s in self.sent:
+            s.wait_send()
+
+
+class Settle:
+    def __init__(self, got, ssem, rsem):
+        self.got, self.ssem, self.rsem = got, ssem, rsem
+        self.dev = seq_place()[3]
+        self.sent = {}
+
+    def send(self, src, i, b):
+        k = i * SIDE + b
+        dev = self.dev(b, 0) if i == 0 else self.dev(0, b)
+        self.sent[i, b] = cp(src, self.got(i, b), self.ssem.at[k], self.rsem.at[k], dev)
+        self.sent[i, b].start()
+
+    def others(self, i):
+        for b in (1, 3, 2):
+            self.sent[i, b].wait_recv()
+        return (self.got(i, 1)[...].astype(F32) + self.got(i, 3)[...].astype(F32)) + self.got(i, 2)[...].astype(F32)
+
+    def end(self):
+        for s in self.sent.values():
+            s.wait_send()
+
+
+def share_start(src, got, place, to, ssem, rsem):
     got[place] = src[...]
-    out = [cp(src, got.at[place], ssem.at[d], rsem.at[d], to(d)) for d in range(1, SIDE)]
+    out = [cp(src, got.at[place], ssem.at[d], rsem.at[d], to(d)) for d in (2, 1, 3)]
     for s in out:
         s.start()
-    for d in range(1, SIDE):
-        back = lax.rem(place + SIDE - d, SIDE)
-        cp(src, got.at[back], ssem.at[d], rsem.at[d], to(d)).wait_recv()
+
+    def wait():
+        for d in (1, 3, 2):
+            back = lax.rem(place + SIDE - d, SIDE)
+            cp(src, got.at[back], ssem.at[d], rsem.at[d], to(d)).wait_recv()
+
+    return out, wait
+
+
+def share(src, got, place, to, ssem, rsem):
+    out, wait = share_start(src, got, place, to, ssem, rsem)
+    wait()
     return out
 
 
@@ -564,11 +745,22 @@
         s.wait_send()
 
 
-def states_backward(inc, ga, ta, later_o, got1, tot, got2, s1, r1, s2, r2):
+def states_backward(inc, ga, ta, middle, cot, gated_t, d_mixed, later_o, g_down_o, g_out_o, got1, tot, got2, s1, r1, s2, r2):
     me, z, y, dev = seq_place()
     heads = inc.shape[0]
+    seqs = g_down_o.shape[0]
+
+    def blocks(o, left, right, part):
+        for j in range(part * seqs // 4, (part + 1) * seqs // 4):
+            if j % 2 == 0:
+                both = dot(left[...], right[:, j * LANES : (j + 2) * LANES]).astype(BF16)
+                o[j], o[j + 1] = both[:, :LANES], both[:, LANES:]
+
     greet(side_peers())
-    out = share(inc, got1, y, lambda d: dev(0, d), s1, r1)
+    out, wait = share_start(inc, got1, y, lambda d: dev(0, d), s1, r1)
+    blocks(g_down_o, middle, cot, 0)
+    blocks(g_down_o, middle, cot, 1)
+    wait()
     after = []
     for h in range(heads):
         whole = add_low(dot(unit_top(), ga[SIDE - 1, h], "nt"), got1[SIDE - 1, h].astype(F32))
@@ -579,7 +771,13 @@
                 suffix = jnp.where(y < j, whole, suffix)
         tot[h] = whole[DK:].astype(BF16)
         after.append(suffix)
-    out += share(tot, got2, z, lambda d: dev(d, 0), s2, r2)
+    more, wait = share_start(tot, got2, z, lambda d: dev(d, 0), s2, r2)
+    out += more
+    blocks(g_down_o, middle, cot, 2)
+    blocks(g_down_o, middle, cot, 3)
+    for part in range(4):
+        blocks(g_out_o, gated_t, d_mixed, part)
+    wait()
     for h in range(heads):
         held = jnp.zeros((DV, DK), F32)
         for j in range(SIDE - 1, 0, -1):
@@ -624,14 +822,12 @@
     return total[...] + ((got[1].astype(F32) + got[3].astype(F32)) + got[2].astype(F32))
 
 
-FAR = (2, 1, 3, 0)
-
-
 def finish(
     dproj, normed, w, d_rate, rate_w, d_tail, d_edge, feed, hidden, tokens, d_hidden, gain, convs, decay, g_feed, g_head,
-    layer_o, d_tokens_o, g_mixer_o, gains_o, convs_o, rate_o,
-    dp, wv, edge, g, got1, mid, got2, dn, ta, pa, ga, ma, tb, pb, gb, mb, gains, gbuf, sbuf, rbuf,
-    es, er, ls, s1, r1, sa, ra, sb, rb, sg, rg, ss, rs
+    s_down, s_out,
+    layer_o, d_tokens_o, g_mixer_o, gains_o, convs_o, rate_o, g_down_o, g_out_o,
+    dp, wv, edge, g, relay, got1, mid, got2, dn, ta, pa, ga, ma, tb, pb, gb, mb, gains, gbuf, sbuf, rbuf, got_d, got_o,
+    es, er, ls, s1, r1, s2, r2, sa, ra, sb, rb, sg, rg, ss, rs, s5, r5
 ):
     me, z, y, dev = seq_place()
     head = lax.axis_index("head")
@@ -656,23 +852,23 @@
     for i in range(2):
         dp[rows - 2 * PAD :, pl.ds(i * half, wide)] = tail[:, i * wide : (i + 1) * wide]
 
-    ways = (lambda a, b: dev(b, a), lambda a, b: dev(a, b))
-
-    def piece(i, owner):
-        return g.at[i, owner]
-
-    first, second = {}, {}
-    places = [(dz, dy) for dz in FAR for dy in FAR]
-    for dz, dy in places:
-        owner = dev(dz, dy)[0]
+    sums = (s_down, s_out)
+    settle = Settle(lambda i, b: (got_d, got_o)[i].at[b], s5, r5)
+    for b in (2, 1, 3):
+        for i in range(2):
+            settle.send(sums[i].at[b], i, b)
+
+    spread = Spread(
+        lambda i, owner: g.at[i, owner], lambda i, b: relay.at[i, b], lambda i, s, b: got1.at[i, s, b], s1, r1
+    )
+    settle_two = Settle(lambda i, b: got2.at[i, b], s2, r2)
+    for place in PLACES:
+        owner = dev(*place)[0]
         left = normed[:, pl.ds(pl.multiple_of(owner * part, part), part)]
+        both = dot(left, dp[...], "tn").astype(BF16)
         for i in range(2):
-            a, b = (dy, dz) if i == 0 else (dz, dy)
-            g[i, owner] = dot(left, dp[:, i * half : (i + 1) * half], "tn").astype(BF16)
-            if a:
-                k = (i * SIDE + a) * SIDE + b
-                first[i, a, b] = cp(piece(i, owner), got1.at[i, a, b], s1.at[k], r1.at[k], ways[i](a, 0))
-                first[i, a, b].start()
+            g[i, owner] = both[:, i * half : (i + 1) * half]
+        spread.ready(*place)
     feed_two = chip_sends(feed, feed_one, ta, pa, ga, ma, sa, ra, FAR)
     rates_t = dot(d_rate[:, :PAD], normed[...], "tn")
 
@@ -686,6 +882,7 @@
         dn[here, :] = (dot(dp[here, :], wv[...], "nt") + dot(d_rate[here, :], rate_w[...], "nt")).astype(BF16)
         dn_one.update(pair_sends(dn, pb, sb, rb, (d,)))
     dn_two = chip_sends(dn, dn_one, tb, pb, gb, mb, sb, rb, FAR)
+    spread.relays()
     layer_o[...] = (hidden[...] + chip_sum(feed_two, ta, ga)).astype(BF16)
     d_norm, d_gain = norm_back(tokens[...].astype(F32), gain[...], chip_sum(dn_two, tb, gb))
     d_tokens_o[...] = d_hidden[...] + d_norm
@@ -732,19 +929,15 @@
         s.start()
         s_out.append(s)
 
+    for i, o in ((0, g_down_o), (1, g_out_o)):
+        o[...] = sums[i][0].astype(F32) + settle.others(i)
+
     for b in FAR:
         for i in range(2):
-            for a in (1, 3, 2):
-                first[i, a, b].wait_recv()
-            mine = g[i, ways[i](0, b)[0]].astype(F32)
-            both = mine + (
-                (got1[i, 1, b].astype(F32) + got1[i, 3, b].astype(F32)) + got1[i, 2, b].astype(F32)
-            )
+            both = spread.total(i, b)
             if b:
                 mid[i, b] = both.astype(BF16)
-                k = 2 * SIDE * SIDE + i * SIDE + b
-                second[i, b] = cp(mid.at[i, b], got2.at[i, b], s1.at[k], r1.at[k], ways[i](0, b))
-                second[i, b].start()
+                settle_two.send(mid.at[i, b], i, b)
             else:
                 g_mixer_o[i] = both
     for d in range(1, seqs):
@@ -756,24 +949,14 @@
     convs_o[...] = total[ng : ng + nc + PAD]
     rate_o[...] = total[ng + nc + PAD :]
     for i in range(2):
-        for b in (1, 3, 2):
-            second[i, b].wait_recv()
-        g_mixer_o[i] = g_mixer_o[i] + (
-            (got2[i, 1].astype(F32) + got2[i, 3].astype(F32)) + got2[i, 2].astype(F32)
-        )
-    done = list(first.values()) + list(second.values()) + g_out + s_out + [back]
+        g_mixer_o[i] = g_mixer_o[i] + settle_two.others(i)
+    spread.end()
+    settle.end()
+    settle_two.end()
+    done = g_out + s_out + [back]
     done += list(feed_one.values()) + list(feed_two.values()) + list(dn_one.values()) + list(dn_two.values())
     for s in done:
         s.wait_send()
-
-
-def weight_grads(d_gu, middle, gated, n2, cot, d_mixed, o):
-    a, b = d_gu.shape[0], middle.shape[0]
-    for lo, left, right in ((0, d_gu, n2), (a, middle, cot), (a + b, gated, d_mixed)):
-        out = dot(left[...], right[...]).astype(BF16)
-        n = left.shape[0]
-        o[0, lo : lo + n] = out[:, :LANES]
-        o[1, lo : lo + n] = out[:, LANES:]
 
 
 def passed_along(shard, axis, by):
@@ -858,34 +1041,25 @@
     middle = (gate * s * up).astype(BF16)
     d_gate_up = jnp.concatenate([d_middle * up * (s * (1.0 + gate * (1.0 - s))), d_middle * gate * s]).astype(BF16)
     d_two = lax.dot_general(d_gate_up, gu_t, by_first, preferred_element_type=F32).astype(BF16)
-    d_mixed, d_hidden, g_feed_gain = reach(
+    part, half, n_head = D // seq, MIXW, lax.axis_size("head")
+    d_mixed, d_hidden, g_feed_gain, grads = reach(
         mid_backward,
-        [sds((rows, D), BF16), sds((own, D)), sds((1, D))],
-        [pltpu.VMEM((own, D), F32), pltpu.VMEM((own, D), BF16)] + reduce_scratch(own, D) + gather_scratch(),
-        3, 48, d_two, hidden, cotangent, feed_row,
-    )
-    wide = 3 * hid + heads * DV
-    right = pl.BlockSpec((rows, 2 * LANES), lambda j: (0, j))
-
-    def whole(a):
-        return pl.BlockSpec(a.shape, lambda j: (0, 0))
-
+        [sds((rows, D), BF16), sds((own, D)), sds((1, D)), sds((2, hid, LANES))],
+        [pltpu.VMEM((own, D), F32), pltpu.VMEM((own, D), BF16)]
+        + [pltpu.VMEM((CHIPS, own, D), BF16) for _ in range(3)]
+        + [
+            pltpu.VMEM((seq, 2, hid, LANES), BF16), pltpu.VMEM((2, SIDE, hid, LANES), BF16),
+            pltpu.VMEM((2, 2, SIDE, hid, LANES), BF16), pltpu.VMEM((2, SIDE, hid, LANES), BF16),
+            pltpu.VMEM((2, SIDE, hid, LANES), BF16), sems(2 * CHIPS), sems(2 * CHIPS),
+        ]
+        + gather_scratch()
+        + [sems(2 * SIDE * SIDE), sems(2 * SIDE * SIDE), sems(2 * SIDE), sems(2 * SIDE)],
+        3, 60, d_two, hidden, cotangent, feed_row, d_gate_up, gathered_two, nbytes=30_000_000,
+    )
+    grad_gate_up = grads.transpose(2, 0, 1)
+    d_mixed, middle = lax.optimization_barrier((d_mixed, middle))
+    feed = lax.dot_general(middle, down_weight, by_first, preferred_element_type=F32).astype(BF16)
     gated_t = gated.T
-    grads = pl.pallas_call(
-        weight_grads,
-        grid=(seq // 2,),
-        out_shape=sds((seq, wide, LANES), BF16),
-        in_specs=[whole(d_gate_up), whole(middle), whole(gated_t), right, right, right],
-        out_specs=pl.BlockSpec((2, wide, LANES), lambda j: (j, 0, 0)),
-        compiler_params=pltpu.CompilerParams(vmem_limit_bytes=48 << 20),
-        cost_estimate=pl.CostEstimate(flops=2 * wide * rows * D, bytes_accessed=24_000_000, transcendentals=0),
-    )(d_gate_up, middle, gated_t, gathered_two, cot_rows, d_mixed)
-    d_mixed, grads, middle = lax.optimization_barrier((d_mixed, grads, middle))
-    feed = lax.dot_general(middle, down_weight, by_first, preferred_element_type=F32).astype(BF16)
-    grads = lax.psum_scatter(grads.reshape(seq * wide, LANES), "seq", scatter_dimension=0, tiled=True).astype(F32)
-    grad_gate_up = grads[: 2 * hid].reshape(2, hid, LANES).transpose(2, 0, 1)
-    grad_down = grads[2 * hid : 3 * hid]
-    grad_output = grads[3 * hid :].reshape(heads, DV, LANES)
     d_gated = jnp.einsum("td,vd->tv", d_mixed, out_flat, preferred_element_type=F32)
     d_out, d_gate, g_head_gain, y, inc = call(
         bwd_head,
@@ -895,60 +1069,65 @@
         ],
         [], 48, d_gated, head_out, projected, gain, qe, step,
     )
-    (later,) = reach(
+    later, g_down, g_out = reach(
         states_backward,
-        [sds((heads, DV, DK))],
+        [sds((heads, DV, DK)), sds((seq, hid, LANES), BF16), sds((seq, heads * DV, LANES), BF16)],
         [
             pltpu.VMEM((SIDE, heads, DV, DK), BF16), pltpu.VMEM((heads, DV, DK), BF16),
             pltpu.VMEM((SIDE, heads, DV, DK), BF16), sems(SIDE), sems(SIDE), sems(SIDE), sems(SIDE),
         ],
-        4, 40, inc, ga, ta,
-    )
-    d_projected, d_tail, d_edge, d_rate, d_convw, d_decay = call(
+        4, 48, inc, ga, ta, middle, cot_rows, gated_t, d_mixed,
+    )
+    d_projected, d_tail, d_edge, d_rate, d_convw, d_decay, s_down, s_out = reach(
         bwd_mix,
         [
             sds((rows, heads * MIXW), BF16), sds((2 * PAD, heads * CONVW)), sds((PAD, heads * CONVW)),
             sds((rows, 2 * heads)), sds((KCONV, heads * CONVW)), sds((1, 2 * heads)),
+            sds((SIDE, hid, LANES), BF16), sds((SIDE, heads * DV, LANES), BF16),
         ],
         [
             pltpu.VMEM((PAD + rows, CONVW), F32), pltpu.VMEM((PAD + rows, CONVW), F32),
             pltpu.VMEM((units, DV, DK), F32), pltpu.VMEM((rows, DK), F32), pltpu.VMEM((rows, heads * CONVW), F32),
+            pltpu.VMEM((SIDE, hid, LANES), BF16), pltpu.VMEM((SIDE, heads * DV, LANES), BF16),
+            pltpu.VMEM((2, SIDE, hid, LANES), BF16), pltpu.VMEM((2, SIDE, heads * DV, LANES), BF16),
+            sems(2 * SIDE * SIDE), sems(2 * SIDE * SIDE),
         ],
-        60, info, later, conv, dec, inv, wu, states, step, y, d_out, d_gate, rate_proj, projected, halo, convw,
-        dlog, dbias,
-    )
-    part, half, n_head = D // seq, MIXW, lax.axis_size("head")
+        6, 62, info, later, conv, dec, inv, wu, states, step, y, d_out, d_gate, rate_proj, projected, halo, convw,
+        dlog, dbias, g_down, g_out, scalars=(0,), nbytes=30_000_000,
+    )
     d_rate_low = jnp.pad(d_rate.astype(BF16), ((0, 0), (0, LANES - 2 * heads)))
     rate_pad = jnp.pad(rate_weight.reshape(D, 2 * heads), ((0, 0), (0, LANES - 2 * heads)))
     d_decay = jnp.pad(d_decay, ((0, 0), (0, LANES - 2 * heads)))
     n_gain, n_conv = 40, KCONV * heads * CONVW // LANES + PAD
     small = n_gain + n_conv + PAD
-    layer_out, grad_tokens, grad_mixer, gains, convs, rate_own = reach(
+    layer_out, grad_tokens, grad_mixer, gains, convs, rate_own, grad_down, grad_output = reach(
         finish,
         [
             sds((own, D), BF16), sds((own, D)), sds((2, part, half)), sds((n_gain, LANES)), sds((n_conv, LANES)),
-            sds((PAD, LANES)),
+            sds((PAD, LANES)), sds((hid, LANES)), sds((heads * DV, LANES)),
         ],
         [
             pltpu.VMEM((rows, heads * MIXW), BF16), pltpu.VMEM((D, heads * MIXW), BF16),
             pltpu.VMEM((PAD, heads * CONVW), F32), pltpu.VMEM((2, seq, part, half), BF16),
-            pltpu.VMEM((2, SIDE, SIDE, part, half), BF16), pltpu.VMEM((2, SIDE, part, half), BF16),
-            pltpu.VMEM((2, SIDE, part, half), BF16), pltpu.VMEM((rows, D), BF16),
+            pltpu.VMEM((2, SIDE, part, half), BF16), pltpu.VMEM((2, 2, SIDE, part, half), BF16),
+            pltpu.VMEM((2, SIDE, part, half), BF16), pltpu.VMEM((2, SIDE, part, half), BF16), pltpu.VMEM((rows, D), BF16),
         ]
         + 2 * ([pltpu.VMEM((own, D), F32)] + [pltpu.VMEM((CHIPS, own, D), BF16) for _ in range(3)])
         + [
             pltpu.VMEM((n_gain, LANES), F32), pltpu.VMEM((n_head, n_gain, LANES), F32),
             pltpu.VMEM((seq, small, LANES), F32), pltpu.VMEM((seq, small, LANES), F32),
+            pltpu.VMEM((SIDE, hid, LANES), BF16), pltpu.VMEM((SIDE, heads * DV, LANES), BF16),
             pltpu.SemaphoreType.DMA, pltpu.SemaphoreType.DMA, sems(2),
-            sems(2 * SIDE * SIDE + 2 * SIDE), sems(2 * SIDE * SIDE + 2 * SIDE),
+            sems(2 * SIDE * SIDE), sems(2 * SIDE * SIDE), sems(2 * SIDE), sems(2 * SIDE),
             sems(2 * CHIPS), sems(2 * CHIPS), sems(2 * CHIPS), sems(2 * CHIPS),
-            sems(n_head), sems(n_head), sems(seq), sems(seq),
+            sems(n_head), sems(n_head), sems(seq), sems(seq), sems(2 * SIDE), sems(2 * SIDE),
         ],
         5, 62, d_projected, gathered, mixer_flat, d_rate_low, rate_pad, d_tail, d_edge, feed, hidden, tokens,
-        d_hidden, mixer_gain.reshape(1, D), d_convw, d_decay, g_feed_gain, g_head_gain,
+        d_hidden, mixer_gain.reshape(1, D), d_convw, d_decay, g_feed_gain, g_head_gain, s_down, s_out,
         anywhere=(0, 2), nbytes=40_000_000,
     )
     grad_mixer = grad_mixer.transpose(1, 0, 2)
+    grad_output = grad_output.reshape(heads, DV, LANES)
     gains, convs = gains.reshape(-1), convs.reshape(-1)
     grad_mixer_gain, grad_feed_gain, grad_head_gain = gains[:D], gains[D : 2 * D], gains[2 * D : 2 * D + DV]
     n = KCONV * heads * CONVW

time: 387 us -> 392 us (1.013)
  Pallas kernels: 257 us -> 266 us
  local copies, waits for them, and re-layouts: 43.6 us -> 38.7 us
    pallas_call x5 -> x6, Pallas kernels: 197 us -> 234 us  [reach(): pl.pallas_call(kernel, out_shape=outs, in_specs=[pl.BlockSpec(memory_spac...]
    pallas_call x4 -> x3, Pallas kernels: 48.7 us -> 31.9 us  [call(): pl.pallas_call(kernel, out_shape=outs, in_specs=[spec(a) for a in args],...]
    pallas_call x1 -> x0, Pallas kernels: 11.3 us -> none  [local(): pl.pallas_call(weight_grads, grid=(seq // 2,), out_shape=sds((seq, wide,...]
    slice x3 -> x0, local copies, waits for them, and re-layouts: 5.18 us -> none  [the longest x1 1.88 us: local(): grad_gate_up = grads[:2 * hid].reshape(2, hid, LANES).transpose(2, 0, 1)]
    unnamed x69 -> x68, local copies, waits for them, and re-layouts: 25.9 us -> 27.9 us
  transfers between devices with their start and end apart: 4 -> 3, of which waited for: 1 -> 1; matrix products, arithmetic and copies ran while one was open for 13% -> 7% of each run, Pallas kernels for 55% -> 23%
where the time goes in v4:
time: 392 us; the launch traced here: 389 us
  Pallas kernels  266 us (68%)
  local copies, waits for them, and re-layouts  38.7 us (10%)
  matrix products  37.8 us (10%)
  waiting for transfers between devices  22 us (6%)
  between operations  14.9 us (4%)
  other arithmetic  6.27 us (2%)
    pallas_call x6, Pallas kernels, reach(): pl.pallas_call(kernel, out_shape=outs, in_specs=[pl.BlockSpec(memory_spac...  234 us
    pallas_call x3, Pallas kernels, call(): pl.pallas_call(kernel, out_shape=outs, in_specs=[spec(a) for a in args],...  31.9 us
    unnamed x68, local copies, waits for them, and re-layouts  27.9 us
    all_gather x1, waiting for transfers between devices, local(): gathered = lax.all_gather(normed, 'head', axis=0, tiled=True)  22 us
  transfers between devices with their start and end apart: 3, of which 1 were waited for; matrix products, arithmetic and copies ran while one was open for 7% of the time, Pallas kernels for 23%

profile of v4, /device:TPU:1, one launch (start us, length us, event | category | flops | bytes accessed | tf_op | source)
XLA Modules:
  0.0 388.6 jit_solution(4661956065376429559)
XLA Ops:
  8.3 1.8 fusion.4
  10.2 6.8 %copy.36 = bf16[256,8,2,768]{3,1,2,0:T(8,128)(2,1)} copy(bf16[256,8,2,768]{3,2,1,0:T(2,128)(2,1)} %bitcast.63) | data formatting | bytes 12582912
  17.1 22.0 %all-gather.3.cloned.1.call-done.normed = bf16[512,2048]{1,0:T(8,128)(2,1)} async-done(((bf16[64,2048]{1,0:T(8,128)(2,1)}), bf16[512,2048]{1,0:T(8,128)(2,1)}) %all-gather.3.cloned.1.call-update) | async-done | bytes 2097168 | tf_op jit(solution)/shard_map/all_gather | solution.py:978
  41.6 6.9 %fusion.6.proj = f32[512,1536]{1,0:T(8,128)S(1)} fusion(bf16[512,2048]{1,0:T(8,128)(2,1)} %all-gather.3.cloned.1.call-done.normed, bf16[2048,1536]{1,0:T(8,128)(2,1)} %bitcast.61), kind=kOutput, calls=%fused_computation.24 | convolution fusion | flops 3221225472 | bytes 11534336 | tf_op jit(solution)/shard_map/dot_general | solution.py:988
  48.5 1.6 copy-done.20
  50.1 3.3 collective-permute-start
  55.6 25.6 %shard_map.237 = (f32[512,1024]{1,0:T(8,128)}, f32[4,256,256]{2,1,0:T(8,128)}, bf16[4,256,256]{2,1,0:T(8,128)(2,1)}, f32[4,256,384]{2,1,0:T(8,128)}, f32[512,256...) custom-call(s32[6]{0:T(128)} %pad_add_fusion.info, ...), custom_call_target="tpu_custom_call" | custom-call | flops 2000000000 | bytes 16000000 | tf_op jit(solution)/shard_map/pallas_call | solution.py:352
  82.1 28.0 %shard_map.238 = (f32[2,256,128]{2,1,0:T(8,128)S(1)}, bf16[4,2,128,128]{3,2,1,0:T(8,128)(2,1)S(1)}, bf16[4,2,128,128]{3,2,1,0:T(8,128)(2,1)S(1)}) custom-call(bf16[2,384,128]{2,1,0:T(8,128)(2,1)S(1)} %copy-done.11), custom_call_target="tpu_custom_call" | custom-call | bytes 12000000 | tf_op jit(solution)/shard_map/pallas_call | solution.py:549
  112.3 1.2 copy-done.19
  113.5 2.8 shard_map.239
  118.3 2.9 convolution_convert_fusion.1.x
  121.3 33.5 %shard_map.240 = (bf16[512,2048]{1,0:T(8,128)(2,1)S(1)}, f32[64,2048]{1,0:T(8,128)S(1)}) custom-call(bf16[512,2048]{1,0:T(8,128)(2,1)S(1)} %convolution_convert_fusion.1.x, bf16[64,2048]{1,0:T(8,128)(2,1)S(1)} %copy-done, f32[1,2048]{1,0:T(1,128)S(1)} %bitcast.58), custom_call_target="tpu_custom_call" | custom-call | bytes 12000000 | tf_op jit(solution)/shard_map/pallas_call | solution.py:549
  155.5 1.4 copy-done.3
  157.0 7.4 %convolution_bitcast_fusion = f32[1376,512]{1,0:T(8,128)} fusion(bf16[512,2048]{1,0:T(8,128)(2,1)S(1)} %get-tuple-element.71.n2, bf16[1376,2048]{1,0:T(8,128)(2,1)} %bitcast.79), kind=kOutput, calls=%fused_computation | convolution fusion | flops 2885681152 | bytes 10551296 | tf_op jit(solution)/shard_map/dot_general | solution.py:1038
  164.3 5.5 %multiply_convert_fusion.2 = (bf16[688,512]{1,0:T(8,128)(2,1)S(1)}, bf16[688,512]{1,0:T(8,128)(2,1)S(1)}, bf16[688,512]{1,0:T(8,128)(2,1)S(1)}) fusion(f32[1376,512]{1,0:T(8,128)} %convolution_bitcast_fusion, bf16[512,2048]{1,0:T(8,128)(2,1)} %all-gather.5.cloned.1.call-done.cot, bf16[688,2048]{1,0:T(8,128)(2,1)} %param.25), kind=kOutput, calls=%fused_computation.10 | convolution fusion | flops 1448476672 | bytes 9846784 | tf_op jit(solution)/shard_map/dot_general | solution.py:1037
  169.8 1.2 pad_maximum_fusion.d_gu
  171.0 7.6 %convolution_convert_fusion.2.x = bf16[512,2048]{1,0:T(8,128)(2,1)} fusion(bf16[1376,2048]{1,0:T(8,128)(2,1)} %bitcast.80, bf16[688,512]{1,0:T(8,128)(2,1)S(1)} %get-tuple-element.138, bf16[688,512]{1,0:T(8,128)(2,1)S(1)} %get-tuple-element.137), kind=kOutput, calls=%fused_computation.3 | convolution fusion | flops 2889547776 | bytes 9142272 | tf_op jit(solution)/shard_map/dot_general | solution.py:1043
  178.6 47.0 %shard_map.241 = (bf16[512,2048]{1,0:T(8,128)(2,1)}, f32[64,2048]{1,0:T(8,128)}, f32[1,2048]{1,0:T(1,128)}, f32[2,688,128]{2,1,0:T(8,128)}) custom-call(bf16[512,2048]{1,0:T(8,128)(2,1)} %convolution_convert_fusion.2.x, f32[64,2048]{1,0:T(8,128)} %copy-done.2, bf16[64,2048]{1,0:T(8,128)(2,1)} %cot.1, f32[1,2048]{1,0:T(1,128)} %bitcast.57, ...), custom_call_target="tpu_custom_call" | custom-call | bytes 30000000 | tf_op jit(solution)/shard_map/pallas_call | solution.py:549
  225.6 3.6 fusion.7.d_gated
  229.3 3.3 convolution_convert_fusion.feed
  232.6 3.6 shard_map.242
  237.1 24.0 %shard_map.243 = (f32[2,256,128]{2,1,0:T(8,128)S(1)}, bf16[16,688,128]{2,1,0:T(8,128)(2,1)}, bf16[16,512,128]{2,1,0:T(8,128)(2,1)S(1)}) custom-call(bf16[2,256,128]{2,1,0:T(8,128)(2,1)S(1)} %get-tuple-element.76.inc, bf16[4,2,128,128]{3,2,1,0:T(8,128)(2,1)S(1)} %get-tuple-element.77.ga, bf16[4,2,128,128]{3,2,1,0:T(8,128)(2,1)S(1)} %get-tuple-element.78.ta, ...), custom_call_target="tpu_custom_call" | custom-call | bytes 12000000 | tf_op jit(solution)/shard_map/pallas_call | solution.py:549
  261.2 1.3 copy-done.1
  263.2 34.4 %shard_map.244 = (bf16[512,1536]{1,0:T(8,128)(2,1)}, f32[16,1024]{1,0:T(8,128)}, f32[8,1024]{1,0:T(8,128)}, f32[512,4]{1,0:T(8,128)}, f32[4,1024]{1,0:T(4,128)},...) custom-call(s32[6]{0:T(128)} %pad_add_fusion.info, f32[2,256,128]{2,1,0:T(8,128)} %copy-done.10, ...), custom_call_target="tpu_custom_call" | custom-call | bytes 30000000 | tf_op jit(solution)/shard_map/pallas_call | solution.py:549
  299.4 1.2 pad.14.decay
  300.5 66.7 %shard_map.245 = (bf16[64,2048]{1,0:T(8,128)(2,1)}, f32[64,2048]{1,0:T(8,128)}, f32[2,128,768]{2,1,0:T(8,128)}, f32[40,128]{1,0:T(8,128)}, f32[40,128]{1,0:T(8,1...) custom-call(bf16[512,1536]{1,0:T(8,128)(2,1)} %get-tuple-element.91.dproj, ...), custom_call_target="tpu_custom_call" | custom-call | bytes 40000000 | tf_op jit(solution)/shard_map/pallas_call | solution.py:549
  367.3 1.4 slice_bitcast_fusion
  368.7 1.2 slice_bitcast_fusion.2
  369.9 2.6 copy.35
  373.9 1.3 slice.51
  375.2 1.3 fusion.5
  376.5 1.7 copy.43
  (84 shorter events, 19.6 us)
Async XLA Ops:
  7.2 31.9 %all-gather.3.cloned.1.call-start = ((), (), s32[]{:S(2)}) async-start(), calls=%async_computation | async-start | bytes 2359296 | tf_op jit(solution)/shard_map/all_gather | solution.py:978
  10.2 154.2 %all-gather.5.cloned.1.call-start = ((), (), s32[]{:S(2)}) async-start(), calls=%async_computation.1 | async-start | bytes 2359296 | tf_op jit(solution)/shard_map/all_gather | solution.py:983
  10.2 28.9 %copy-start.27 = (bf16[4,2,512]{2,1,0:T(2,128)(2,1)S(1)}, bf16[4,2,512]{2,1,0:T(2,128)(2,1)}, u32[]{:S(2)}) copy-start(bf16[4,2,512]{2,1,0:T(2,128)(2,1)} %param.18) | copy-start | bytes 24580
  10.2 29.5 %copy-start.26 = (bf16[2048,2,2]{0,2,1:T(2,128)(2,1)S(1)}, bf16[2048,2,2]{0,2,1:T(2,128)(2,1)}, u32[]{:S(2)}) copy-start(bf16[2048,2,2]{0,2,1:T(2,128)(2,1)} %param.17) | copy-start | bytes 49156
  10.2 30.8 %copy-start.28 = (s32[4]{0:T(128)S(1)}, s32[4]{0:T(128)}, u32[]{:S(2)}) copy-start(s32[4]{0:T(128)} %param.26) | copy-start | bytes 52
  41.6 11.8 %copy-start.21 = (bf16[512,2048]{1,0:T(8,128)(2,1)S(1)}, bf16[512,2048]{1,0:T(8,128)(2,1)}, u32[]{:S(2)}) copy-start(bf16[512,2048]{1,0:T(8,128)(2,1)} %all-gather.3.cloned.1.call-done.normed) | copy-start | bytes 6291460
  48.5 1.7 copy-start.20
  50.1 4.8 %collective-permute-start = (bf16[8,1024]{1,0:T(8,128)(2,1)S(1)}, bf16[8,1024]{1,0:T(8,128)(2,1)S(1)}, u32[]{:S(2)}, u32[]{:S(2)}) collective-permute-start(bf16[8,1024]{1,0:T(8,128)(2,1)S(1)} %bitcast.71), channel_id=1, source_target_pairs={{0,8},{8,16},{16,24},{24,32},{32,40},{40,48},{48,56},{56,64},{64,7... | collective-permute-start | bytes 49160 | tf_op jit(solution)/shard_map/ppermute | solution.py:965
  55.6 54.5 %copy-start.14 = (f32[256]{0:T(256)S(1)}, f32[256]{0:T(256)}, u32[]{:S(2)}) copy-start(f32[256]{0:T(256)} %param.21) | copy-start | bytes 3076
  81.2 0.9 copy-start.11
  110.1 1.1 copy-start.5
  111.2 1.0 copy-start.17
  112.3 1.2 copy-start.19
  116.3 0.8 copy-start.7
  117.1 1.0 copy-start.15
  118.3 3.0 copy-start
  118.3 3.0 copy-start.12
  154.7 0.8 copy-start.2
  155.5 1.4 copy-start.3
  225.6 3.7 copy-start.29
  229.2 3.3 copy-start.6
  229.3 3.3 copy-start.16
  229.3 3.3 copy-start.18
  236.1 1.0 copy-start.4
  237.1 24.0 %copy-start.8 = (bf16[512,512]{1,0:T(8,128)(2,1)}, bf16[512,512]{1,0:T(8,128)(2,1)S(1)}, u32[]{:S(2)}) copy-start(bf16[512,512]{1,0:T(8,128)(2,1)S(1)} %get-tuple-element.88.d_gate) | copy-start | bytes 1572868
  237.1 24.0 %copy-start.9 = (f32[4,256,128]{2,1,0:T(8,128)}, f32[4,256,128]{2,1,0:T(8,128)S(1)}, u32[]{:S(2)}) copy-start(f32[4,256,128]{2,1,0:T(8,128)S(1)} %get-tuple-element.86.y) | copy-start | bytes 1572868
  237.1 24.1 %copy-start.13 = (f32[1,256]{1,0:T(1,128)}, f32[1,256]{1,0:T(1,128)S(1)}, u32[]{:S(2)}) copy-start(f32[1,256]{1,0:T(1,128)S(1)} %get-tuple-element.99.g_head) | copy-start | bytes 3076
  261.2 1.4 copy-start.1
  367.2 11.0 %copy-start.23 = (f32[64,2048]{1,0:T(8,128)S(1)}, f32[64,2048]{1,0:T(8,128)}, u32[]{:S(2)}) copy-start(f32[64,2048]{1,0:T(8,128)} %get-tuple-element.158) | copy-start | bytes 1572868
  367.2 11.8 %copy-start.25 = (f32[512,128]{1,0:T(8,128)S(1)}, f32[512,128]{1,0:T(8,128)}, u32[]{:S(2)}) copy-start(f32[512,128]{1,0:T(8,128)} %get-tuple-element.108) | copy-start | bytes 786436
  367.3 12.5 %copy-start.22 = (f32[2,688,128]{2,1,0:T(8,128)S(1)}, f32[2,688,128]{2,1,0:T(8,128)}, u32[]{:S(2)}) copy-start(f32[2,688,128]{2,1,0:T(8,128)} %get-tuple-element.109) | copy-start | bytes 2113540
  372.6 8.0 %copy-start.24 = (f32[688,128]{1,0:T(8,128)S(1)}, f32[688,128]{1,0:T(8,128)}, u32[]{:S(2)}) copy-start(f32[688,128]{1,0:T(8,128)} %get-tuple-element.169) | copy-start | bytes 1056772
  (1 other events, 0.7 us)
Sparse Core Ops, SparseCore 0:
  10.3 28.7 all-gather.2
  40.8 25.4 all-gather.4

commit v5 on v4

--- a/solution.py
+++ b/solution.py
@@ -203,7 +203,7 @@
     return dot(ah, b, form) + dot(al, b, form)
 
 
-def bwd_head(d_gated, head_out, proj, gain, qe, step, d_out_o, d_gate_o, d_gain_o, y_o, inc_o):
+def head_back(d_mixed, out_w, head_out, proj, gain, qe, step, d_out_o, d_gate_o, y_o, inc_o):
     rows = qe.shape[0]
     blocks = rows // BLK
     heads = qe.shape[1] // DK
@@ -212,14 +212,13 @@
         cols = pl.ds(h * DV, DV)
         for c in range(blocks):
             here = pl.ds(c * BLK, BLK)
-            dg, out = d_gated[here, cols], head_out[here, cols]
+            dg, out = dot(d_mixed[here, :], out_w[cols, :], "nt"), head_out[here, cols]
             gate = proj[here, pl.ds(h * MIXW + CONVW, DV)]
             s = sigmoid(gate)
             silu = gate * s
             scale = lax.rsqrt(jnp.mean(out * out, axis=1, keepdims=True) + 1e-05)
-            n = out * scale
-            dn = dg * n
-            d_gate_o[here, cols] = (dn * gain[...] * (s * (1.0 + gate * (1.0 - s)))).astype(BF16)
+            dn = dg * (out * scale)
+            d_gate_o[here, pl.ds(h * MIXW + CONVW, DV)] = (dn * gain[...] * (s * (1.0 + gate * (1.0 - s)))).astype(BF16)
             total = total + jnp.sum(dn * silu, axis=0, keepdims=True)
             f = dg * gain[...] * silu
             d_out = scale * f - out * (scale * scale * scale) * jnp.mean(f * out, axis=1, keepdims=True)
@@ -229,22 +228,44 @@
         for c in range(blocks - 2, -1, -1):
             inc = y_o[h * blocks + c] + dot3(inc, step[h * blocks + c, :DK, :], "nt")
         inc_o[h] = inc.astype(inc_o.dtype)
-    d_gain_o[...] = total
-
-
-def bwd_mix(
-    info, later, conv, dec, inv, wu, states, step, y, d_out, d_gate, rate, proj, halo, convw, dlog, dbias, g_down, g_out,
-    d_proj_o, d_tail_o, d_edge_o, d_rate_o, d_convw_o, d_decay_o, s_down_o, s_out_o,
-    xpad, dpad, dsend, cols_s, d_pre_o, relay_d, relay_o, got_d, got_o, s1, r1
+    return total
+
+
+def mixer_back(
+    info, d_mixed, out_w, head_out, proj, gain, qe, step, ga, ta, middle, cot, gated_t, s_gu, conv, dec, inv, wu, states,
+    rate, halo, convw, dlog, dbias,
+    d_proj_o, d_tail_o, d_edge_o, d_rate_o, d_convw_o, d_decay_o, d_gain_o, s_down_o, s_out_o, g_gu_o,
+    d_out, y, inc, later, got1, tot, got2, xpad, dpad, dsend, cols_s, d_pre_o,
+    g_down, g_out, relay_d, relay_o, got_d, got_o, last_got, s1, r1, s2, r2, s3, r3, s4, r4
 ):
     greet(side_peers())
+    settle = Settle(lambda i, b: last_got.at[i, b], s4, r4)
+    for b in (2, 1, 3):
+        for i in range(2):
+            settle.send(s_gu.at[i, b], i, b)
     grads = (g_down, g_out)
     spread = Spread(
         lambda i, owner: grads[i].at[owner], lambda i, b: (relay_d, relay_o)[i].at[b],
-        lambda i, s, b: (got_d, got_o)[i].at[s, b], s1, r1,
-    )
+        lambda i, s, b: (got_d, got_o)[i].at[s, b], s3, r3,
+    )
+    d_gain_o[...] = head_back(d_mixed, out_w, head_out, proj, gain, qe, step, d_out, d_proj_o, y, inc)
+
+    def make(o, left, right):
+        for j in range(0, o.shape[0], 2):
+            both = dot(left[...], right[:, j * LANES : (j + 2) * LANES]).astype(BF16)
+            o[j], o[j + 1] = both[:, :LANES], both[:, LANES:]
+
+    def level_one():
+        make(g_down, middle, cot)
+        make(g_out, gated_t, d_mixed)
+
+    def level_two():
+        for place in PLACES:
+            spread.ready(*place, (0,))
+
+    swaps = states_backward(inc, ga, ta, later, got1, tot, got2, s1, r1, s2, r2, level_one, level_two)
     for place in PLACES:
-        spread.ready(*place)
+        spread.ready(*place, (1,))
     rows = d_out.shape[0]
     heads = later.shape[0]
     blocks = rows // BLK
@@ -316,8 +337,7 @@
             d_ka = rk * d_k - ka * (rk * rk * rk * jnp.sum(d_k * ka, axis=1, keepdims=True))
             d_act = jnp.concatenate([d_qa, d_ka, d_val], axis=1)
             d_pre_o[here, pl.ds(h * CONVW, CONVW)] = d_act * (sg * (1.0 + cv * (1.0 - sg)))
-            if h == 1:
-                spread.relays(c)
+            spread.relays(c * heads + h)
     d_g, d_beta = cols_s[:, :heads], cols_s[:, heads : 2 * heads]
     d_bias = -d_g * jnp.exp(dlog[...]) * sigmoid(pre)
     d_rate_o[:, :heads] = d_bias
@@ -338,11 +358,15 @@
         d_edge_o[:, dst] = dpad[:PAD, :]
         d_tail_o[:, dst] = dpad[rows - PAD :, :]
         d_proj_o[:, src] = dpad[PAD:, :].astype(BF16)
-        d_proj_o[:, pl.ds(h * MIXW + CONVW, DV)] = d_gate[:, pl.ds(h * DV, DV)]
+    for i in range(2):
+        g_gu_o[i] = s_gu[i, 0].astype(F32) + settle.others(i)
     for i, o in ((0, s_down_o), (1, s_out_o)):
         for b in FAR:
             o[b] = spread.total(i, b).astype(BF16)
     spread.end()
+    settle.end()
+    for s in swaps:
+        s.wait_send()
 
 
 def call(kernel, outs, scratch, limit, *args, flops=2_000_000_000, nbytes=16_000_000):
@@ -494,15 +518,14 @@
 
 
 def mid_backward(
-    x, hidden, cot, gain, d_gu, n2, all_o, d_hidden_o, d_gain_o, grad_o,
-    total, block, pair, got, mid, g, relay, seqs_got, part, last_got, s1, r1, s2, r2, ls, s3, r3, s4, r4
+    x, hidden, cot, gain, d_gu, n2, all_o, d_hidden_o, d_gain_o, sums_o,
+    total, block, pair, got, mid, g, relay, seqs_got, s1, r1, s2, r2, ls, s3, r3
 ):
     greet(head_peers() + side_peers())
     one = pair_sends(x, pair, s1, r1, FAR)
     spread = Spread(
         lambda i, owner: g.at[owner, i], lambda i, b: relay.at[i, b], lambda i, s, b: seqs_got.at[i, s, b], s3, r3
     )
-    settle = Settle(lambda i, b: last_got.at[i, b], s4, r4)
     dev = seq_place()[3]
     hid = g.shape[2]
 
@@ -514,33 +537,24 @@
         g[owner, 1] = out[hid:]
         spread.ready(*place)
 
-    for place in PLACES[:2]:
+    for place in PLACES[:3]:
         make(place)
     two = chip_sends(x, one, total, pair, got, mid, s1, r1, FAR)
-    for place in PLACES[2:]:
+    for place in PLACES[3:]:
         make(place)
-    spread.relays(0)
     d_norm, d_gain = norm_back(hidden[...], gain[...], chip_sum(two, total, got))
     d_hidden = cot[...].astype(F32) + d_norm
     d_hidden_o[...] = d_hidden
     d_gain_o[...] = d_gain
     block[...] = d_hidden.astype(BF16)
     ahead = gather_start(block, all_o, s2, r2, ls)
-    spread.relays(1)
+    spread.relays()
     ahead += gather_forward(block, all_o, s2, r2)
     for b in FAR:
         for i in range(2):
-            both = spread.total(i, b)
-            if b:
-                part[i, b] = both.astype(BF16)
-                settle.send(part.at[i, b], i, b)
-            else:
-                grad_o[i] = both
+            sums_o[i, b] = spread.total(i, b).astype(BF16)
     gather_end(block, all_o, s2, r2, ls, ahead)
-    for i in range(2):
-        grad_o[i] = grad_o[i] + settle.others(i)
     spread.end()
-    settle.end()
     for s in list(one.values()) + list(two.values()):
         s.wait_send()
 
@@ -625,16 +639,16 @@
     def late(self, a, b):
         return a == 1 and b in FIRST or a == 3 and b in OTHER
 
-    def ready(self, dz, dy):
+    def ready(self, dz, dy, halves_=(0, 1)):
         owner = self.dev(dz, dy)[0]
-        for i in range(2):
+        for i in halves_:
             a, b = (dy, dz) if i == 0 else (dz, dy)
             if a and not self.late(a, b):
                 self.send(i, a, b, owner)
 
     def relays(self, part=None):
         for n, b in enumerate(FAR):
-            if part is not None and n // 2 != part:
+            if part is not None and n != part:
                 continue
             for i in range(2):
                 a = 1 if b in FIRST else 3
@@ -745,21 +759,11 @@
         s.wait_send()
 
 
-def states_backward(inc, ga, ta, middle, cot, gated_t, d_mixed, later_o, g_down_o, g_out_o, got1, tot, got2, s1, r1, s2, r2):
+def states_backward(inc, ga, ta, later_o, got1, tot, got2, s1, r1, s2, r2, level_one, level_two):
     me, z, y, dev = seq_place()
     heads = inc.shape[0]
-    seqs = g_down_o.shape[0]
-
-    def blocks(o, left, right, part):
-        for j in range(part * seqs // 4, (part + 1) * seqs // 4):
-            if j % 2 == 0:
-                both = dot(left[...], right[:, j * LANES : (j + 2) * LANES]).astype(BF16)
-                o[j], o[j + 1] = both[:, :LANES], both[:, LANES:]
-
-    greet(side_peers())
     out, wait = share_start(inc, got1, y, lambda d: dev(0, d), s1, r1)
-    blocks(g_down_o, middle, cot, 0)
-    blocks(g_down_o, middle, cot, 1)
+    level_one()
     wait()
     after = []
     for h in range(heads):
@@ -772,19 +776,14 @@
         tot[h] = whole[DK:].astype(BF16)
         after.append(suffix)
     more, wait = share_start(tot, got2, z, lambda d: dev(d, 0), s2, r2)
-    out += more
-    blocks(g_down_o, middle, cot, 2)
-    blocks(g_down_o, middle, cot, 3)
-    for part in range(4):
-        blocks(g_out_o, gated_t, d_mixed, part)
+    level_two()
     wait()
     for h in range(heads):
         held = jnp.zeros((DV, DK), F32)
         for j in range(SIDE - 1, 0, -1):
             held = jnp.where(z < j, dot_left2(held, ta[j, h], "nt") + got2[j, h].astype(F32), held)
         later_o[h] = dot3(held, after[h][:DK]) + after[h][DK:]
-    for s in out:
-        s.wait_send()
+    return out + more
 
 
 def pair_sends(x, pair, ssem, rsem, steps):
@@ -881,8 +880,8 @@
         here = pl.ds(pl.multiple_of(chip * low, low), low)
         dn[here, :] = (dot(dp[here, :], wv[...], "nt") + dot(d_rate[here, :], rate_w[...], "nt")).astype(BF16)
         dn_one.update(pair_sends(dn, pb, sb, rb, (d,)))
+        spread.relays(FAR.index(d))
     dn_two = chip_sends(dn, dn_one, tb, pb, gb, mb, sb, rb, FAR)
-    spread.relays()
     layer_o[...] = (hidden[...] + chip_sum(feed_two, ta, ga)).astype(BF16)
     d_norm, d_gain = norm_back(tokens[...].astype(F32), gain[...], chip_sum(dn_two, tb, gb))
     d_tokens_o[...] = d_hidden[...] + d_norm
@@ -1044,57 +1043,45 @@
     part, half, n_head = D // seq, MIXW, lax.axis_size("head")
     d_mixed, d_hidden, g_feed_gain, grads = reach(
         mid_backward,
-        [sds((rows, D), BF16), sds((own, D)), sds((1, D)), sds((2, hid, LANES))],
+        [sds((rows, D), BF16), sds((own, D)), sds((1, D)), sds((2, SIDE, hid, LANES), BF16)],
         [pltpu.VMEM((own, D), F32), pltpu.VMEM((own, D), BF16)]
         + [pltpu.VMEM((CHIPS, own, D), BF16) for _ in range(3)]
         + [
             pltpu.VMEM((seq, 2, hid, LANES), BF16), pltpu.VMEM((2, SIDE, hid, LANES), BF16),
-            pltpu.VMEM((2, 2, SIDE, hid, LANES), BF16), pltpu.VMEM((2, SIDE, hid, LANES), BF16),
-            pltpu.VMEM((2, SIDE, hid, LANES), BF16), sems(2 * CHIPS), sems(2 * CHIPS),
+            pltpu.VMEM((2, 2, SIDE, hid, LANES), BF16), sems(2 * CHIPS), sems(2 * CHIPS),
         ]
         + gather_scratch()
-        + [sems(2 * SIDE * SIDE), sems(2 * SIDE * SIDE), sems(2 * SIDE), sems(2 * SIDE)],
+        + [sems(2 * SIDE * SIDE), sems(2 * SIDE * SIDE)],
         3, 60, d_two, hidden, cotangent, feed_row, d_gate_up, gathered_two, nbytes=30_000_000,
     )
-    grad_gate_up = grads.transpose(2, 0, 1)
     d_mixed, middle = lax.optimization_barrier((d_mixed, middle))
     feed = lax.dot_general(middle, down_weight, by_first, preferred_element_type=F32).astype(BF16)
     gated_t = gated.T
-    d_gated = jnp.einsum("td,vd->tv", d_mixed, out_flat, preferred_element_type=F32)
-    d_out, d_gate, g_head_gain, y, inc = call(
-        bwd_head,
-        [
-            sds((rows, heads * DV)), sds((rows, heads * DV), BF16), sds((1, DV)),
-            sds((units, DV, DK)), sds((heads, DV, DK), BF16),
-        ],
-        [], 48, d_gated, head_out, projected, gain, qe, step,
-    )
-    later, g_down, g_out = reach(
-        states_backward,
-        [sds((heads, DV, DK)), sds((seq, hid, LANES), BF16), sds((seq, heads * DV, LANES), BF16)],
-        [
-            pltpu.VMEM((SIDE, heads, DV, DK), BF16), pltpu.VMEM((heads, DV, DK), BF16),
-            pltpu.VMEM((SIDE, heads, DV, DK), BF16), sems(SIDE), sems(SIDE), sems(SIDE), sems(SIDE),
-        ],
-        4, 48, inc, ga, ta, middle, cot_rows, gated_t, d_mixed,
-    )
-    d_projected, d_tail, d_edge, d_rate, d_convw, d_decay, s_down, s_out = reach(
-        bwd_mix,
+    d_projected, d_tail, d_edge, d_rate, d_convw, d_decay, g_head_gain, s_down, s_out, grad_gate_up = reach(
+        mixer_back,
         [
             sds((rows, heads * MIXW), BF16), sds((2 * PAD, heads * CONVW)), sds((PAD, heads * CONVW)),
-            sds((rows, 2 * heads)), sds((KCONV, heads * CONVW)), sds((1, 2 * heads)),
-            sds((SIDE, hid, LANES), BF16), sds((SIDE, heads * DV, LANES), BF16),
+            sds((rows, 2 * heads)), sds((KCONV, heads * CONVW)), sds((1, 2 * heads)), sds((1, DV)),
+            sds((SIDE, hid, LANES), BF16), sds((SIDE, heads * DV, LANES), BF16), sds((2, hid, LANES)),
         ],
         [
+            pltpu.VMEM((rows, heads * DV), F32), pltpu.VMEM((units, DV, DK), F32),
+            pltpu.VMEM((heads, DV, DK), BF16), pltpu.VMEM((heads, DV, DK), F32),
+            pltpu.VMEM((SIDE, heads, DV, DK), BF16), pltpu.VMEM((heads, DV, DK), BF16),
+            pltpu.VMEM((SIDE, heads, DV, DK), BF16),
             pltpu.VMEM((PAD + rows, CONVW), F32), pltpu.VMEM((PAD + rows, CONVW), F32),
             pltpu.VMEM((units, DV, DK), F32), pltpu.VMEM((rows, DK), F32), pltpu.VMEM((rows, heads * CONVW), F32),
+            pltpu.VMEM((seq, hid, LANES), BF16), pltpu.VMEM((seq, heads * DV, LANES), BF16),
             pltpu.VMEM((SIDE, hid, LANES), BF16), pltpu.VMEM((SIDE, heads * DV, LANES), BF16),
             pltpu.VMEM((2, SIDE, hid, LANES), BF16), pltpu.VMEM((2, SIDE, heads * DV, LANES), BF16),
-            sems(2 * SIDE * SIDE), sems(2 * SIDE * SIDE),
+            pltpu.VMEM((2, SIDE, hid, LANES), BF16),
+            sems(SIDE), sems(SIDE), sems(SIDE), sems(SIDE), sems(2 * SIDE * SIDE), sems(2 * SIDE * SIDE),
+            sems(2 * SIDE), sems(2 * SIDE),
         ],
-        6, 62, info, later, conv, dec, inv, wu, states, step, y, d_out, d_gate, rate_proj, projected, halo, convw,
-        dlog, dbias, g_down, g_out, scalars=(0,), nbytes=30_000_000,
-    )
+        4, 63, info, d_mixed, out_flat, head_out, projected, gain, qe, step, ga, ta, middle, cot_rows, gated_t, grads,
+        conv, dec, inv, wu, states, rate_proj, halo, convw, dlog, dbias, scalars=(0,), nbytes=40_000_000,
+    )
+    grad_gate_up = grad_gate_up.transpose(2, 0, 1)
     d_rate_low = jnp.pad(d_rate.astype(BF16), ((0, 0), (0, LANES - 2 * heads)))
     rate_pad = jnp.pad(rate_weight.reshape(D, 2 * heads), ((0, 0), (0, LANES - 2 * heads)))
     d_decay = jnp.pad(d_decay, ((0, 0), (0, LANES - 2 * heads)))

time: 392 us -> 376 us (0.959)
  Pallas kernels: 266 us -> 258 us
  matrix products: 37.8 us -> 32.9 us
    unnamed x68 -> x58, local copies, waits for them, and re-layouts: 27.9 us -> 23.1 us
    pallas_call x6 -> x5, Pallas kernels: 234 us -> 230 us  [reach(): pl.pallas_call(kernel, out_shape=outs, in_specs=[pl.BlockSpec(memory_spac...]
    pallas_call x3 -> x2, Pallas kernels: 31.9 us -> 28.5 us  [call(): pl.pallas_call(kernel, out_shape=outs, in_specs=[spec(a) for a in args],...]
  transfers between devices with their start and end apart: 3 -> 3, of which waited for: 1 -> 1; matrix products, arithmetic and copies ran while one was open for 7% -> 8% of each run, Pallas kernels for 23% -> 24%
where the time goes in v5:
time: 376 us; the launch traced here: 372 us
  Pallas kernels  258 us (69%)
  local copies, waits for them, and re-layouts  34.8 us (9%)
  matrix products  32.9 us (9%)
  waiting for transfers between devices  22.1 us (6%)
  between operations  14.8 us (4%)
  other arithmetic  6.35 us (2%)
    pallas_call x5, Pallas kernels, reach(): pl.pallas_call(kernel, out_shape=outs, in_specs=[pl.BlockSpec(memory_spac...  230 us
    pallas_call x2, Pallas kernels, call(): pl.pallas_call(kernel, out_shape=outs, in_specs=[spec(a) for a in args],...  28.5 us
    unnamed x58, local copies, waits for them, and re-layouts  23.1 us
    all_gather x1, waiting for transfers between devices, local(): gathered = lax.all_gather(normed, 'head', axis=0, tiled=True)  22.1 us
    dot_general x1, matrix products, local(): lax.dot_general(gu_t, gathered_two, by_last, preferred_element_type=F32)  8.03 us
    dot_general x1, matrix products, local(): lax.dot_general(d_gate_up, gu_t, by_first, preferred_element_type=F32)  7.6 us
  transfers between devices with their start and end apart: 3, of which 1 were waited for; matrix products, arithmetic and copies ran while one was open for 8% of the time, Pallas kernels for 24%

profile of v5, /device:TPU:1, one launch (start us, length us, event | category | flops | bytes accessed | tf_op | source)
XLA Modules:
  0.0 372.4 jit_solution(7316320865027537251)
XLA Ops:
  7.2 1.1 fusion.2
  8.3 1.8 fusion.4
  10.2 6.8 %copy.36 = bf16[256,8,2,768]{3,1,2,0:T(8,128)(2,1)} copy(bf16[256,8,2,768]{3,2,1,0:T(2,128)(2,1)} %bitcast.60) | data formatting | bytes 12582912
  17.0 22.1 %all-gather.3.cloned.1.call-done.normed = bf16[512,2048]{1,0:T(8,128)(2,1)} async-done(((bf16[64,2048]{1,0:T(8,128)(2,1)}), bf16[512,2048]{1,0:T(8,128)(2,1)}) %all-gather.3.cloned.1.call-update) | async-done | bytes 2097168 | tf_op jit(solution)/shard_map/all_gather | solution.py:977
  41.7 6.9 %fusion.6.proj = f32[512,1536]{1,0:T(8,128)S(1)} fusion(bf16[512,2048]{1,0:T(8,128)(2,1)} %all-gather.3.cloned.1.call-done.normed, bf16[2048,1536]{1,0:T(8,128)(2,1)} %bitcast.58), kind=kOutput, calls=%fused_computation.24 | convolution fusion | flops 3221225472 | bytes 11534336 | tf_op jit(solution)/shard_map/dot_general | solution.py:987
  48.6 3.3 collective-permute-start
  54.1 25.5 %shard_map.237 = (f32[512,1024]{1,0:T(8,128)}, f32[4,256,256]{2,1,0:T(8,128)}, bf16[4,256,256]{2,1,0:T(8,128)(2,1)}, f32[4,256,384]{2,1,0:T(8,128)}, f32[512,256...) custom-call(s32[6]{0:T(128)} %pad_add_fusion.info, ...), custom_call_target="tpu_custom_call" | custom-call | flops 2000000000 | bytes 16000000 | tf_op jit(solution)/shard_map/pallas_call | solution.py:376
  80.5 28.0 %shard_map.238 = (f32[2,256,128]{2,1,0:T(8,128)S(1)}, bf16[4,2,128,128]{3,2,1,0:T(8,128)(2,1)S(1)}, bf16[4,2,128,128]{3,2,1,0:T(8,128)(2,1)S(1)}) custom-call(bf16[2,384,128]{2,1,0:T(8,128)(2,1)S(1)} %copy-done.9), custom_call_target="tpu_custom_call" | custom-call | bytes 12000000 | tf_op jit(solution)/shard_map/pallas_call | solution.py:563
  109.9 1.1 copy-done.4
  111.0 1.0 copy-done.5
  112.1 1.2 copy-done.12
  113.3 2.9 shard_map.239
  116.3 1.0 copy-done.3
  118.1 1.0 copy.32
  119.1 1.3 convolution_convert_fusion.1.x
  120.4 33.6 %shard_map.240 = (bf16[512,2048]{1,0:T(8,128)(2,1)S(1)}, f32[64,2048]{1,0:T(8,128)S(1)}) custom-call(bf16[512,2048]{1,0:T(8,128)(2,1)S(1)} %convolution_convert_fusion.1.x, bf16[64,2048]{1,0:T(8,128)(2,1)S(1)} %copy-done, f32[1,2048]{1,0:T(1,128)S(1)} %bitcast.55), custom_call_target="tpu_custom_call" | custom-call | bytes 12000000 | tf_op jit(solution)/shard_map/pallas_call | solution.py:563
  154.7 8.0 %convolution_bitcast_fusion = f32[1376,512]{1,0:T(8,128)} fusion(bf16[512,2048]{1,0:T(8,128)(2,1)S(1)} %get-tuple-element.65.n2, bf16[1376,2048]{1,0:T(8,128)(2,1)} %bitcast.79), kind=kOutput, calls=%fused_computation | convolution fusion | flops 2885681152 | bytes 10551296 | tf_op jit(solution)/shard_map/dot_general | solution.py:1037
  162.8 5.4 %multiply_convert_fusion.2 = (bf16[688,512]{1,0:T(8,128)(2,1)S(1)}, bf16[688,512]{1,0:T(8,128)(2,1)S(1)}, bf16[688,512]{1,0:T(8,128)(2,1)S(1)}) fusion(f32[1376,512]{1,0:T(8,128)} %convolution_bitcast_fusion, bf16[512,2048]{1,0:T(8,128)(2,1)} %all-gather.5.cloned.1.call-done.cot, bf16[688,2048]{1,0:T(8,128)(2,1)} %param.25), kind=kOutput, calls=%fused_computation.10 | convolution fusion | flops 1448476672 | bytes 9846784 | tf_op jit(solution)/shard_map/dot_general | solution.py:1036
  168.2 1.3 pad_maximum_fusion.d_gu
  169.4 7.6 %convolution_convert_fusion.2.x = bf16[512,2048]{1,0:T(8,128)(2,1)} fusion(bf16[1376,2048]{1,0:T(8,128)(2,1)} %bitcast.80, bf16[688,512]{1,0:T(8,128)(2,1)S(1)} %get-tuple-element.126, bf16[688,512]{1,0:T(8,128)(2,1)S(1)} %get-tuple-element.125), kind=kOutput, calls=%fused_computation.3 | convolution fusion | flops 2889547776 | bytes 9142272 | tf_op jit(solution)/shard_map/dot_general | solution.py:1042
  177.1 40.1 %shard_map.241 = (bf16[512,2048]{1,0:T(8,128)(2,1)}, f32[64,2048]{1,0:T(8,128)}, f32[1,2048]{1,0:T(1,128)}, bf16[2,4,688,128]{3,2,1,0:T(8,128)(2,1)}) custom-call(bf16[512,2048]{1,0:T(8,128)(2,1)} %convolution_convert_fusion.2.x, f32[64,2048]{1,0:T(8,128)} %copy-done.1, bf16[64,2048]{1,0:T(8,128)(2,1)} %cot.1, f32[1,2048]{1,0:T(1,128)} %bitcast.54, ...), custom_call_target="tpu_custom_call" | custom-call | bytes 30000000 | tf_op jit(solution)/shard_map/pallas_call | solution.py:563
  217.2 3.1 convolution_convert_fusion.feed
  220.4 55.2 %shard_map.242 = (bf16[512,1536]{1,0:T(8,128)(2,1)}, f32[16,1024]{1,0:T(8,128)}, f32[8,1024]{1,0:T(8,128)}, f32[512,4]{1,0:T(8,128)}, f32[4,1024]{1,0:T(4,128)},...) custom-call(s32[6]{0:T(128)} %pad_add_fusion.info, ...), custom_call_target="tpu_custom_call" | custom-call | bytes 40000000 | tf_op jit(solution)/shard_map/pallas_call | solution.py:563
  275.6 1.0 convert_element_type.42
  277.2 1.1 pad.14.decay
  278.3 72.7 %shard_map.243 = (bf16[64,2048]{1,0:T(8,128)(2,1)}, f32[64,2048]{1,0:T(8,128)}, f32[2,128,768]{2,1,0:T(8,128)}, f32[40,128]{1,0:T(8,128)}, f32[40,128]{1,0:T(8,1...) custom-call(bf16[512,1536]{1,0:T(8,128)(2,1)} %get-tuple-element.79.dproj, ...), custom_call_target="tpu_custom_call" | custom-call | bytes 40000000 | tf_op jit(solution)/shard_map/pallas_call | solution.py:563
  351.1 1.4 slice_bitcast_fusion
  352.5 1.3 slice_bitcast_fusion.2
  353.7 2.6 copy.35
  357.7 1.3 slice.51
  359.0 1.3 fusion.5
  360.3 1.7 copy.43
  (71 shorter events, 13.9 us)
Async XLA Ops:
  7.2 31.9 %all-gather.3.cloned.1.call-start = ((), (), s32[]{:S(2)}) async-start(), calls=%async_computation | async-start | bytes 2359296 | tf_op jit(solution)/shard_map/all_gather | solution.py:977
  10.2 152.6 %all-gather.5.cloned.1.call-start = ((), (), s32[]{:S(2)}) async-start(), calls=%async_computation.1 | async-start | bytes 2359296 | tf_op jit(solution)/shard_map/all_gather | solution.py:982
  10.2 28.9 %copy-start.22 = (bf16[4,2,512]{2,1,0:T(2,128)(2,1)S(1)}, bf16[4,2,512]{2,1,0:T(2,128)(2,1)}, u32[]{:S(2)}) copy-start(bf16[4,2,512]{2,1,0:T(2,128)(2,1)} %param.18) | copy-start | bytes 24580
  10.2 29.5 %copy-start.21 = (bf16[2048,2,2]{0,2,1:T(2,128)(2,1)S(1)}, bf16[2048,2,2]{0,2,1:T(2,128)(2,1)}, u32[]{:S(2)}) copy-start(bf16[2048,2,2]{0,2,1:T(2,128)(2,1)} %param.17) | copy-start | bytes 49156
  10.2 30.8 %copy-start.23 = (s32[4]{0:T(128)S(1)}, s32[4]{0:T(128)}, u32[]{:S(2)}) copy-start(s32[4]{0:T(128)} %param.26) | copy-start | bytes 52
  41.7 10.2 %copy-start.15 = (bf16[512,2048]{1,0:T(8,128)(2,1)S(1)}, bf16[512,2048]{1,0:T(8,128)(2,1)}, u32[]{:S(2)}) copy-start(bf16[512,2048]{1,0:T(8,128)(2,1)} %all-gather.3.cloned.1.call-done.normed) | copy-start | bytes 6291460
  48.6 5.5 %copy-start.13 = (f32[512,1536]{1,0:T(8,128)}, f32[512,1536]{1,0:T(8,128)S(1)}, u32[]{:S(2)}) copy-start(f32[512,1536]{1,0:T(8,128)S(1)} %fusion.6.proj) | copy-start | bytes 9437188
  48.6 4.8 %collective-permute-start = (bf16[8,1024]{1,0:T(8,128)(2,1)S(1)}, bf16[8,1024]{1,0:T(8,128)(2,1)S(1)}, u32[]{:S(2)}, u32[]{:S(2)}) collective-permute-start(bf16[8,1024]{1,0:T(8,128)(2,1)S(1)} %bitcast.71), channel_id=1, source_target_pairs={{0,8},{8,16},{16,24},{24,32},{32,40},{40,48},{48,56},{56,64},{64,7... | collective-permute-start | bytes 49160 | tf_op jit(solution)/shard_map/ppermute | solution.py:964
  54.0 55.9 %copy-start.11 = (f32[256]{0:T(256)S(1)}, f32[256]{0:T(256)}, u32[]{:S(2)}) copy-start(f32[256]{0:T(256)} %param.21) | copy-start | bytes 3076
  79.6 0.9 copy-start.9
  108.5 0.7 copy-start.7
  109.2 0.7 copy-start.8
  109.9 1.1 copy-start.4
  111.0 1.0 copy-start.5
  112.1 1.2 copy-start.12
  113.3 5.8 %copy-start.14 = (bf16[2,256,2048]{2,1,0:T(8,128)(2,1)S(1)}, bf16[2,256,2048]{2,1,0:T(8,128)(2,1)}, u32[]{:S(2)}) copy-start(bf16[2,256,2048]{2,1,0:T(8,128)(2,1)} %param.22) | copy-start | bytes 6291460
  116.3 1.0 copy-start.3
  117.3 0.8 copy-start.6
  119.1 1.3 copy-start
  119.1 1.3 copy-start.10
  153.9 0.8 copy-start.1
  154.7 8.0 %copy-start.2 = (bf16[512,2048]{1,0:T(8,128)(2,1)}, bf16[512,2048]{1,0:T(8,128)(2,1)S(1)}, u32[]{:S(2)}) copy-start(bf16[512,2048]{1,0:T(8,128)(2,1)S(1)} %get-tuple-element.65.n2) | copy-start | bytes 6291460
  168.1 49.1 %copy-start.16 = (bf16[688,512]{1,0:T(8,128)(2,1)}, bf16[688,512]{1,0:T(8,128)(2,1)S(1)}, u32[]{:S(2)}) copy-start(bf16[688,512]{1,0:T(8,128)(2,1)S(1)} %get-tuple-element.72.middle) | copy-start | bytes 2113540
  177.1 40.2 %copy-start.24 = (bf16[688,2048]{1,0:T(8,128)(2,1)S(1)}, bf16[688,2048]{1,0:T(8,128)(2,1)}, u32[]{:S(2)}) copy-start(bf16[688,2048]{1,0:T(8,128)(2,1)} %param.25) | copy-start | bytes 8454148
  351.0 11.0 %copy-start.18 = (f32[64,2048]{1,0:T(8,128)S(1)}, f32[64,2048]{1,0:T(8,128)}, u32[]{:S(2)}) copy-start(f32[64,2048]{1,0:T(8,128)} %get-tuple-element.146) | copy-start | bytes 1572868
  351.0 11.8 %copy-start.20 = (f32[512,128]{1,0:T(8,128)S(1)}, f32[512,128]{1,0:T(8,128)}, u32[]{:S(2)}) copy-start(f32[512,128]{1,0:T(8,128)} %get-tuple-element.96) | copy-start | bytes 786436
  351.0 12.5 %copy-start.17 = (f32[2,688,128]{2,1,0:T(8,128)S(1)}, f32[2,688,128]{2,1,0:T(8,128)}, u32[]{:S(2)}) copy-start(f32[2,688,128]{2,1,0:T(8,128)} %get-tuple-element.97) | copy-start | bytes 2113540
  356.4 8.0 %copy-start.19 = (f32[688,128]{1,0:T(8,128)S(1)}, f32[688,128]{1,0:T(8,128)}, u32[]{:S(2)}) copy-start(f32[688,128]{1,0:T(8,128)} %get-tuple-element.157) | copy-start | bytes 1056772
Sparse Core Ops, SparseCore 0:
  10.3 28.7 all-gather.2
  40.8 25.4 all-gather.4
